TPU v7x, 512 devices: a whole 4x4x16 slice. The times are simulated.
512 devices in a mesh: dp: 16 (over y, x), expert: 32 (over z, core).
Axes of the slice: x: 4, y: 4, z: 16, core: 2. Of those that a mesh axis runs over, the one named last changes fastest.
Arguments:
- tokens: bfloat16 [16384, 2048], P(('dp', 'expert')), may hold values from -6 to 6
- routes: int32 [16384, 8], P(('dp', 'expert')), may hold values from 0 to 31, all different within a row; in each aligned block of 32 rows (0 to 31, 32 to 63, ...) at most 12 rows name the same one
- gates: float32 [16384, 8], P(('dp', 'expert')), may hold values from 0.05 to 0.5
- curvature: float32 [16384], P(('dp', 'expert')), may hold values from 0.25 to 4
- w_gate: bfloat16 [32, 2048, 768], P('expert', 'dp'), may hold values from -0.125 to 0.125
- w_up: bfloat16 [32, 2048, 768], P('expert', 'dp'), may hold values from -0.125 to 0.125
- direction: bfloat16 [32, 2048, 768], P('expert', 'dp'), may hold values from -0.21875 to 0.21875
Outputs:
- output_tangent: bfloat16 [16384, 2048], P(('dp', 'expert'))
- curvature_product: bfloat16 [32, 2048, 768], P('expert', 'dp')
Inputs may be any that keep to these rules, and one draw needn't show every extreme that they name: `routes`: the 8 ids of a token differ. Among the tokens of one device no expert is named by more than 12 tokens, a bound that some block reaches of them.
All inputs are finite; a program needn't handle non-finite values.
Results may differ from a plain program's by a relative error of at most 0.017.
Values may be sent and summed in bfloat16 or wider, within the bound.
No kernel may reach another device: no remote copies, remote signals or barrier semaphores. Data moves between devices by JAX's collectives and lax.ppermute only.
A program may use at most 64 MiB of HBM per device.

v0:
```python
import jax
import jax.numpy as jnp
from jax import lax
from jax.sharding import PartitionSpec as P


def slot_positions(route_ids, experts, capacity):
    flat = route_ids.reshape(-1)
    onehot = (flat[:, None] == jnp.arange(experts, dtype=jnp.int32)[None, :]).astype(jnp.int32)
    before = jnp.cumsum(onehot, axis=0) - onehot
    slot = jnp.sum(before * onehot, axis=1)
    return flat * capacity + slot


def local(tokens, routes, gates, curvature, w_gate, w_up, direction):
    tok_count = tokens.shape[0]
    top_count = routes.shape[1]
    width = tokens.shape[1]
    experts = lax.axis_size("expert")
    capacity = min(tok_count, max(2, tok_count * top_count * 3 // (2 * experts)))
    slot_count = experts * capacity
    positions = slot_positions(routes, experts, capacity)
    grid = jnp.arange(slot_count, dtype=jnp.int32)
    picker = (grid[:, None] == positions[None, :]).astype(jnp.bfloat16)
    token_picker = jnp.sum(
        picker.reshape(slot_count, tok_count, top_count).astype(jnp.float32), axis=2
    ).astype(jnp.bfloat16)
    outgoing = jnp.dot(token_picker, tokens, preferred_element_type=jnp.float32).astype(
        jnp.bfloat16
    )
    arrived = lax.all_to_all(
        outgoing.reshape(experts, capacity, width),
        "expert",
        split_axis=0,
        concat_axis=0,
        tiled=True,
    )
    rows = arrived.reshape(slot_count, width)

    def add_rows(piece):
        return jnp.dot(rows, piece, preferred_element_type=jnp.float32)

    gate_pre = add_rows(lax.all_gather(w_gate[0], "dp", axis=0, tiled=True))
    up_pre = add_rows(lax.all_gather(w_up[0], "dp", axis=0, tiled=True))
    hidden = (jax.nn.silu(gate_pre) * up_pre).astype(jnp.bfloat16)
    tangent = lax.dot_general(
        hidden,
        lax.all_gather(direction[0], "dp", axis=0, tiled=True),
        (((1,), (1,)), ((), ())),
        preferred_element_type=jnp.float32,
    ).astype(jnp.bfloat16)
    returned = lax.all_to_all(
        tangent.reshape(experts, capacity, width), "expert", split_axis=0, concat_axis=0, tiled=True
    )
    returned = returned.reshape(slot_count, width)
    per_route = lax.dot_general(
        picker, returned, (((0,), (0,)), ((), ())), preferred_element_type=jnp.float32
    )
    per_route = per_route.reshape(tok_count, top_count, width)
    jv = jnp.sum(gates[:, :, None] * per_route, axis=1)
    output_tangent = jv.astype(jnp.bfloat16)
    scale = gates * curvature[:, None]
    weighted = (
        (scale[:, :, None] * jv[:, None, :])
        .astype(jnp.bfloat16)
        .reshape(tok_count * top_count, width)
    )
    weighted_out = jnp.dot(picker, weighted, preferred_element_type=jnp.float32).astype(
        jnp.bfloat16
    )
    weighted_in = lax.all_to_all(
        weighted_out.reshape(experts, capacity, width),
        "expert",
        split_axis=0,
        concat_axis=0,
        tiled=True,
    )
    weighted_rows = weighted_in.reshape(slot_count, width)
    share = lax.psum_scatter(
        lax.dot_general(
            weighted_rows, hidden, (((0,), (0,)), ((), ())), preferred_element_type=jnp.float32
        ).astype(jnp.bfloat16),
        "dp",
        scatter_dimension=0,
        tiled=True,
    )
    curvature_product = share[None]
    return (output_tangent, curvature_product)


def solution(mesh):
    placed = (
        P(("dp", "expert"), None),
        P(("dp", "expert"), None),
        P(("dp", "expert"), None),
        P(("dp", "expert")),
        P("expert", "dp", None),
        P("expert", "dp", None),
        P("expert", "dp", None),
    )
    return jax.shard_map(
        local,
        mesh=mesh,
        in_specs=placed,
        out_specs=(P(("dp", "expert"), None), P("expert", "dp", None)),
        check_vma=False,
    )
```

profile of v0, /device:TPU:1, one launch (start us, length us, event | category | flops | bytes accessed | tf_op | source)
XLA Modules:
  0.0 531.9 jit_solution(11582596804335707904)
XLA Ops:
  7.2 0.7 all-gather.7.cloned.1.call-update
  8.0 0.7 all-gather.9.cloned.1.call-update
  8.7 0.8 copy.18
  9.4 0.1 eq.62
  9.6 0.6 reduce-window.6
  10.2 0.2 slice_reduce_fusion
  10.4 0.1 fusion.28
  10.6 0.2 fusion.23
  10.9 0.6 convolution_convert_fusion.1
  11.5 1.5 reshape.96
  13.0 16.7 %all-to-all-start = ((bf16[32,12,2048]{2,1,0:T(8,128)(2,1)}), bf16[32,12,2048]{2,1,0:T(8,128)(2,1)S(1)}, u32[]{:S(2)}, u32[]{:S(2)}) async-start(bf16[32,12,2048]{2,1,0:T(8,128)(2,1)} %reshape.96), calls=%async_computation | async-start | bytes 4194304 | tf_op jit(solution)/shard_map/all_to_all | solution.py:31
  29.8 0.7 all-gather.11.cloned.1.call-update
  30.4 97.9 %all-to-all-done = bf16[32,12,2048]{2,1,0:T(8,128)(2,1)S(1)} async-done(((bf16[32,12,2048]{2,1,0:T(8,128)(2,1)}), bf16[32,12,2048]{2,1,0:T(8,128)(2,1)S(1)}, u32[]{:S(2)}, u32[]{:S(2)}) %all-to-all-start) | async-done | bytes 1572896 | tf_op jit(solution)/shard_map/all_to_all | solution.py:31
  128.3 1.3 reshape.97
  129.7 4.9 fusion.4
  134.5 10.1 %all-gather.9.cloned.1.call-done = bf16[1,2048,768]{2,1,0:T(8,128)(2,1)} async-done(((bf16[1,128,768]{2,1,0:T(8,128)(2,1)}), bf16[1,2048,768]{2,1,0:T(8,128)(2,1)}) %all-gather.9.cloned.1.call-update) | async-done | bytes 3145744 | tf_op jit(solution)/shard_map/all_gather | solution.py:44
  144.6 3.6 fusion.14
  148.3 61.7 %all-gather.11.cloned.1.call-done = bf16[1,2048,768]{2,1,0:T(8,128)(2,1)} async-done(((bf16[1,128,768]{2,1,0:T(8,128)(2,1)}), bf16[1,2048,768]{2,1,0:T(8,128)(2,1)}) %all-gather.11.cloned.1.call-update) | async-done | bytes 3145744 | tf_op jit(solution)/shard_map/all_gather | solution.py:48
  210.0 3.3 fusion.6
  213.3 1.5 reshape.98
  214.8 13.4 %all-to-all-start.1 = ((bf16[32,12,2048]{2,1,0:T(8,128)(2,1)}), bf16[32,12,2048]{2,1,0:T(8,128)(2,1)S(1)}, u32[]{:S(2)}, u32[]{:S(2)}) async-start(bf16[32,12,2048]{2,1,0:T(8,128)(2,1)} %reshape.98), calls=%async_computation.1 | async-start | bytes 4194304 | tf_op jit(solution)/shard_map/all_to_all | solution.py:52
  228.5 0.1 mul.70
  228.6 98.3 %all-to-all-done.1 = bf16[32,12,2048]{2,1,0:T(8,128)(2,1)S(1)} async-done(((bf16[32,12,2048]{2,1,0:T(8,128)(2,1)}), bf16[32,12,2048]{2,1,0:T(8,128)(2,1)S(1)}, u32[]{:S(2)}, u32[]{:S(2)}) %all-to-all-start.1) | async-done | bytes 1572896 | tf_op jit(solution)/shard_map/all_to_all | solution.py:52
  326.9 1.3 reshape.105
  328.2 2.4 fusion.13
  330.6 1.8 convolution_convert_fusion.2
  332.5 2.4 reshape.100
  334.8 105.7 %all_to_all.15 = bf16[32,12,2048]{2,1,0:T(8,128)(2,1)} all-to-all(bf16[32,12,2048]{2,1,0:T(8,128)(2,1)S(1)} %reshape.100), channel_id=1, replica_groups=mesh['dp'=16,'expert'=32] {'expert'}, dimensions={0} | all-to-all | bytes 3145728 | tf_op jit(solution)/shard_map/all_to_all | solution.py:71
  440.6 2.5 reshape.101
  443.1 3.5 convolution_convert_fusion
  446.6 0.7 convert_element_type.41
  447.3 78.0 %reduce-scatter.2.cloned.1.call-done = bf16[128,768]{1,0:T(8,128)(2,1)} async-done(((bf16[2048,768]{1,0:T(8,128)(2,1)}), bf16[128,768]{1,0:T(8,128)(2,1)}) %reduce-scatter.2.cloned.1.call-update) | async-done | bytes 196624 | tf_op jit(solution)/shard_map/reduce_scatter | solution.py:79
  (24 shorter events, 0.6 us)
Async XLA Ops:
  7.2 3.7 copy-start
  7.2 122.5 %all-gather.7.cloned.1.call-start = ((), (), s32[]{:S(2)}) async-start(), calls=%async_computation.5 | async-start | bytes 3342336 | tf_op jit(solution)/shard_map/all_gather | solution.py:43
  7.9 136.7 %all-gather.9.cloned.1.call-start = ((), (), s32[]{:S(2)}) async-start(), calls=%async_computation.6 | async-start | bytes 3342336 | tf_op jit(solution)/shard_map/all_gather | solution.py:44
  13.0 115.4 %all-to-all-start = ((bf16[32,12,2048]{2,1,0:T(8,128)(2,1)}), bf16[32,12,2048]{2,1,0:T(8,128)(2,1)S(1)}, u32[]{:S(2)}, u32[]{:S(2)}) async-start(bf16[32,12,2048]{2,1,0:T(8,128)(2,1)} %reshape.96), calls=%async_computation | async-start | bytes 4194304 | tf_op jit(solution)/shard_map/all_to_all | solution.py:31
  29.7 180.3 %all-gather.11.cloned.1.call-start = ((), (), s32[]{:S(2)}) async-start(), calls=%async_computation.7 | async-start | bytes 3342336 | tf_op jit(solution)/shard_map/all_gather | solution.py:48
  129.7 15.0 %copy-start.1 = (bf16[384,2048]{1,0:T(8,128)(2,1)S(1)}, bf16[384,2048]{1,0:T(8,128)(2,1)}, u32[]{:S(2)}) copy-start(bf16[384,2048]{1,0:T(8,128)(2,1)} %reshape.97) | copy-start | bytes 4718596
  214.8 13.5 %copy-start.2 = (f32[32,8]{0,1:T(8,128)S(1)}, f32[32,8]{0,1:T(8,128)}, u32[]{:S(2)}) copy-start(f32[32,8]{0,1:T(8,128)} %param.9) | copy-start | bytes 3076
  214.8 13.6 %copy-start.3 = (f32[32]{0:T(128)S(1)}, f32[32]{0:T(128)}, u32[]{:S(2)}) copy-start(f32[32]{0:T(128)} %param.10) | copy-start | bytes 388
  214.8 112.1 %all-to-all-start.1 = ((bf16[32,12,2048]{2,1,0:T(8,128)(2,1)}), bf16[32,12,2048]{2,1,0:T(8,128)(2,1)S(1)}, u32[]{:S(2)}, u32[]{:S(2)}) async-start(bf16[32,12,2048]{2,1,0:T(8,128)(2,1)} %reshape.98), calls=%async_computation.1 | async-start | bytes 4194304 | tf_op jit(solution)/shard_map/all_to_all | solution.py:52
  228.3 297.0 %reduce-scatter.2.cloned.1.call-start = ((), (), s32[]{:S(2)}) async-start(), calls=%async_computation.4 | async-start | bytes 3342336 | tf_op jit(solution)/shard_map/reduce_scatter | solution.py:79
Sparse Core Ops, SparseCore 0:
  11.0 68.2 all-gather.6
  82.3 62.2 all-gather.8
  147.7 62.2 all-gather.10
  446.7 78.5 reduce-scatter.1
where the time goes:
time: 533 us; the launch traced here: 532 us
  waiting for transfers between devices  348 us (65%)
  blocking collectives  106 us (20%)
  starting transfers between devices  30.3 us (6%)
  matrix products  20.1 us (4%)
  between operations  13.9 us (3%)
  local copies, waits for them, and re-layouts  12.1 us (2%)
    all_to_all x1, blocking collectives, local(): lax.all_to_all(weighted_out.reshape(experts, capacity, width), 'expert',...  106 us
    all_to_all x1, waiting for transfers between devices, local(): lax.all_to_all(tangent.reshape(experts, capacity, width), 'expert', split...  98.3 us
    all_to_all x1, waiting for transfers between devices, local(): lax.all_to_all(outgoing.reshape(experts, capacity, width), 'expert', spli...  97.9 us
    reduce_scatter x1, waiting for transfers between devices, local(): lax.psum_scatter(lax.dot_general(weighted_rows, hidden, (((0,), (0,)), ((...  78 us
    all_gather x1, waiting for transfers between devices, local(): lax.all_gather(direction[0], 'dp', axis=0, tiled=True)  61.7 us
    all_to_all x1, starting transfers between devices, local(): lax.all_to_all(outgoing.reshape(experts, capacity, width), 'expert', spli...  16.7 us
    all_to_all x1, starting transfers between devices, local(): lax.all_to_all(tangent.reshape(experts, capacity, width), 'expert', split...  13.4 us
  transfers between devices with their start and end apart: 6, of which 5 were waited for; matrix products, arithmetic and copies ran while one was open for 3% of the time, Pallas kernels for 0%

commit v1 on v0

v1 whole, which is shorter than its diff:
```python
import jax
import jax.numpy as jnp
from jax import lax
from jax.sharding import Mesh, PartitionSpec as P

BF = jnp.bfloat16
F32 = jnp.float32


def fetch(value, axis, shift, size):
    return lax.ppermute(value, axis, [((i + shift) % size, i) for i in range(size)])


def ring4(value, axis):
    half = value.shape[-2] // 2
    after = fetch(value, axis, 1, 4)
    before = fetch(value, axis, -1, 4)
    low = fetch(after[..., :half, :], axis, 1, 4)
    high = fetch(before[..., half:, :], axis, -1, 4)
    return jnp.stack([value, after, jnp.concatenate([low, high], -2), before])


def turn(value, axis, start):
    doubled = jnp.concatenate([value, value], axis)
    return lax.dynamic_slice_in_dim(doubled, start, value.shape[axis], axis)


def to_relative(value, y, x):
    rows, width = value.shape
    value = turn(turn(value.reshape(rows, 4, 4, width // 16), 1, y), 2, x)
    first, second = jnp.split(value, 2, axis=3)
    second = second.swapaxes(1, 2)
    return jnp.concatenate([first.reshape(rows, -1), second.reshape(rows, -1)], 1)


def to_absolute(value, y, x):
    rows, width = value.shape
    first, second = jnp.split(value, 2, axis=1)
    first = first.reshape(rows, 4, 4, width // 32)
    second = second.reshape(rows, 4, 4, width // 32).swapaxes(1, 2)
    both = jnp.concatenate([first, second], 3)
    return turn(turn(both, 1, (4 - y) % 4), 2, (4 - x) % 4).reshape(rows, width)


def local(tokens, routes, gates, curvature, w_gate, w_up, direction):
    rows, width = tokens.shape
    hidden_width = w_gate.shape[2]
    z_count, cores = lax.axis_size("z"), lax.axis_size("c")
    experts = z_count * cores
    y, x, core = lax.axis_index("y"), lax.axis_index("x"), lax.axis_index("c")
    me = lax.axis_index(("z", "c"))

    chosen = routes[:, :, None] == jnp.arange(experts, dtype=jnp.int32)
    table = jnp.sum(jnp.where(chosen, gates[:, :, None], 0.0), axis=1)
    table_high = table.astype(BF)
    table_low = (table - table_high.astype(F32)).astype(BF)
    sent = jnp.concatenate(
        [
            to_relative(tokens, y, x),
            table_high,
            table_low,
            jnp.zeros((rows, 128 - 2 * experts), BF),
        ],
        1,
    )
    arrived = lax.all_gather(sent, ("z", "c"), axis=0, tiled=True)

    stacked = jnp.concatenate([w_gate[0], w_up[0], direction[0]], 1)
    half = stacked.shape[0] // 2
    first = ring4(ring4(stacked[:half], "x"), "y")
    second = ring4(ring4(stacked[half:], "y"), "x")
    weights = jnp.concatenate(
        [first.reshape(width // 2, -1), second.reshape(width // 2, -1)], 0
    )

    lanes = lax.broadcasted_iota(jnp.int32, (1, 128), 1)
    mine = (lanes == me) | (lanes == me + experts)
    share = jnp.sum(
        jnp.where(mine, arrived[:, width:].astype(F32), 0.0), axis=1, keepdims=True
    )
    group = arrived[:, :width]
    gate_pre = jnp.dot(group, weights[:, :hidden_width], preferred_element_type=F32)
    up_pre = jnp.dot(
        group, weights[:, hidden_width : 2 * hidden_width], preferred_element_type=F32
    )
    hidden = (jax.nn.silu(gate_pre) * up_pre * share).astype(BF)

    by_core = hidden.reshape(z_count, cores, rows, hidden_width)
    away = lax.dynamic_index_in_dim(by_core, 1 - core, 1, False).reshape(-1, hidden_width)
    home = lax.dynamic_index_in_dim(by_core, core, 1, False).reshape(-1, hidden_width)

    def tangent(part):
        return lax.dot_general(
            part,
            weights[:, 2 * hidden_width :],
            (((1,), (1,)), ((), ())),
            preferred_element_type=F32,
        )

    other = lax.ppermute(tangent(away).astype(BF), "c", [(0, 1), (1, 0)])
    paired = (tangent(home) + other.astype(F32)).astype(BF)
    jv = lax.psum_scatter(paired, "z", scatter_dimension=0, tiled=True)
    output_tangent = to_absolute(jv, y, x)
    curved = (curvature[:, None] * output_tangent.astype(F32)).astype(BF)
    spread = lax.all_gather(curved, ("z", "c"), axis=0, tiled=True)
    part = lax.dot_general(
        spread, hidden, (((0,), (0,)), ((), ())), preferred_element_type=F32
    ).astype(BF)

    def add_over(value, axis):
        value = value.reshape(4, -1, hidden_width)
        moved = lax.all_to_all(value, axis, 0, 0, tiled=True)
        return jnp.sum(moved.astype(F32), axis=0).astype(BF)

    product = add_over(add_over(part, "y"), "x")
    return output_tangent, product[None]


def solution(mesh):
    torus = Mesh(mesh.devices.reshape(4, 4, 16, 2), ("y", "x", "z", "c"))
    tokens = P(("y", "x", "z", "c"), None)
    matrix = P(("z", "c"), ("y", "x"), None)
    return jax.shard_map(
        local,
        mesh=torus,
        in_specs=(tokens, tokens, tokens, P(("y", "x", "z", "c")), matrix, matrix, matrix),
        out_specs=(tokens, matrix),
        check_vma=False,
    )
```

time: 533 us -> 354 us (0.66)
  waiting for transfers between devices: 348 us -> 174 us
  blocking collectives: 106 us -> 55.8 us
  starting transfers between devices: 30.3 us -> 59 us
  other arithmetic: 1.63 us -> 15 us
    all_to_all x2 -> x0, waiting for transfers between devices: 196 us -> none  [the longest x1 98.3 us: local(): lax.all_to_all(tangent.reshape(experts, capacity, width), 'expert', split...]
    ppermute x0 -> x17, starting transfers between devices: none -> 58.7 us  [the longest x16 49.2 us: fetch(): lax.ppermute(value, axis, [((i + shift) % size, i) for i in range(size)])]
    all_to_all x1 -> x2, blocking collectives: 106 us -> 55.8 us  [add_over(): moved = lax.all_to_all(value, axis, 0, 0, tiled=True)]
    all_to_all x2 -> x0, starting transfers between devices: 30.2 us -> none  [the longest x1 16.7 us: local(): lax.all_to_all(outgoing.reshape(experts, capacity, width), 'expert', spli...]
    ppermute x0 -> x17, waiting for transfers between devices: none -> 26 us  [the longest x16 22.2 us: fetch(): lax.ppermute(value, axis, [((i + shift) % size, i) for i in range(size)])]
    reduce_scatter x1, waiting for transfers between devices: 78 us -> 65.6 us  [local(): jv = lax.psum_scatter(paired, 'z', scatter_dimension=0, tiled=True)]
    all_gather x3 -> x2, waiting for transfers between devices: 71.8 us -> 82.8 us  [the longest x1 82.8 us: local(): spread = lax.all_gather(curved, ('z', 'c'), axis=0, tiled=True)]
    reshape x7 -> x8, local copies, waits for them, and re-layouts: 10.7 us -> 1.73 us  [the longest x2 1.03 us: to_relative(): value = turn(turn(value.reshape(rows, 4, 4, width // 16), 1, y), 2, x)]
  transfers between devices with their start and end apart: 6 -> 20, of which waited for: 5 -> 7; matrix products, arithmetic and copies ran while one was open for 3% -> 4% of each run, Pallas kernels for 0% -> 0%
where the time goes in v1:
time: 354 us; the launch traced here: 352 us
  waiting for transfers between devices  174 us (49%)
  starting transfers between devices  59 us (17%)
  blocking collectives  55.8 us (16%)
  matrix products  21.6 us (6%)
  other arithmetic  15 us (4%)
  between operations  14.4 us (4%)
  local copies, waits for them, and re-layouts  12.1 us (3%)
    all_gather x1, waiting for transfers between devices, local(): spread = lax.all_gather(curved, ('z', 'c'), axis=0, tiled=True)  82.8 us
    reduce_scatter x1, waiting for transfers between devices, local(): jv = lax.psum_scatter(paired, 'z', scatter_dimension=0, tiled=True)  65.6 us
    all_to_all x2, blocking collectives, add_over(): moved = lax.all_to_all(value, axis, 0, 0, tiled=True)  55.8 us
    ppermute x16, starting transfers between devices, fetch(): lax.ppermute(value, axis, [((i + shift) % size, i) for i in range(size)])  49.2 us
    ppermute x16, waiting for transfers between devices, fetch(): lax.ppermute(value, axis, [((i + shift) % size, i) for i in range(size)])  22.2 us
    ppermute x1, starting transfers between devices, local(): other = lax.ppermute(tangent(away).astype(BF), 'c', [(0, 1), (1, 0)])  9.5 us
    another operation x8, other arithmetic, ring4(): return jnp.stack([value, after, jnp.concatenate([low, high], -2), before])  7.98 us
    dot_general x1, matrix products, local(): jnp.dot(group, weights[:, :hidden_width], preferred_element_type=F32)  7.14 us
  transfers between devices with their start and end apart: 20, of which 7 were waited for; matrix products, arithmetic and copies ran while one was open for 4% of the time, Pallas kernels for 0%

profile of v1, /device:TPU:1, one launch (start us, length us, event | category | flops | bytes accessed | tf_op | source)
XLA Modules:
  0.0 352.4 jit_solution(16143572678705327174)
XLA Ops:
  13.0 4.0 %collective-permute-start.10 = (bf16[64,2304]{1,0:T(8,128)(2,1)S(1)}, bf16[64,2304]{1,0:T(8,128)(2,1)S(1)}, u32[]{:S(2)}, u32[]{:S(2)}) collective-permute-start(bf16[64,2304]{1,0:T(8,128)(2,1)S(1)} %get-tuple-element.12), channel_id=1, source_target_pairs={{384,0},{0,128},{128,256},{256,384},{385,1},{1,129},{129,257},{257... | collective-permute-start | bytes 884744 | tf_op jit(solution)/shard_map/ppermute | solution.py:11
  17.0 3.4 collective-permute-start.8
  20.4 4.4 %collective-permute-start = (bf16[64,2304]{1,0:T(8,128)(2,1)S(1)}, bf16[64,2304]{1,0:T(8,128)(2,1)S(1)}, u32[]{:S(2)}, u32[]{:S(2)}) collective-permute-start(bf16[64,2304]{1,0:T(8,128)(2,1)S(1)} %get-tuple-element.13), channel_id=1, source_target_pairs={{32,0},{64,32},{96,64},{0,96},{33,1},{65,33},{97,65},{1,97},{34,2}... | collective-permute-start | bytes 884744 | tf_op jit(solution)/shard_map/ppermute | solution.py:11
  24.8 1.9 collective-permute-start.2
  26.7 1.9 collective-permute-start.11
  28.7 4.6 %collective-permute-start.9 = (bf16[32,2304]{1,0:T(8,128)(2,1)S(1)}, bf16[32,2304]{1,0:T(8,128)(2,1)S(1)}, u32[]{:S(2)}, u32[]{:S(2)}) collective-permute-start(bf16[32,2304]{1,0:T(8,128)(2,1)S(1)} %slice.68), channel_id=1, source_target_pairs={{128,0},{256,128},{384,256},{0,384},{129,1},{257,129},{385,257},{1... | collective-permute-start | bytes 442376 | tf_op jit(solution)/shard_map/ppermute | solution.py:11
  33.3 4.6 %collective-permute-start.1 = (bf16[32,2304]{1,0:T(8,128)(2,1)S(1)}, bf16[32,2304]{1,0:T(8,128)(2,1)S(1)}, u32[]{:S(2)}, u32[]{:S(2)}) collective-permute-start(bf16[32,2304]{1,0:T(8,128)(2,1)S(1)} %slice.63), channel_id=1, source_target_pairs={{32,0},{64,32},{96,64},{0,96},{33,1},{65,33},{97,65},{1,97},{34,2}... | collective-permute-start | bytes 442376 | tf_op jit(solution)/shard_map/ppermute | solution.py:11
  37.9 1.9 collective-permute-start.3
  40.1 4.6 %collective-permute-start.12 = (bf16[4,64,2304]{2,1,0:T(8,128)(2,1)S(1)}, bf16[4,64,2304]{2,1,0:T(8,128)(2,1)S(1)}, u32[]{:S(2)}, u32[]{:S(2)}) collective-permute-start(bf16[4,64,2304]{2,1,0:T(8,128)(2,1)S(1)} %get-tuple-element.7), channel_id=1, source_target_pairs={{32,0},{64,32},{96,64},{0,96},{33,1},{65,33},{97,65},{1,97},{34,2}... | collective-permute-start | bytes 3538952 | tf_op jit(solution)/shard_map/ppermute | solution.py:11
  44.7 1.9 collective-permute-start.14
  46.9 2.2 collective-permute-start.4
  49.0 3.1 collective-permute-start.6
  52.2 14.6 %collective-permute-done.12 = bf16[4,64,2304]{2,1,0:T(8,128)(2,1)S(1)} collective-permute-done((bf16[4,64,2304]{2,1,0:T(8,128)(2,1)S(1)}, bf16[4,64,2304]{2,1,0:T(8,128)(2,1)S(1)}, u32[]{:S(2)}, u32[]{:S(2)}) %collective-permute-start.12) | collective-permute-done | bytes 1179680 | tf_op jit(solution)/shard_map/ppermute | solution.py:11
  67.6 3.4 collective-permute-start.13
  72.9 1.9 collective-permute-start.15
  76.8 2.3 collective-permute-start.5
  81.0 3.1 collective-permute-start.7
  88.0 5.1 %collective-permute-done.7 = bf16[4,32,2304]{2,1,0:T(8,128)(2,1)} collective-permute-done((bf16[4,32,2304]{2,1,0:T(8,128)(2,1)}, bf16[4,32,2304]{2,1,0:T(8,128)(2,1)}, u32[]{:S(2)}, u32[]{:S(2)}) %collective-permute-start.7) | collective-permute-done | bytes 589856 | tf_op jit(solution)/shard_map/ppermute | solution.py:11
  94.5 2.5 pad_maximum_fusion.1
  97.0 2.5 pad_maximum_fusion
  100.7 7.1 %fusion.2 = f32[1024,768]{1,0:T(8,128)S(1)} fusion(bf16[1024,2176]{1,0:T(8,128)(2,1)} %all-gather.3.cloned.1.call-done, bf16[1024,2304]{1,0:T(8,128)(2,1)} %bitcast.48, bf16[1024,2304]{1,0:T(8,128)(2,1)} %bitcast.42), kind=kOutput, calls=%fused_computation.9 | convolution fusion | flops 3227516928 | bytes 16777216 | tf_op jit(solution)/shard_map/dot_general | solution.py:82
  108.0 3.7 %multiply_convert_fusion = bf16[1024,768]{1,0:T(8,128)(2,1)S(1)} fusion(f32[1024,768]{1,0:T(8,128)S(1)} %fusion.2, f32[1024]{0:T(1024)S(1)} %select_reduce_fusion, bf16[1024,2304]{1,0:T(8,128)(2,1)S(1)} %bitcast.51, bf16[1024,2304]{1,0:T(8,128)(2,1)S(1)} %bitcast.45, bf16[1024,2176]{1,0:T(8,128)(2,1)S(1)} %bitcast.73), kind=kOutput, calls=%fused_computation.15 | convolution fusion | flops 3233021952 | bytes 18354176 | tf_op jit(solution)/shard_map/dot_general | solution.py:83
  111.8 1.8 convolution_convert_fusion.1
  113.7 9.5 %collective-permute-start.16 = (bf16[512,2048]{1,0:T(8,128)(2,1)S(1)}, bf16[512,2048]{1,0:T(8,128)(2,1)S(1)}, u32[]{:S(2)}, u32[]{:S(2)}) collective-permute-start(bf16[512,2048]{1,0:T(8,128)(2,1)S(1)} %convolution_convert_fusion.1), channel_id=1, source_target_pairs={{0,1},{1,0},{2,3},{3,2},{4,5},{5,4},{6,7},{7,6},{8,9},{9,8},{10,11... | collective-permute-start | bytes 6291464 | tf_op jit(solution)/shard_map/ppermute | solution.py:100
  123.2 3.8 %collective-permute-done.16 = bf16[512,2048]{1,0:T(8,128)(2,1)S(1)} collective-permute-done((bf16[512,2048]{1,0:T(8,128)(2,1)S(1)}, bf16[512,2048]{1,0:T(8,128)(2,1)S(1)}, u32[]{:S(2)}, u32[]{:S(2)}) %collective-permute-start.16) | collective-permute-done | bytes 2097184 | tf_op jit(solution)/shard_map/ppermute | solution.py:100
  126.9 3.2 add_convert_fusion
  130.5 65.6 %reduce-scatter.2.cloned.1.call-done = bf16[32,2048]{1,0:T(8,128)(2,1)} async-done(((bf16[512,2048]{1,0:T(8,128)(2,1)}), bf16[32,2048]{1,0:T(8,128)(2,1)}) %reduce-scatter.2.cloned.1.call-update) | async-done | bytes 131088 | tf_op jit(solution)/shard_map/reduce_scatter | solution.py:102
  199.2 82.8 %all-gather.5.cloned.1.call-done = bf16[1024,2048]{1,0:T(8,128)(2,1)} async-done(((bf16[32,2048]{1,0:T(8,128)(2,1)}), bf16[1024,2048]{1,0:T(8,128)(2,1)}) %all-gather.5.cloned.1.call-update) | async-done | bytes 4194320 | tf_op jit(solution)/shard_map/all_gather | solution.py:105
  281.9 5.7 %convolution_convert_fusion = bf16[2048,768]{1,0:T(8,128)(2,1)S(1)} fusion(bf16[1024,2048]{1,0:T(8,128)(2,1)} %all-gather.5.cloned.1.call-done, bf16[1024,768]{1,0:T(8,128)(2,1)S(1)} %multiply_convert_fusion), kind=kOutput, calls=%fused_computation.11 | convolution fusion | flops 3222798336 | bytes 8912896 | tf_op jit(solution)/shard_map/dot_general | solution.py:106
  287.7 41.2 %all_to_all.10 = bf16[4,512,768]{2,1,0:T(8,128)(2,1)S(1)} all-to-all(bf16[4,512,768]{2,1,0:T(8,128)(2,1)S(1)} %bitcast.55), channel_id=1, replica_groups=mesh['y'=4,'x'=4,'z'=16,'c'=2] {'y'}, dimensions={0} | all-to-all | bytes 6291456 | tf_op jit(solution)/shard_map/all_to_all | solution.py:112
  328.9 1.6 reduce_sum.44
  330.5 14.6 %all_to_all.11 = bf16[4,128,768]{2,1,0:T(8,128)(2,1)S(1)} all-to-all(bf16[4,128,768]{2,1,0:T(8,128)(2,1)} %bitcast.57), channel_id=1, replica_groups=mesh['y'=4,'x'=4,'z'=16,'c'=2] {'x'}, dimensions={0} | all-to-all | bytes 1572864 | tf_op jit(solution)/shard_map/all_to_all | solution.py:112
  (95 shorter events, 23.5 us)
Async XLA Ops:
  7.2 92.3 %all-gather.3.cloned.1.call-start = ((), (), s32[]{:S(2)}) async-start(), calls=%async_computation.3 | async-start | bytes 4595712 | tf_op jit(solution)/shard_map/all_gather | solution.py:66
  11.7 184.5 %reduce-scatter.2.cloned.1.call-start = ((), (), s32[]{:S(2)}) async-start(), calls=%async_computation.4 | async-start | bytes 2228224 | tf_op jit(solution)/shard_map/reduce_scatter | solution.py:102
  13.0 13.7 %collective-permute-start.10 = (bf16[64,2304]{1,0:T(8,128)(2,1)S(1)}, bf16[64,2304]{1,0:T(8,128)(2,1)S(1)}, u32[]{:S(2)}, u32[]{:S(2)}) collective-permute-start(bf16[64,2304]{1,0:T(8,128)(2,1)S(1)} %get-tuple-element.12), channel_id=1, source_target_pairs={{384,0},{0,128},{128,256},{256,384},{385,1},{1,129},{129,257},{257... | collective-permute-start | bytes 884744 | tf_op jit(solution)/shard_map/ppermute | solution.py:11
  17.0 11.7 %collective-permute-start.8 = (bf16[64,2304]{1,0:T(8,128)(2,1)S(1)}, bf16[64,2304]{1,0:T(8,128)(2,1)S(1)}, u32[]{:S(2)}, u32[]{:S(2)}) collective-permute-start(bf16[64,2304]{1,0:T(8,128)(2,1)S(1)} %get-tuple-element.12), channel_id=1, source_target_pairs={{128,0},{256,128},{384,256},{0,384},{129,1},{257,129},{385,257},{1... | collective-permute-start | bytes 884744 | tf_op jit(solution)/shard_map/ppermute | solution.py:11
  20.4 12.9 %collective-permute-start = (bf16[64,2304]{1,0:T(8,128)(2,1)S(1)}, bf16[64,2304]{1,0:T(8,128)(2,1)S(1)}, u32[]{:S(2)}, u32[]{:S(2)}) collective-permute-start(bf16[64,2304]{1,0:T(8,128)(2,1)S(1)} %get-tuple-element.13), channel_id=1, source_target_pairs={{32,0},{64,32},{96,64},{0,96},{33,1},{65,33},{97,65},{1,97},{34,2}... | collective-permute-start | bytes 884744 | tf_op jit(solution)/shard_map/ppermute | solution.py:11
  24.8 13.1 %collective-permute-start.2 = (bf16[64,2304]{1,0:T(8,128)(2,1)S(1)}, bf16[64,2304]{1,0:T(8,128)(2,1)S(1)}, u32[]{:S(2)}, u32[]{:S(2)}) collective-permute-start(bf16[64,2304]{1,0:T(8,128)(2,1)S(1)} %get-tuple-element.13), channel_id=1, source_target_pairs={{96,0},{0,32},{32,64},{64,96},{97,1},{1,33},{33,65},{65,97},{98,2}... | collective-permute-start | bytes 884744 | tf_op jit(solution)/shard_map/ppermute | solution.py:11
  26.7 13.1 %collective-permute-start.11 = (bf16[32,2304]{1,0:T(8,128)(2,1)S(1)}, bf16[32,2304]{1,0:T(8,128)(2,1)S(1)}, u32[]{:S(2)}, u32[]{:S(2)}) collective-permute-start(bf16[32,2304]{1,0:T(8,128)(2,1)S(1)} %slice.69), channel_id=1, source_target_pairs={{384,0},{0,128},{128,256},{256,384},{385,1},{1,129},{129,257},{257... | collective-permute-start | bytes 442376 | tf_op jit(solution)/shard_map/ppermute | solution.py:11
  28.7 11.2 %collective-permute-start.9 = (bf16[32,2304]{1,0:T(8,128)(2,1)S(1)}, bf16[32,2304]{1,0:T(8,128)(2,1)S(1)}, u32[]{:S(2)}, u32[]{:S(2)}) collective-permute-start(bf16[32,2304]{1,0:T(8,128)(2,1)S(1)} %slice.68), channel_id=1, source_target_pairs={{128,0},{256,128},{384,256},{0,384},{129,1},{257,129},{385,257},{1... | collective-permute-start | bytes 442376 | tf_op jit(solution)/shard_map/ppermute | solution.py:11
  33.3 13.3 %collective-permute-start.1 = (bf16[32,2304]{1,0:T(8,128)(2,1)S(1)}, bf16[32,2304]{1,0:T(8,128)(2,1)S(1)}, u32[]{:S(2)}, u32[]{:S(2)}) collective-permute-start(bf16[32,2304]{1,0:T(8,128)(2,1)S(1)} %slice.63), channel_id=1, source_target_pairs={{32,0},{64,32},{96,64},{0,96},{33,1},{65,33},{97,65},{1,97},{34,2}... | collective-permute-start | bytes 442376 | tf_op jit(solution)/shard_map/ppermute | solution.py:11
  37.9 8.7 %collective-permute-start.3 = (bf16[32,2304]{1,0:T(8,128)(2,1)S(1)}, bf16[32,2304]{1,0:T(8,128)(2,1)S(1)}, u32[]{:S(2)}, u32[]{:S(2)}) collective-permute-start(bf16[32,2304]{1,0:T(8,128)(2,1)S(1)} %slice.64), channel_id=1, source_target_pairs={{96,0},{0,32},{32,64},{64,96},{97,1},{1,33},{33,65},{65,97},{98,2}... | collective-permute-start | bytes 442376 | tf_op jit(solution)/shard_map/ppermute | solution.py:11
  40.1 26.6 %collective-permute-start.12 = (bf16[4,64,2304]{2,1,0:T(8,128)(2,1)S(1)}, bf16[4,64,2304]{2,1,0:T(8,128)(2,1)S(1)}, u32[]{:S(2)}, u32[]{:S(2)}) collective-permute-start(bf16[4,64,2304]{2,1,0:T(8,128)(2,1)S(1)} %get-tuple-element.7), channel_id=1, source_target_pairs={{32,0},{64,32},{96,64},{0,96},{33,1},{65,33},{97,65},{1,97},{34,2}... | collective-permute-start | bytes 3538952 | tf_op jit(solution)/shard_map/ppermute | solution.py:11
  44.7 26.4 %collective-permute-start.14 = (bf16[4,64,2304]{2,1,0:T(8,128)(2,1)S(1)}, bf16[4,64,2304]{2,1,0:T(8,128)(2,1)S(1)}, u32[]{:S(2)}, u32[]{:S(2)}) collective-permute-start(bf16[4,64,2304]{2,1,0:T(8,128)(2,1)S(1)} %get-tuple-element.7), channel_id=1, source_target_pairs={{96,0},{0,32},{32,64},{64,96},{97,1},{1,33},{33,65},{65,97},{98,2}... | collective-permute-start | bytes 3538952 | tf_op jit(solution)/shard_map/ppermute | solution.py:11
  46.9 28.0 %collective-permute-start.4 = (bf16[4,64,2304]{2,1,0:T(8,128)(2,1)S(1)}, bf16[4,64,2304]{2,1,0:T(8,128)(2,1)S(1)}, u32[]{:S(2)}, u32[]{:S(2)}) collective-permute-start(bf16[4,64,2304]{2,1,0:T(8,128)(2,1)S(1)} %get-tuple-element.9), channel_id=1, source_target_pairs={{128,0},{256,128},{384,256},{0,384},{129,1},{257,129},{385,257},{1... | collective-permute-start | bytes 3538952 | tf_op jit(solution)/shard_map/ppermute | solution.py:11
  49.0 30.1 %collective-permute-start.6 = (bf16[4,64,2304]{2,1,0:T(8,128)(2,1)S(1)}, bf16[4,64,2304]{2,1,0:T(8,128)(2,1)S(1)}, u32[]{:S(2)}, u32[]{:S(2)}) collective-permute-start(bf16[4,64,2304]{2,1,0:T(8,128)(2,1)S(1)} %get-tuple-element.9), channel_id=1, source_target_pairs={{384,0},{0,128},{128,256},{256,384},{385,1},{1,129},{129,257},{257... | collective-permute-start | bytes 3538952 | tf_op jit(solution)/shard_map/ppermute | solution.py:11
  67.6 16.6 %collective-permute-start.13 = (bf16[4,32,2304]{2,1,0:T(8,128)(2,1)}, bf16[4,32,2304]{2,1,0:T(8,128)(2,1)}, u32[]{:S(2)}, u32[]{:S(2)}) collective-permute-start(bf16[4,32,2304]{2,1,0:T(8,128)(2,1)} %slice.70), channel_id=1, source_target_pairs={{32,0},{64,32},{96,64},{0,96},{33,1},{65,33},{97,65},{1,97},{34,2}... | collective-permute-start | bytes 1769480 | tf_op jit(solution)/shard_map/ppermute | solution.py:11
  72.9 12.3 %collective-permute-start.15 = (bf16[4,32,2304]{2,1,0:T(8,128)(2,1)}, bf16[4,32,2304]{2,1,0:T(8,128)(2,1)}, u32[]{:S(2)}, u32[]{:S(2)}) collective-permute-start(bf16[4,32,2304]{2,1,0:T(8,128)(2,1)} %slice.71), channel_id=1, source_target_pairs={{96,0},{0,32},{32,64},{64,96},{97,1},{1,33},{33,65},{65,97},{98,2}... | collective-permute-start | bytes 1769480 | tf_op jit(solution)/shard_map/ppermute | solution.py:11
  74.9 1.1 copy-start.2
  76.8 11.2 %collective-permute-start.5 = (bf16[4,32,2304]{2,1,0:T(8,128)(2,1)}, bf16[4,32,2304]{2,1,0:T(8,128)(2,1)}, u32[]{:S(2)}, u32[]{:S(2)}) collective-permute-start(bf16[4,32,2304]{2,1,0:T(8,128)(2,1)} %slice.65), channel_id=1, source_target_pairs={{128,0},{256,128},{384,256},{0,384},{129,1},{257,129},{385,257},{1... | collective-permute-start | bytes 1769480 | tf_op jit(solution)/shard_map/ppermute | solution.py:11
  81.0 12.1 %collective-permute-start.7 = (bf16[4,32,2304]{2,1,0:T(8,128)(2,1)}, bf16[4,32,2304]{2,1,0:T(8,128)(2,1)}, u32[]{:S(2)}, u32[]{:S(2)}) collective-permute-start(bf16[4,32,2304]{2,1,0:T(8,128)(2,1)} %slice.66), channel_id=1, source_target_pairs={{384,0},{0,128},{128,256},{256,384},{385,1},{1,129},{129,257},{257... | collective-permute-start | bytes 1769480 | tf_op jit(solution)/shard_map/ppermute | solution.py:11
  84.2 10.3 %copy-start.1 = (bf16[4,64,2304]{2,1,0:T(8,128)(2,1)S(1)}, bf16[4,64,2304]{2,1,0:T(8,128)(2,1)}, u32[]{:S(2)}) copy-start(bf16[4,64,2304]{2,1,0:T(8,128)(2,1)} %copy-done) | copy-start | bytes 3538948
  94.5 2.5 copy-start.3
  94.5 2.5 copy-start.5
  97.0 10.9 %slice-start = ((s8[4718592]{0:T(1024)(128)(4,1)}), s8[524288]{0:T(1024)(128)(4,1)S(1)}, s32[]{:S(2)}) async-start(s8[4718592]{0:T(1024)(128)(4,1)} %bitcast.43), calls=%async_computation.6 | async-start | bytes 1048576
  99.5 8.4 %slice-start.2 = ((s8[4718592]{0:T(1024)(128)(4,1)}), s8[4194304]{0:T(1024)(128)(4,1)S(1)}, s32[]{:S(2)}) async-start(s8[4718592]{0:T(1024)(128)(4,1)} %bitcast.49), calls=%async_computation.8 | async-start | bytes 8388608
  99.5 8.4 %slice-start.4 = ((s8[4456448]{0:T(1024)(128)(4,1)}), s8[4194304]{0:T(1024)(128)(4,1)S(1)}, s32[]{:S(2)}) async-start(s8[4456448]{0:T(1024)(128)(4,1)} %bitcast.72), calls=%async_computation.10 | async-start | bytes 8388608
  100.7 7.2 %slice-start.1 = ((s8[4718592]{0:T(1024)(128)(4,1)}), s8[4194304]{0:T(1024)(128)(4,1)S(1)}, s32[]{:S(2)}) async-start(s8[4718592]{0:T(1024)(128)(4,1)} %bitcast.43), calls=%async_computation.7 | async-start | bytes 8388608
  100.7 7.2 %slice-start.3 = ((s8[4718592]{0:T(1024)(128)(4,1)}), s8[524288]{0:T(1024)(128)(4,1)S(1)}, s32[]{:S(2)}) async-start(s8[4718592]{0:T(1024)(128)(4,1)} %bitcast.49), calls=%async_computation.9 | async-start | bytes 1048576
  100.7 7.2 %slice-start.5 = ((s8[4456448]{0:T(1024)(128)(4,1)}), s8[262144]{0:T(1024)(128)(4,1)S(1)}, s32[]{:S(2)}) async-start(s8[4456448]{0:T(1024)(128)(4,1)} %bitcast.72), calls=%async_computation.11 | async-start | bytes 524288
  113.7 13.3 %collective-permute-start.16 = (bf16[512,2048]{1,0:T(8,128)(2,1)S(1)}, bf16[512,2048]{1,0:T(8,128)(2,1)S(1)}, u32[]{:S(2)}, u32[]{:S(2)}) collective-permute-start(bf16[512,2048]{1,0:T(8,128)(2,1)S(1)} %convolution_convert_fusion.1), channel_id=1, source_target_pairs={{0,1},{1,0},{2,3},{3,2},{4,5},{5,4},{6,7},{7,6},{8,9},{9,8},{10,11... | collective-permute-start | bytes 6291464 | tf_op jit(solution)/shard_map/ppermute | solution.py:100
  130.2 68.2 %copy-start.7 = (f32[32]{0:T(128)S(1)}, f32[32]{0:T(128)}, u32[]{:S(2)}) copy-start(f32[32]{0:T(128)} %param.10) | copy-start | bytes 388
  130.2 151.8 %all-gather.5.cloned.1.call-start = ((), (), s32[]{:S(2)}) async-start(), calls=%async_computation.5 | async-start | bytes 4325376 | tf_op jit(solution)/shard_map/all_gather | solution.py:105
  198.4 89.3 %copy-start.6 = (bf16[32,2048]{1,0:T(8,128)(2,1)}, bf16[32,2048]{1,0:T(8,128)(2,1)S(1)}, u32[]{:S(2)}) copy-start(bf16[32,2048]{1,0:T(8,128)(2,1)S(1)} %reshape.70) | copy-start | bytes 393220
  (2 other events, 2.1 us)
Sparse Core Ops, SparseCore 0:
  11.8 80.2 all-gather.2
  130.3 65.7 reduce-scatter.1
  199.3 82.6 all-gather.4

commit v2 on v1

v2 whole, which is shorter than its diff:
```python
import jax
import jax.numpy as jnp
from jax import lax
from jax.sharding import Mesh, PartitionSpec as P

BF = jnp.bfloat16
F32 = jnp.float32
FAR = (-6, -3, 0, 3, 6)


def fetch(value, axis, shift, size):
    return lax.ppermute(value, axis, [((i + shift) % size, i) for i in range(size)])


def swap_cores(value):
    return lax.ppermute(value, "c", [(0, 1), (1, 0)])


def ring4_one(value, axis):
    return value, fetch(value, axis, 1, 4), fetch(value, axis, -1, 4)


def ring4_two(hop, axis):
    value, ahead, behind = hop
    half = value.shape[-2] // 2
    low = fetch(ahead[..., :half, :], axis, 1, 4)
    high = fetch(behind[..., half:, :], axis, -1, 4)
    return jnp.stack([value, ahead, jnp.concatenate([low, high], -2), behind])


def ring4(value, axis):
    return ring4_two(ring4_one(value, axis), axis)


def turn(value, axis, start):
    doubled = jnp.concatenate([value, value], axis)
    return lax.dynamic_slice_in_dim(doubled, start, value.shape[axis], axis)


def to_relative(value, y, x):
    rows, width = value.shape
    value = turn(turn(value.reshape(rows, 4, 4, width // 16), 1, y), 2, x)
    first, second = jnp.split(value, 2, axis=3)
    second = second.swapaxes(1, 2)
    return jnp.concatenate([first.reshape(rows, -1), second.reshape(rows, -1)], 1)


def to_absolute(value, y, x, flip):
    rows, width = value.shape
    value = value.reshape(rows, 4, 4, width // 16)
    if flip:
        value = value.swapaxes(1, 2)
    return turn(turn(value, 1, (4 - y) % 4), 2, (4 - x) % 4)


def after(value, *others):
    return lax.optimization_barrier((value,) + others)[0]


def reduce_near(parts, rows):
    block, half = len(FAR) * rows, rows // 2
    behind, own, ahead, across = jnp.split(parts, [block, 2 * block, 3 * block])
    return (
        own,
        fetch(ahead, "z", -1, 16),
        fetch(behind, "z", 1, 16),
        fetch(across[:half], "z", -2, 16),
        fetch(across[half:], "z", 2, 16),
    )


def reduce_far(own, ahead, behind, low, high):
    half = low.shape[0]
    total = own.astype(F32) + ahead.astype(F32) + behind.astype(F32)
    pieces = jnp.split(total, len(FAR))
    pieces[0] = jnp.concatenate([pieces[0][:half], pieces[0][half:] + high.astype(F32)])
    pieces[-1] = jnp.concatenate([pieces[-1][:half] + low.astype(F32), pieces[-1][half:]])
    moved = [fetch(p.astype(BF), "z", -o, 16) if o else p for o, p in zip(FAR, pieces)]
    return moved


def spread_near(own, rows):
    half = rows // 2
    return (
        fetch(own, "z", -1, 16),
        own,
        fetch(own, "z", 1, 16),
        fetch(own[-rows:][:half], "z", 2, 16),
        fetch(own[:rows][half:], "z", -2, 16),
    )


def local(tokens, routes, gates, curvature, w_gate, w_up, direction):
    rows, width = tokens.shape
    hidden_width = w_gate.shape[2]
    z_count, cores = lax.axis_size("z"), lax.axis_size("c")
    experts = z_count * cores
    y, x, z, core = (lax.axis_index(name) for name in ("y", "x", "z", "c"))
    me = z * cores + core

    chosen = routes[:, :, None] == jnp.arange(experts, dtype=jnp.int32)
    table = jnp.sum(jnp.where(chosen, gates[:, :, None], 0.0), axis=1)
    table_high = table.astype(BF)
    table_low = (table - table_high.astype(F32)).astype(BF)
    sent = jnp.concatenate(
        [
            to_relative(tokens, y, x),
            table_high,
            table_low,
            jnp.zeros((rows, 128 - 2 * experts), BF),
        ],
        1,
    )
    arrived = lax.all_gather(sent, ("z", "c"), axis=0, tiled=True)

    stacked = jnp.concatenate([w_gate[0], w_up[0], direction[0]], 1)
    half = stacked.shape[0] // 2
    first = ring4(stacked[:half], "x")
    second = ring4(stacked[half:], "y")
    cut = 2 * hidden_width
    first_hop = ring4_one(first[..., :cut], "y")
    second_hop = ring4_one(second[..., :cut], "x")
    first_hop, second_hop, first_back, second_back = lax.optimization_barrier(
        (first_hop, second_hop, first[..., cut:], second[..., cut:])
    )
    first_in = ring4_two(first_hop, "y").reshape(width // 2, -1)
    second_in = ring4_two(second_hop, "x").reshape(width // 2, -1)
    back = (
        ring4(first_back, "y").reshape(width // 2, -1),
        ring4(second_back, "x").reshape(width // 2, -1),
    )
    weights = jnp.concatenate([first_in, second_in], 0)

    lanes = lax.broadcasted_iota(jnp.int32, (1, 128), 1)
    mine = (lanes == me) | (lanes == me + experts)
    share = jnp.sum(
        jnp.where(mine, arrived[:, width:].astype(F32), 0.0), axis=1, keepdims=True
    )
    group = arrived[:, :width]
    gate_pre = jnp.dot(group, weights[:, :hidden_width], preferred_element_type=F32)
    up_pre = jnp.dot(group, weights[:, hidden_width:], preferred_element_type=F32)
    hidden = (jax.nn.silu(gate_pre) * up_pre * share).astype(BF)

    by_core = hidden.reshape(z_count, cores, rows, hidden_width)
    by_core = jnp.concatenate([by_core, by_core], 0)
    start = (z + 9) % 16

    def of_core(which):
        turned = lax.dynamic_slice(
            by_core, (start, which, 0, 0), (z_count, 1, rows, hidden_width)
        )
        grouped = turned[:-1].reshape(len(FAR), 3, rows, hidden_width).swapaxes(0, 1)
        return jnp.concatenate(
            [grouped.reshape(-1, hidden_width), turned[-1, 0]]
        )

    home, away = of_core(core), of_core(1 - core)

    def paired(matrix):
        def tangent(part):
            return lax.dot_general(
                part, matrix, (((1,), (1,)), ((), ())), preferred_element_type=F32
            )

        other = swap_cores(tangent(away).astype(BF))
        return (tangent(home) + other.astype(F32)).astype(BF)

    def settle(pieces, flip):
        jv = to_absolute(sum(p.astype(F32) for p in pieces), y, x, flip)
        curved = (curvature[:, None, None, None] * jv).astype(BF).reshape(rows, -1)
        return jv.astype(BF), curved

    def spread_far(curved):
        return jnp.concatenate([fetch(curved, "z", o, 16) if o else curved for o in FAR])

    def outer(near, away_near):
        def product(left, right):
            return lax.dot_general(
                left, right, (((0,), (0,)), ((), ())), preferred_element_type=F32
            )

        return (product(near, home) + product(away_near, away)).astype(BF)

    near_0 = reduce_near(paired(back[0]), rows)
    parts_1 = after(paired(back[1]), *near_0)
    far_0 = reduce_far(*near_0)
    near_1 = reduce_near(parts_1, rows)
    out_0, curved_0 = settle(far_0, False)
    own_0 = spread_far(curved_0)
    near_1 = lax.optimization_barrier(near_1 + tuple(far_0))[: len(near_1)]
    far_1 = reduce_far(*near_1)
    near_0 = spread_near(own_0, rows)
    out_1, curved_1 = settle(far_1, True)
    own_1 = spread_far(after(curved_1, own_0))
    near_0 = jnp.concatenate(near_0)
    away_0 = swap_cores(near_0)
    near_1 = spread_near(after(own_1, near_0), rows)
    part_0 = outer(near_0, away_0)
    near_1 = jnp.concatenate(
        lax.optimization_barrier(near_1 + (part_0,))[: len(near_1)]
    )
    away_1 = swap_cores(near_1)
    product_0 = lax.psum_scatter(part_0, ("y", "x"), scatter_dimension=0, tiled=True)
    product_1 = outer(near_1, away_1)
    for axis in ("y", "x"):
        moved = lax.all_to_all(
            product_1.reshape(4, -1, hidden_width), axis, 0, 0, tiled=True
        )
        product_1 = jnp.sum(moved.astype(F32), axis=0).astype(BF)
    output_tangent = jnp.concatenate([out_0, out_1], 3).reshape(rows, width)
    return output_tangent, jnp.concatenate([product_0, product_1])[None]


def solution(mesh):
    torus = Mesh(mesh.devices.reshape(4, 4, 16, 2), ("y", "x", "z", "c"))
    tokens = P(("y", "x", "z", "c"), None)
    matrix = P(("z", "c"), ("y", "x"), None)
    return jax.shard_map(
        local,
        mesh=torus,
        in_specs=(tokens, tokens, tokens, P(("y", "x", "z", "c")), matrix, matrix, matrix),
        out_specs=(tokens, matrix),
        check_vma=False,
    )
```

time: 354 us -> 461 us (1.30)
  starting transfers between devices: 59 us -> 249 us
  waiting for transfers between devices: 174 us -> 94.9 us
  blocking collectives: 55.8 us -> 25.8 us
  local copies, waits for them, and re-layouts: 12.1 us -> 25.4 us
  matrix products: 21.6 us -> 26.8 us
  other arithmetic: 15 us -> 19.7 us
    ppermute x16 -> x56, starting transfers between devices: 49.2 us -> 219 us  [fetch(): lax.ppermute(value, axis, [((i + shift) % size, i) for i in range(size)])]
    all_gather x1 -> x0, waiting for transfers between devices: 82.8 us -> none  [local(): spread = lax.all_gather(curved, ('z', 'c'), axis=0, tiled=True)]
    all_to_all x2 -> x1, blocking collectives: 55.8 us -> 25.8 us  [local(): lax.all_to_all(product_1.reshape(4, -1, hidden_width), axis, 0, 0, tiled=...]
    reduce_scatter x1, waiting for transfers between devices: 65.6 us -> 37.5 us  [local(): lax.psum_scatter(part_0, ('y', 'x'), scatter_dimension=0, tiled=True)]
    ppermute x16 -> x56, waiting for transfers between devices: 22.2 us -> 48.8 us  [fetch(): lax.ppermute(value, axis, [((i + shift) % size, i) for i in range(size)])]
    ppermute x1 -> x4, starting transfers between devices: 9.5 us -> 26.8 us  [swap_cores(): return lax.ppermute(value, 'c', [(0, 1), (1, 0)])]
    unnamed x30 -> x64, local copies, waits for them, and re-layouts: 4.7 us -> 12.1 us
    dot_general x4 -> x9, matrix products: 14.5 us -> 20.6 us  [the longest x4 9.09 us: tangent(): lax.dot_general(part, matrix, (((1,), (1,)), ((), ())), preferred_element...]
  transfers between devices with their start and end apart: 20 -> 63, of which waited for: 7 -> 20; matrix products, arithmetic and copies ran while one was open for 4% -> 12% of each run, Pallas kernels for 0% -> 0%
where the time goes in v2:
time: 461 us; the launch traced here: 458 us
  starting transfers between devices  249 us (54%)
  waiting for transfers between devices  94.9 us (21%)
  matrix products  26.8 us (6%)
  blocking collectives  25.8 us (6%)
  local copies, waits for them, and re-layouts  25.4 us (6%)
  other arithmetic  19.7 us (4%)
  between operations  15.7 us (3%)
    ppermute x56, starting transfers between devices, fetch(): lax.ppermute(value, axis, [((i + shift) % size, i) for i in range(size)])  219 us
    ppermute x56, waiting for transfers between devices, fetch(): lax.ppermute(value, axis, [((i + shift) % size, i) for i in range(size)])  48.8 us
    reduce_scatter x1, waiting for transfers between devices, local(): lax.psum_scatter(part_0, ('y', 'x'), scatter_dimension=0, tiled=True)  37.5 us
    ppermute x4, starting transfers between devices, swap_cores(): return lax.ppermute(value, 'c', [(0, 1), (1, 0)])  26.8 us
    all_to_all x1, blocking collectives, local(): lax.all_to_all(product_1.reshape(4, -1, hidden_width), axis, 0, 0, tiled=...  25.8 us
    unnamed x64, local copies, waits for them, and re-layouts  12.1 us
    another operation x12, other arithmetic, ring4_two(): return jnp.stack([value, ahead, jnp.concatenate([low, high], -2), behind])  10.7 us
  transfers between devices with their start and end apart: 63, of which 20 were waited for; matrix products, arithmetic and copies ran while one was open for 12% of the time, Pallas kernels for 0%

profile of v2, /device:TPU:1, one launch (start us, length us, event | category | flops | bytes accessed | tf_op | source)
XLA Modules:
  0.0 457.8 jit_solution(3588422679878614595)
XLA Ops:
  10.7 5.5 %collective-permute-start.6 = (bf16[64,2304]{1,0:T(8,128)(2,1)S(1)}, bf16[64,2304]{1,0:T(8,128)(2,1)S(1)}, u32[]{:S(2)}, u32[]{:S(2)}) collective-permute-start(bf16[64,2304]{1,0:T(8,128)(2,1)S(1)} %get-tuple-element.67), channel_id=1, source_target_pairs={{128,0},{256,128},{384,256},{0,384},{129,1},{257,129},{385,257},{1... | collective-permute-start | bytes 884744 | tf_op jit(solution)/shard_map/ppermute | solution.py:12
  31.0 4.6 collective-permute-start.1
  37.8 4.6 collective-permute-start.10
  56.2 5.0 %collective-permute-done.11 = bf16[4,64,1536]{2,1,0:T(8,128)(2,1)S(1)} collective-permute-done((bf16[4,64,1536]{2,1,0:T(8,128)(2,1)S(1)}, bf16[4,64,1536]{2,1,0:T(8,128)(2,1)S(1)}, u32[]{:S(2)}, u32[]{:S(2)}) %collective-permute-start.11) | collective-permute-done | bytes 786464 | tf_op jit(solution)/shard_map/ppermute | solution.py:12
  62.8 5.1 %collective-permute-done.5 = bf16[4,64,1536]{2,1,0:T(8,128)(2,1)S(1)} collective-permute-done((bf16[4,64,1536]{2,1,0:T(8,128)(2,1)S(1)}, bf16[4,64,1536]{2,1,0:T(8,128)(2,1)S(1)}, u32[]{:S(2)}, u32[]{:S(2)}) %collective-permute-start.5) | collective-permute-done | bytes 786464 | tf_op jit(solution)/shard_map/ppermute | solution.py:12
  88.9 4.6 collective-permute-start.29
  114.1 6.2 %fusion.2 = f32[1024,768]{1,0:T(8,128)S(1)} fusion(bf16[1024,2176]{1,0:T(8,128)(2,1)} %all-gather.2.cloned.1.call-done, bf16[1024,1536]{1,0:T(8,128)(2,1)} %bitcast.82, bf16[1024,1536]{1,0:T(8,128)(2,1)S(1)} %bitcast.80), kind=kOutput, calls=%fused_computation.4 | convolution fusion | flops 3227516928 | bytes 13631488 | tf_op jit(solution)/shard_map/dot_general | solution.py:140
  128.1 9.3 %collective-permute-start.20 = (bf16[512,1024]{1,0:T(8,128)(2,1)}, bf16[512,1024]{1,0:T(8,128)(2,1)}, u32[]{:S(2)}, u32[]{:S(2)}) collective-permute-start(bf16[512,1024]{1,0:T(8,128)(2,1)} %convolution_convert_fusion.1), channel_id=1, source_target_pairs={{0,1},{1,0},{2,3},{3,2},{4,5},{5,4},{6,7},{7,6},{8,9},{9,8},{10,11... | collective-permute-start | bytes 3145736 | tf_op jit(solution)/shard_map/ppermute | solution.py:16
  138.3 4.9 %collective-permute-start.30 = (bf16[4,32,768]{2,1,0:T(8,128)(2,1)S(1)}, bf16[4,32,768]{2,1,0:T(8,128)(2,1)S(1)}, u32[]{:S(2)}, u32[]{:S(2)}) collective-permute-start(bf16[4,32,768]{2,1,0:T(8,128)(2,1)S(1)} %slice.212), channel_id=1, source_target_pairs={{32,0},{64,32},{96,64},{0,96},{33,1},{65,33},{97,65},{1,97},{34,2}... | collective-permute-start | bytes 589832 | tf_op jit(solution)/shard_map/ppermute | solution.py:12
  147.5 6.0 %collective-permute-done.32 = bf16[4,32,768]{2,1,0:T(8,128)(2,1)S(1)} collective-permute-done((bf16[4,32,768]{2,1,0:T(8,128)(2,1)S(1)}, bf16[4,32,768]{2,1,0:T(8,128)(2,1)S(1)}, u32[]{:S(2)}, u32[]{:S(2)}) %collective-permute-start.32) | collective-permute-done | bytes 196640 | tf_op jit(solution)/shard_map/ppermute | solution.py:12
  166.5 9.5 %collective-permute-start.22 = (bf16[160,1024]{1,0:T(8,128)(2,1)S(1)}, bf16[160,1024]{1,0:T(8,128)(2,1)S(1)}, u32[]{:S(2)}, u32[]{:S(2)}) collective-permute-start(bf16[160,1024]{1,0:T(8,128)(2,1)S(1)} %get-tuple-element.59), channel_id=1, source_target_pairs={{2,0},{4,2},{6,4},{8,6},{10,8},{12,10},{14,12},{16,14},{18,16},{20... | collective-permute-start | bytes 983048 | tf_op jit(solution)/shard_map/ppermute | solution.py:12
  193.2 6.0 %collective-permute-start.24 = (bf16[32,1024]{1,0:T(8,128)(2,1)S(1)}, bf16[32,1024]{1,0:T(8,128)(2,1)S(1)}, u32[]{:S(2)}, u32[]{:S(2)}) collective-permute-start(bf16[32,1024]{1,0:T(8,128)(2,1)S(1)} %pad_maximum_fusion.16), channel_id=1, source_target_pairs={{12,0},{14,2},{16,4},{18,6},{20,8},{22,10},{24,12},{26,14},{28,16}... | collective-permute-start | bytes 196616 | tf_op jit(solution)/shard_map/ppermute | solution.py:12
  199.2 5.0 %collective-permute-start.28 = (bf16[32,1024]{1,0:T(8,128)(2,1)S(1)}, bf16[32,1024]{1,0:T(8,128)(2,1)S(1)}, u32[]{:S(2)}, u32[]{:S(2)}) collective-permute-start(bf16[32,1024]{1,0:T(8,128)(2,1)S(1)} %pad_maximum_fusion.17), channel_id=1, source_target_pairs={{20,0},{22,2},{24,4},{26,6},{28,8},{30,10},{0,12},{2,14},{4,16},{6... | collective-permute-start | bytes 196616 | tf_op jit(solution)/shard_map/ppermute | solution.py:12
  215.0 4.6 %collective-permute-start.37 = (bf16[16,1024]{1,0:T(8,128)(2,1)S(1)}, bf16[16,1024]{1,0:T(8,128)(2,1)S(1)}, u32[]{:S(2)}, u32[]{:S(2)}) collective-permute-start(bf16[16,1024]{1,0:T(8,128)(2,1)S(1)} %get-tuple-element.52), channel_id=1, source_target_pairs={{4,0},{6,2},{8,4},{10,6},{12,8},{14,10},{16,12},{18,14},{20,16},{2... | collective-permute-start | bytes 98312 | tf_op jit(solution)/shard_map/ppermute | solution.py:12
  223.1 9.2 %collective-permute-start.38 = (bf16[32,1024]{1,0:T(8,128)(2,1)S(1)}, bf16[32,1024]{1,0:T(8,128)(2,1)S(1)}, u32[]{:S(2)}, u32[]{:S(2)}) collective-permute-start(bf16[32,1024]{1,0:T(8,128)(2,1)S(1)} %pad_maximum_fusion.18), channel_id=1, source_target_pairs={{12,0},{14,2},{16,4},{18,6},{20,8},{22,10},{24,12},{26,14},{28,16}... | collective-permute-start | bytes 196616 | tf_op jit(solution)/shard_map/ppermute | solution.py:12
  234.2 4.8 %collective-permute-start.39 = (bf16[32,1024]{1,0:T(8,128)(2,1)S(1)}, bf16[32,1024]{1,0:T(8,128)(2,1)S(1)}, u32[]{:S(2)}, u32[]{:S(2)}) collective-permute-start(bf16[32,1024]{1,0:T(8,128)(2,1)S(1)} %get-tuple-element.73), channel_id=1, source_target_pairs={{6,0},{8,2},{10,4},{12,6},{14,8},{16,10},{18,12},{20,14},{22,16},{... | collective-permute-start | bytes 196616 | tf_op jit(solution)/shard_map/ppermute | solution.py:12
  239.0 5.0 %collective-permute-start.40 = (bf16[32,1024]{1,0:T(8,128)(2,1)S(1)}, bf16[32,1024]{1,0:T(8,128)(2,1)S(1)}, u32[]{:S(2)}, u32[]{:S(2)}) collective-permute-start(bf16[32,1024]{1,0:T(8,128)(2,1)S(1)} %get-tuple-element.74), channel_id=1, source_target_pairs={{26,0},{28,2},{30,4},{0,6},{2,8},{4,10},{6,12},{8,14},{10,16},{12,... | collective-permute-start | bytes 196616 | tf_op jit(solution)/shard_map/ppermute | solution.py:12
  245.2 6.6 %collective-permute-done.40 = bf16[32,1024]{1,0:T(8,128)(2,1)S(1)} collective-permute-done((bf16[32,1024]{1,0:T(8,128)(2,1)S(1)}, bf16[32,1024]{1,0:T(8,128)(2,1)S(1)}, u32[]{:S(2)}, u32[]{:S(2)}) %collective-permute-start.40) | collective-permute-done | bytes 65568 | tf_op jit(solution)/shard_map/ppermute | solution.py:12
  253.0 6.0 %collective-permute-start.42 = (bf16[32,1024]{1,0:T(8,128)(2,1)S(1)}, bf16[32,1024]{1,0:T(8,128)(2,1)S(1)}, u32[]{:S(2)}, u32[]{:S(2)}) collective-permute-start(bf16[32,1024]{1,0:T(8,128)(2,1)S(1)} %reshape.91), channel_id=1, source_target_pairs={{20,0},{22,2},{24,4},{26,6},{28,8},{30,10},{0,12},{2,14},{4,16},{6... | collective-permute-start | bytes 196616 | tf_op jit(solution)/shard_map/ppermute | solution.py:12
  258.9 5.1 %collective-permute-start.43 = (bf16[32,1024]{1,0:T(8,128)(2,1)S(1)}, bf16[32,1024]{1,0:T(8,128)(2,1)S(1)}, u32[]{:S(2)}, u32[]{:S(2)}) collective-permute-start(bf16[32,1024]{1,0:T(8,128)(2,1)S(1)} %reshape.91), channel_id=1, source_target_pairs={{26,0},{28,2},{30,4},{0,6},{2,8},{4,10},{6,12},{8,14},{10,16},{12,... | collective-permute-start | bytes 196616 | tf_op jit(solution)/shard_map/ppermute | solution.py:12
  267.2 6.2 %collective-permute-start.45 = (bf16[32,1024]{1,0:T(8,128)(2,1)S(1)}, bf16[32,1024]{1,0:T(8,128)(2,1)S(1)}, u32[]{:S(2)}, u32[]{:S(2)}) collective-permute-start(bf16[32,1024]{1,0:T(8,128)(2,1)S(1)} %reshape.91), channel_id=1, source_target_pairs={{12,0},{14,2},{16,4},{18,6},{20,8},{22,10},{24,12},{26,14},{28,16}... | collective-permute-start | bytes 196616 | tf_op jit(solution)/shard_map/ppermute | solution.py:12
  273.6 5.4 %collective-permute-done.45 = bf16[32,1024]{1,0:T(8,128)(2,1)S(1)} collective-permute-done((bf16[32,1024]{1,0:T(8,128)(2,1)S(1)}, bf16[32,1024]{1,0:T(8,128)(2,1)S(1)}, u32[]{:S(2)}, u32[]{:S(2)}) %collective-permute-start.45) | collective-permute-done | bytes 65568 | tf_op jit(solution)/shard_map/ppermute | solution.py:12
  285.5 4.7 %collective-permute-start.48 = (bf16[16,1024]{1,0:T(8,128)(2,1)S(1)}, bf16[16,1024]{1,0:T(8,128)(2,1)S(1)}, u32[]{:S(2)}, u32[]{:S(2)}) collective-permute-start(bf16[16,1024]{1,0:T(8,128)(2,1)S(1)} %slice.218), channel_id=1, source_target_pairs={{4,0},{6,2},{8,4},{10,6},{12,8},{14,10},{16,12},{18,14},{20,16},{2... | collective-permute-start | bytes 98312 | tf_op jit(solution)/shard_map/ppermute | solution.py:12
  299.6 10.2 %collective-permute-start.50 = (bf16[512,1024]{1,0:T(8,128)(2,1)}, bf16[512,1024]{1,0:T(8,128)(2,1)S(1)}, u32[]{:S(2)}, u32[]{:S(2)}) collective-permute-start(bf16[512,1024]{1,0:T(8,128)(2,1)} %constant_dynamic-update-slice_fusion.5), channel_id=1, source_target_pairs={{0,1},{1,0},{2,3},{3,2},{4,5},{5,4},{6,7},{7,6},{8,9},{9,8},{10,11... | collective-permute-start | bytes 3145736 | tf_op jit(solution)/shard_map/ppermute | solution.py:16
  310.0 5.2 %collective-permute-start.51 = (bf16[32,1024]{1,0:T(8,128)(2,1)S(1)}, bf16[32,1024]{1,0:T(8,128)(2,1)S(1)}, u32[]{:S(2)}, u32[]{:S(2)}) collective-permute-start(bf16[32,1024]{1,0:T(8,128)(2,1)S(1)} %reshape.92), channel_id=1, source_target_pairs={{20,0},{22,2},{24,4},{26,6},{28,8},{30,10},{0,12},{2,14},{4,16},{6... | collective-permute-start | bytes 196616 | tf_op jit(solution)/shard_map/ppermute | solution.py:12
  318.9 4.6 %collective-permute-start.53 = (bf16[32,1024]{1,0:T(8,128)(2,1)S(1)}, bf16[32,1024]{1,0:T(8,128)(2,1)S(1)}, u32[]{:S(2)}, u32[]{:S(2)}) collective-permute-start(bf16[32,1024]{1,0:T(8,128)(2,1)S(1)} %reshape.92), channel_id=1, source_target_pairs={{6,0},{8,2},{10,4},{12,6},{14,8},{16,10},{18,12},{20,14},{22,16},{... | collective-permute-start | bytes 196616 | tf_op jit(solution)/shard_map/ppermute | solution.py:12
  323.5 7.0 %collective-permute-start.54 = (bf16[32,1024]{1,0:T(8,128)(2,1)S(1)}, bf16[32,1024]{1,0:T(8,128)(2,1)S(1)}, u32[]{:S(2)}, u32[]{:S(2)}) collective-permute-start(bf16[32,1024]{1,0:T(8,128)(2,1)S(1)} %reshape.92), channel_id=1, source_target_pairs={{12,0},{14,2},{16,4},{18,6},{20,8},{22,10},{24,12},{26,14},{28,16}... | collective-permute-start | bytes 196616 | tf_op jit(solution)/shard_map/ppermute | solution.py:12
  331.6 6.4 %collective-permute-done.54 = bf16[32,1024]{1,0:T(8,128)(2,1)S(1)} collective-permute-done((bf16[32,1024]{1,0:T(8,128)(2,1)S(1)}, bf16[32,1024]{1,0:T(8,128)(2,1)S(1)}, u32[]{:S(2)}, u32[]{:S(2)}) %collective-permute-start.54) | collective-permute-done | bytes 65568 | tf_op jit(solution)/shard_map/ppermute | solution.py:12
  345.1 6.1 %collective-permute-start.57 = (bf16[16,1024]{1,0:T(8,128)(2,1)}, bf16[16,1024]{1,0:T(8,128)(2,1)S(1)}, u32[]{:S(2)}, u32[]{:S(2)}) collective-permute-start(bf16[16,1024]{1,0:T(8,128)(2,1)} %get-tuple-element.70), channel_id=1, source_target_pairs={{4,0},{6,2},{8,4},{10,6},{12,8},{14,10},{16,12},{18,14},{20,16},{2... | collective-permute-start | bytes 98312 | tf_op jit(solution)/shard_map/ppermute | solution.py:12
  373.8 25.8 %all_to_all.10 = bf16[4,256,768]{2,1,0:T(8,128)(2,1)S(1)} all-to-all(bf16[4,256,768]{2,1,0:T(8,128)(2,1)S(1)} %bitcast.77), channel_id=1, replica_groups=mesh['y'=4,'x'=4,'z'=16,'c'=2] {'y'}, dimensions={0} | all-to-all | bytes 3145728 | tf_op jit(solution)/shard_map/all_to_all | solution.py:206
  405.7 6.1 %all-to-all-done.1 = bf16[4,64,768]{2,1,0:T(8,128)(2,1)S(1)} async-done(((bf16[4,64,768]{2,1,0:T(8,128)(2,1)}), bf16[4,64,768]{2,1,0:T(8,128)(2,1)S(1)}, u32[]{:S(2)}, u32[]{:S(2)}) %all-to-all-start.1) | async-done | bytes 393248 | tf_op jit(solution)/shard_map/all_to_all | solution.py:206
  411.8 37.5 %reduce-scatter.2.cloned.1.call-done = bf16[64,768]{1,0:T(8,128)(2,1)} async-done(((bf16[1024,768]{1,0:T(8,128)(2,1)}), bf16[64,768]{1,0:T(8,128)(2,1)}) %reduce-scatter.2.cloned.1.call-update) | async-done | bytes 98320 | tf_op jit(solution)/shard_map/reduce_scatter | solution.py:203
  (262 shorter events, 199.5 us)
Async XLA Ops:
  7.2 105.6 %all-gather.2.cloned.1.call-start = ((), (), s32[]{:S(2)}) async-start(), calls=%async_computation.3 | async-start | bytes 4595712 | tf_op jit(solution)/shard_map/all_gather | solution.py:114
  10.5 438.9 %reduce-scatter.2.cloned.1.call-start = ((), (), s32[]{:S(2)}) async-start(), calls=%async_computation.4 | async-start | bytes 1671168 | tf_op jit(solution)/shard_map/reduce_scatter | solution.py:203
  37.8 18.3 %collective-permute-start.10 = (bf16[4,64,1536]{2,1,0:T(8,128)(2,1)S(1)}, bf16[4,64,1536]{2,1,0:T(8,128)(2,1)S(1)}, u32[]{:S(2)}, u32[]{:S(2)}) collective-permute-start(bf16[4,64,1536]{2,1,0:T(8,128)(2,1)S(1)} %slice.196), channel_id=1, source_target_pairs={{32,0},{64,32},{96,64},{0,96},{33,1},{65,33},{97,65},{1,97},{34,2}... | collective-permute-start | bytes 2359304 | tf_op jit(solution)/shard_map/ppermute | solution.py:12
  42.4 18.8 %collective-permute-start.11 = (bf16[4,64,1536]{2,1,0:T(8,128)(2,1)S(1)}, bf16[4,64,1536]{2,1,0:T(8,128)(2,1)S(1)}, u32[]{:S(2)}, u32[]{:S(2)}) collective-permute-start(bf16[4,64,1536]{2,1,0:T(8,128)(2,1)S(1)} %slice.196), channel_id=1, source_target_pairs={{96,0},{0,32},{32,64},{64,96},{97,1},{1,33},{33,65},{65,97},{98,2}... | collective-permute-start | bytes 2359304 | tf_op jit(solution)/shard_map/ppermute | solution.py:12
  44.6 18.2 %collective-permute-start.4 = (bf16[4,64,1536]{2,1,0:T(8,128)(2,1)S(1)}, bf16[4,64,1536]{2,1,0:T(8,128)(2,1)S(1)}, u32[]{:S(2)}, u32[]{:S(2)}) collective-permute-start(bf16[4,64,1536]{2,1,0:T(8,128)(2,1)S(1)} %slice.192), channel_id=1, source_target_pairs={{128,0},{256,128},{384,256},{0,384},{129,1},{257,129},{385,257},{1... | collective-permute-start | bytes 2359304 | tf_op jit(solution)/shard_map/ppermute | solution.py:12
  49.2 18.7 %collective-permute-start.5 = (bf16[4,64,1536]{2,1,0:T(8,128)(2,1)S(1)}, bf16[4,64,1536]{2,1,0:T(8,128)(2,1)S(1)}, u32[]{:S(2)}, u32[]{:S(2)}) collective-permute-start(bf16[4,64,1536]{2,1,0:T(8,128)(2,1)S(1)} %slice.192), channel_id=1, source_target_pairs={{384,0},{0,128},{128,256},{256,384},{385,1},{1,129},{129,257},{257... | collective-permute-start | bytes 2359304 | tf_op jit(solution)/shard_map/ppermute | solution.py:12
  67.9 17.8 %collective-permute-start.16 = (bf16[4,64,768]{2,1,0:T(8,128)(2,1)}, bf16[4,64,768]{2,1,0:T(8,128)(2,1)}, u32[]{:S(2)}, u32[]{:S(2)}) collective-permute-start(bf16[4,64,768]{2,1,0:T(8,128)(2,1)} %pad_maximum_fusion.14), channel_id=1, source_target_pairs={{128,0},{256,128},{384,256},{0,384},{129,1},{257,129},{385,257},{1... | collective-permute-start | bytes 1179656 | tf_op jit(solution)/shard_map/ppermute | solution.py:12
  69.8 19.0 %collective-permute-start.18 = (bf16[4,64,768]{2,1,0:T(8,128)(2,1)}, bf16[4,64,768]{2,1,0:T(8,128)(2,1)}, u32[]{:S(2)}, u32[]{:S(2)}) collective-permute-start(bf16[4,64,768]{2,1,0:T(8,128)(2,1)} %pad_maximum_fusion.14), channel_id=1, source_target_pairs={{384,0},{0,128},{128,256},{256,384},{385,1},{1,129},{129,257},{257... | collective-permute-start | bytes 1179656 | tf_op jit(solution)/shard_map/ppermute | solution.py:12
  74.0 20.4 %collective-permute-start.14 = (bf16[4,32,1536]{2,1,0:T(8,128)(2,1)}, bf16[4,32,1536]{2,1,0:T(8,128)(2,1)}, u32[]{:S(2)}, u32[]{:S(2)}) collective-permute-start(bf16[4,32,1536]{2,1,0:T(8,128)(2,1)} %slice.159), channel_id=1, source_target_pairs={{32,0},{64,32},{96,64},{0,96},{33,1},{65,33},{97,65},{1,97},{34,2}... | collective-permute-start | bytes 1179656 | tf_op jit(solution)/shard_map/ppermute | solution.py:12
  79.1 17.2 %collective-permute-start.15 = (bf16[4,32,1536]{2,1,0:T(8,128)(2,1)}, bf16[4,32,1536]{2,1,0:T(8,128)(2,1)}, u32[]{:S(2)}, u32[]{:S(2)}) collective-permute-start(bf16[4,32,1536]{2,1,0:T(8,128)(2,1)} %slice.160), channel_id=1, source_target_pairs={{96,0},{0,32},{32,64},{64,96},{97,1},{1,33},{33,65},{65,97},{98,2}... | collective-permute-start | bytes 1179656 | tf_op jit(solution)/shard_map/ppermute | solution.py:12
  81.8 20.1 %collective-permute-start.12 = (bf16[4,32,1536]{2,1,0:T(8,128)(2,1)}, bf16[4,32,1536]{2,1,0:T(8,128)(2,1)}, u32[]{:S(2)}, u32[]{:S(2)}) collective-permute-start(bf16[4,32,1536]{2,1,0:T(8,128)(2,1)} %slice.157), channel_id=1, source_target_pairs={{128,0},{256,128},{384,256},{0,384},{129,1},{257,129},{385,257},{1... | collective-permute-start | bytes 1179656 | tf_op jit(solution)/shard_map/ppermute | solution.py:12
  85.7 18.3 %collective-permute-start.13 = (bf16[4,32,1536]{2,1,0:T(8,128)(2,1)}, bf16[4,32,1536]{2,1,0:T(8,128)(2,1)}, u32[]{:S(2)}, u32[]{:S(2)}) collective-permute-start(bf16[4,32,1536]{2,1,0:T(8,128)(2,1)} %slice.158), channel_id=1, source_target_pairs={{384,0},{0,128},{128,256},{256,384},{385,1},{1,129},{129,257},{257... | collective-permute-start | bytes 1179656 | tf_op jit(solution)/shard_map/ppermute | solution.py:12
  88.9 48.5 %collective-permute-start.29 = (bf16[4,64,768]{2,1,0:T(8,128)(2,1)S(1)}, bf16[4,64,768]{2,1,0:T(8,128)(2,1)}, u32[]{:S(2)}, u32[]{:S(2)}) collective-permute-start(bf16[4,64,768]{2,1,0:T(8,128)(2,1)S(1)} %pad_maximum_fusion.13), channel_id=1, source_target_pairs={{32,0},{64,32},{96,64},{0,96},{33,1},{65,33},{97,65},{1,97},{34,2}... | collective-permute-start | bytes 1179656 | tf_op jit(solution)/shard_map/ppermute | solution.py:12
  94.4 48.7 %collective-permute-start.31 = (bf16[4,64,768]{2,1,0:T(8,128)(2,1)S(1)}, bf16[4,64,768]{2,1,0:T(8,128)(2,1)}, u32[]{:S(2)}, u32[]{:S(2)}) collective-permute-start(bf16[4,64,768]{2,1,0:T(8,128)(2,1)S(1)} %pad_maximum_fusion.13), channel_id=1, source_target_pairs={{96,0},{0,32},{32,64},{64,96},{97,1},{1,33},{33,65},{65,97},{98,2}... | collective-permute-start | bytes 1179656 | tf_op jit(solution)/shard_map/ppermute | solution.py:12
  128.1 31.9 %collective-permute-start.20 = (bf16[512,1024]{1,0:T(8,128)(2,1)}, bf16[512,1024]{1,0:T(8,128)(2,1)}, u32[]{:S(2)}, u32[]{:S(2)}) collective-permute-start(bf16[512,1024]{1,0:T(8,128)(2,1)} %convolution_convert_fusion.1), channel_id=1, source_target_pairs={{0,1},{1,0},{2,3},{3,2},{4,5},{5,4},{6,7},{7,6},{8,9},{9,8},{10,11... | collective-permute-start | bytes 3145736 | tf_op jit(solution)/shard_map/ppermute | solution.py:16
  156.8 25.4 %collective-permute-start.33 = (bf16[512,1024]{1,0:T(8,128)(2,1)}, bf16[512,1024]{1,0:T(8,128)(2,1)}, u32[]{:S(2)}, u32[]{:S(2)}) collective-permute-start(bf16[512,1024]{1,0:T(8,128)(2,1)} %convolution_convert_fusion), channel_id=1, source_target_pairs={{0,1},{1,0},{2,3},{3,2},{4,5},{5,4},{6,7},{7,6},{8,9},{9,8},{10,11... | collective-permute-start | bytes 3145736 | tf_op jit(solution)/shard_map/ppermute | solution.py:16
  162.9 21.6 %collective-permute-start.21 = (bf16[160,1024]{1,0:T(8,128)(2,1)S(1)}, bf16[160,1024]{1,0:T(8,128)(2,1)S(1)}, u32[]{:S(2)}, u32[]{:S(2)}) collective-permute-start(bf16[160,1024]{1,0:T(8,128)(2,1)S(1)} %get-tuple-element.60), channel_id=1, source_target_pairs={{30,0},{0,2},{2,4},{4,6},{6,8},{8,10},{10,12},{12,14},{14,16},{16,... | collective-permute-start | bytes 983048 | tf_op jit(solution)/shard_map/ppermute | solution.py:12
  166.5 18.0 %collective-permute-start.22 = (bf16[160,1024]{1,0:T(8,128)(2,1)S(1)}, bf16[160,1024]{1,0:T(8,128)(2,1)S(1)}, u32[]{:S(2)}, u32[]{:S(2)}) collective-permute-start(bf16[160,1024]{1,0:T(8,128)(2,1)S(1)} %get-tuple-element.59), channel_id=1, source_target_pairs={{2,0},{4,2},{6,4},{8,6},{10,8},{12,10},{14,12},{16,14},{18,16},{20... | collective-permute-start | bytes 983048 | tf_op jit(solution)/shard_map/ppermute | solution.py:12
  186.6 34.6 %collective-permute-start.34 = (bf16[160,1024]{1,0:T(8,128)(2,1)S(1)}, bf16[160,1024]{1,0:T(8,128)(2,1)S(1)}, u32[]{:S(2)}, u32[]{:S(2)}) collective-permute-start(bf16[160,1024]{1,0:T(8,128)(2,1)S(1)} %get-tuple-element.55), channel_id=1, source_target_pairs={{30,0},{0,2},{2,4},{4,6},{6,8},{8,10},{10,12},{12,14},{14,16},{16,... | collective-permute-start | bytes 983048 | tf_op jit(solution)/shard_map/ppermute | solution.py:12
  189.3 32.0 %collective-permute-start.35 = (bf16[160,1024]{1,0:T(8,128)(2,1)S(1)}, bf16[160,1024]{1,0:T(8,128)(2,1)}, u32[]{:S(2)}, u32[]{:S(2)}) collective-permute-start(bf16[160,1024]{1,0:T(8,128)(2,1)S(1)} %get-tuple-element.54), channel_id=1, source_target_pairs={{2,0},{4,2},{6,4},{8,6},{10,8},{12,10},{14,12},{16,14},{18,16},{20... | collective-permute-start | bytes 983048 | tf_op jit(solution)/shard_map/ppermute | solution.py:12
  193.2 14.7 %collective-permute-start.24 = (bf16[32,1024]{1,0:T(8,128)(2,1)S(1)}, bf16[32,1024]{1,0:T(8,128)(2,1)S(1)}, u32[]{:S(2)}, u32[]{:S(2)}) collective-permute-start(bf16[32,1024]{1,0:T(8,128)(2,1)S(1)} %pad_maximum_fusion.16), channel_id=1, source_target_pairs={{12,0},{14,2},{16,4},{18,6},{20,8},{22,10},{24,12},{26,14},{28,16}... | collective-permute-start | bytes 196616 | tf_op jit(solution)/shard_map/ppermute | solution.py:12
  223.1 21.0 %collective-permute-start.38 = (bf16[32,1024]{1,0:T(8,128)(2,1)S(1)}, bf16[32,1024]{1,0:T(8,128)(2,1)S(1)}, u32[]{:S(2)}, u32[]{:S(2)}) collective-permute-start(bf16[32,1024]{1,0:T(8,128)(2,1)S(1)} %pad_maximum_fusion.18), channel_id=1, source_target_pairs={{12,0},{14,2},{16,4},{18,6},{20,8},{22,10},{24,12},{26,14},{28,16}... | collective-permute-start | bytes 196616 | tf_op jit(solution)/shard_map/ppermute | solution.py:12
  253.0 20.5 %collective-permute-start.42 = (bf16[32,1024]{1,0:T(8,128)(2,1)S(1)}, bf16[32,1024]{1,0:T(8,128)(2,1)S(1)}, u32[]{:S(2)}, u32[]{:S(2)}) collective-permute-start(bf16[32,1024]{1,0:T(8,128)(2,1)S(1)} %reshape.91), channel_id=1, source_target_pairs={{20,0},{22,2},{24,4},{26,6},{28,8},{30,10},{0,12},{2,14},{4,16},{6... | collective-permute-start | bytes 196616 | tf_op jit(solution)/shard_map/ppermute | solution.py:12
  258.9 14.6 %collective-permute-start.43 = (bf16[32,1024]{1,0:T(8,128)(2,1)S(1)}, bf16[32,1024]{1,0:T(8,128)(2,1)S(1)}, u32[]{:S(2)}, u32[]{:S(2)}) collective-permute-start(bf16[32,1024]{1,0:T(8,128)(2,1)S(1)} %reshape.91), channel_id=1, source_target_pairs={{26,0},{28,2},{30,4},{0,6},{2,8},{4,10},{6,12},{8,14},{10,16},{12,... | collective-permute-start | bytes 196616 | tf_op jit(solution)/shard_map/ppermute | solution.py:12
  279.0 14.8 %collective-permute-start.46 = (bf16[160,1024]{1,0:T(8,128)(2,1)S(1)}, bf16[160,1024]{1,0:T(8,128)(2,1)S(1)}, u32[]{:S(2)}, u32[]{:S(2)}) collective-permute-start(bf16[160,1024]{1,0:T(8,128)(2,1)S(1)} %constant_dynamic-update-slice_fusion), channel_id=1, source_target_pairs={{30,0},{0,2},{2,4},{4,6},{6,8},{8,10},{10,12},{12,14},{14,16},{16,... | collective-permute-start | bytes 983048 | tf_op jit(solution)/shard_map/ppermute | solution.py:12
  280.9 16.8 %collective-permute-start.47 = (bf16[160,1024]{1,0:T(8,128)(2,1)S(1)}, bf16[160,1024]{1,0:T(8,128)(2,1)S(1)}, u32[]{:S(2)}, u32[]{:S(2)}) collective-permute-start(bf16[160,1024]{1,0:T(8,128)(2,1)S(1)} %constant_dynamic-update-slice_fusion), channel_id=1, source_target_pairs={{2,0},{4,2},{6,4},{8,6},{10,8},{12,10},{14,12},{16,14},{18,16},{20... | collective-permute-start | bytes 983048 | tf_op jit(solution)/shard_map/ppermute | solution.py:12
  299.6 54.3 %collective-permute-start.50 = (bf16[512,1024]{1,0:T(8,128)(2,1)}, bf16[512,1024]{1,0:T(8,128)(2,1)S(1)}, u32[]{:S(2)}, u32[]{:S(2)}) collective-permute-start(bf16[512,1024]{1,0:T(8,128)(2,1)} %constant_dynamic-update-slice_fusion.5), channel_id=1, source_target_pairs={{0,1},{1,0},{2,3},{3,2},{4,5},{5,4},{6,7},{7,6},{8,9},{9,8},{10,11... | collective-permute-start | bytes 3145736 | tf_op jit(solution)/shard_map/ppermute | solution.py:16
  310.0 20.5 %collective-permute-start.51 = (bf16[32,1024]{1,0:T(8,128)(2,1)S(1)}, bf16[32,1024]{1,0:T(8,128)(2,1)S(1)}, u32[]{:S(2)}, u32[]{:S(2)}) collective-permute-start(bf16[32,1024]{1,0:T(8,128)(2,1)S(1)} %reshape.92), channel_id=1, source_target_pairs={{20,0},{22,2},{24,4},{26,6},{28,8},{30,10},{0,12},{2,14},{4,16},{6... | collective-permute-start | bytes 196616 | tf_op jit(solution)/shard_map/ppermute | solution.py:12
  315.2 16.4 %collective-permute-start.52 = (bf16[32,1024]{1,0:T(8,128)(2,1)S(1)}, bf16[32,1024]{1,0:T(8,128)(2,1)S(1)}, u32[]{:S(2)}, u32[]{:S(2)}) collective-permute-start(bf16[32,1024]{1,0:T(8,128)(2,1)S(1)} %reshape.92), channel_id=1, source_target_pairs={{26,0},{28,2},{30,4},{0,6},{2,8},{4,10},{6,12},{8,14},{10,16},{12,... | collective-permute-start | bytes 196616 | tf_op jit(solution)/shard_map/ppermute | solution.py:12
  323.5 14.5 %collective-permute-start.54 = (bf16[32,1024]{1,0:T(8,128)(2,1)S(1)}, bf16[32,1024]{1,0:T(8,128)(2,1)S(1)}, u32[]{:S(2)}, u32[]{:S(2)}) collective-permute-start(bf16[32,1024]{1,0:T(8,128)(2,1)S(1)} %reshape.92), channel_id=1, source_target_pairs={{12,0},{14,2},{16,4},{18,6},{20,8},{22,10},{24,12},{26,14},{28,16}... | collective-permute-start | bytes 196616 | tf_op jit(solution)/shard_map/ppermute | solution.py:12
  338.0 20.4 %collective-permute-start.55 = (bf16[160,1024]{1,0:T(8,128)(2,1)S(1)}, bf16[160,1024]{1,0:T(8,128)(2,1)}, u32[]{:S(2)}, u32[]{:S(2)}) collective-permute-start(bf16[160,1024]{1,0:T(8,128)(2,1)S(1)} %constant_dynamic-update-slice_fusion.14), channel_id=1, source_target_pairs={{30,0},{0,2},{2,4},{4,6},{6,8},{8,10},{10,12},{12,14},{14,16},{16,... | collective-permute-start | bytes 983048 | tf_op jit(solution)/shard_map/ppermute | solution.py:12
  342.0 16.4 %collective-permute-start.56 = (bf16[160,1024]{1,0:T(8,128)(2,1)S(1)}, bf16[160,1024]{1,0:T(8,128)(2,1)}, u32[]{:S(2)}, u32[]{:S(2)}) collective-permute-start(bf16[160,1024]{1,0:T(8,128)(2,1)S(1)} %constant_dynamic-update-slice_fusion.14), channel_id=1, source_target_pairs={{2,0},{4,2},{6,4},{8,6},{10,8},{12,10},{14,12},{16,14},{18,16},{20... | collective-permute-start | bytes 983048 | tf_op jit(solution)/shard_map/ppermute | solution.py:12
  (52 other events, 568.4 us)
Sparse Core Ops, SparseCore 0:
  10.7 80.2 all-gather.1
  368.2 81.1 reduce-scatter.1

commit v3 on v1

--- a/solution.py
+++ b/solution.py
@@ -9,6 +9,13 @@
 
 def fetch(value, axis, shift, size):
     return lax.ppermute(value, axis, [((i + shift) % size, i) for i in range(size)])
+
+
+Z = ("zh", "zl")
+
+
+def swap_cores(value):
+    return lax.ppermute(value, "c", [(0, 1), (1, 0)])
 
 
 def ring4(value, axis):
@@ -33,6 +40,26 @@
     return jnp.concatenate([first.reshape(rows, -1), second.reshape(rows, -1)], 1)
 
 
+def reduce_near(parts):
+    own, ahead, across, behind = jnp.split(parts, 4)
+    half = across.shape[0] // 2
+    low = fetch(across[:half], Z, -2, 16)
+    high = fetch(across[half:], Z, 2, 16)
+    ahead = fetch(ahead, Z, -1, 16)
+    behind = fetch(behind, Z, 1, 16)
+    across = jnp.concatenate([low, high])
+    return sum(p.astype(F32) for p in (own, ahead, behind, across)).astype(BF)
+
+
+def spread_near(own):
+    half = own.shape[0] // 2
+    low = fetch(own[:half], Z, 2, 16)
+    high = fetch(own[half:], Z, -2, 16)
+    ahead = fetch(own, Z, 1, 16)
+    behind = fetch(own, Z, -1, 16)
+    return jnp.concatenate([own, ahead, low, high, behind])
+
+
 def to_absolute(value, y, x):
     rows, width = value.shape
     first, second = jnp.split(value, 2, axis=1)
@@ -45,10 +72,10 @@
 def local(tokens, routes, gates, curvature, w_gate, w_up, direction):
     rows, width = tokens.shape
     hidden_width = w_gate.shape[2]
-    z_count, cores = lax.axis_size("z"), lax.axis_size("c")
-    experts = z_count * cores
+    z_far, z_near, cores = (lax.axis_size(name) for name in ("zh", "zl", "c"))
+    experts = z_far * z_near * cores
     y, x, core = lax.axis_index("y"), lax.axis_index("x"), lax.axis_index("c")
-    me = lax.axis_index(("z", "c"))
+    me = lax.axis_index(("zh", "zl", "c"))
 
     chosen = routes[:, :, None] == jnp.arange(experts, dtype=jnp.int32)
     table = jnp.sum(jnp.where(chosen, gates[:, :, None], 0.0), axis=1)
@@ -63,7 +90,7 @@
         ],
         1,
     )
-    arrived = lax.all_gather(sent, ("z", "c"), axis=0, tiled=True)
+    arrived = lax.all_gather(sent, ("zh", "zl", "c"), axis=0, tiled=True)
 
     stacked = jnp.concatenate([w_gate[0], w_up[0], direction[0]], 1)
     half = stacked.shape[0] // 2
@@ -85,9 +112,17 @@
     )
     hidden = (jax.nn.silu(gate_pre) * up_pre * share).astype(BF)
 
-    by_core = hidden.reshape(z_count, cores, rows, hidden_width)
-    away = lax.dynamic_index_in_dim(by_core, 1 - core, 1, False).reshape(-1, hidden_width)
-    home = lax.dynamic_index_in_dim(by_core, core, 1, False).reshape(-1, hidden_width)
+    near = lax.axis_index("zl")
+    by_core = hidden.reshape(z_far, z_near, cores, rows, hidden_width)
+    by_core = jnp.concatenate([by_core, by_core], 1)
+
+    def of_core(which):
+        turned = lax.dynamic_slice(
+            by_core, (0, near, which, 0, 0), (z_far, z_near, 1, rows, hidden_width)
+        )
+        return turned[:, :, 0].swapaxes(0, 1).reshape(-1, hidden_width)
+
+    home, away = of_core(core), of_core(1 - core)
 
     def tangent(part):
         return lax.dot_general(
@@ -97,15 +132,20 @@
             preferred_element_type=F32,
         )
 
-    other = lax.ppermute(tangent(away).astype(BF), "c", [(0, 1), (1, 0)])
+    other = swap_cores(tangent(away).astype(BF))
     paired = (tangent(home) + other.astype(F32)).astype(BF)
-    jv = lax.psum_scatter(paired, "z", scatter_dimension=0, tiled=True)
+    jv = lax.psum_scatter(reduce_near(paired), "zh", scatter_dimension=0, tiled=True)
     output_tangent = to_absolute(jv, y, x)
     curved = (curvature[:, None] * output_tangent.astype(F32)).astype(BF)
-    spread = lax.all_gather(curved, ("z", "c"), axis=0, tiled=True)
-    part = lax.dot_general(
-        spread, hidden, (((0,), (0,)), ((), ())), preferred_element_type=F32
-    ).astype(BF)
+    spread = spread_near(lax.all_gather(curved, "zh", axis=0, tiled=True))
+    spread_away = swap_cores(spread)
+
+    def outer(left, right):
+        return lax.dot_general(
+            left, right, (((0,), (0,)), ((), ())), preferred_element_type=F32
+        )
+
+    part = (outer(spread, home) + outer(spread_away, away)).astype(BF)
 
     def add_over(value, axis):
         value = value.reshape(4, -1, hidden_width)
@@ -117,13 +157,13 @@
 
 
 def solution(mesh):
-    torus = Mesh(mesh.devices.reshape(4, 4, 16, 2), ("y", "x", "z", "c"))
-    tokens = P(("y", "x", "z", "c"), None)
-    matrix = P(("z", "c"), ("y", "x"), None)
+    torus = Mesh(mesh.devices.reshape(4, 4, 4, 4, 2), ("y", "x", "zh", "zl", "c"))
+    tokens = P(("y", "x", "zh", "zl", "c"), None)
+    matrix = P(("zh", "zl", "c"), ("y", "x"), None)
     return jax.shard_map(
         local,
         mesh=torus,
-        in_specs=(tokens, tokens, tokens, P(("y", "x", "z", "c")), matrix, matrix, matrix),
+        in_specs=(tokens, tokens, tokens, P(("y", "x", "zh", "zl", "c")), matrix, matrix, matrix),
         out_specs=(tokens, matrix),
         check_vma=False,
     )

time: 354 us -> 348 us (0.983)
  waiting for transfers between devices: 174 us -> 104 us
  starting transfers between devices: 59 us -> 101 us
  blocking collectives: 55.8 us -> 78.7 us
    all_gather x2 -> x1, waiting for transfers between devices: 82.8 us -> 0.01 us  [local(): arrived = lax.all_gather(sent, ('zh', 'zl', 'c'), axis=0, tiled=True)]
    ppermute x16 -> x24, starting transfers between devices: 49.2 us -> 84.5 us  [fetch(): lax.ppermute(value, axis, [((i + shift) % size, i) for i in range(size)])]
    ppermute x16 -> x24, waiting for transfers between devices: 22.2 us -> 54.7 us  [fetch(): lax.ppermute(value, axis, [((i + shift) % size, i) for i in range(size)])]
    reduce_scatter x1, waiting for transfers between devices: 65.6 us -> 41.5 us  [local(): lax.psum_scatter(reduce_near(paired), 'zh', scatter_dimension=0, tiled=True)]
    all_gather x0 -> x1, blocking collectives: none -> 23.6 us  [local(): spread = spread_near(lax.all_gather(curved, 'zh', axis=0, tiled=True))]
    ppermute x1 -> x2, starting transfers between devices: 9.5 us -> 16.8 us  [swap_cores(): return lax.ppermute(value, 'c', [(0, 1), (1, 0)])]
    ppermute x1 -> x2, waiting for transfers between devices: 3.76 us -> 7.46 us  [swap_cores(): return lax.ppermute(value, 'c', [(0, 1), (1, 0)])]
  transfers between devices with their start and end apart: 20 -> 28, of which waited for: 7 -> 12; matrix products, arithmetic and copies ran while one was open for 4% -> 4% of each run, Pallas kernels for 0% -> 0%
where the time goes in v3:
time: 348 us; the launch traced here: 346 us
  waiting for transfers between devices  104 us (30%)
  starting transfers between devices  101 us (29%)
  blocking collectives  78.7 us (23%)
  matrix products  18.4 us (5%)
  other arithmetic  16 us (5%)
  between operations  14.9 us (4%)
  local copies, waits for them, and re-layouts  12.3 us (4%)
    ppermute x24, starting transfers between devices, fetch(): lax.ppermute(value, axis, [((i + shift) % size, i) for i in range(size)])  84.5 us
    all_to_all x2, blocking collectives, add_over(): moved = lax.all_to_all(value, axis, 0, 0, tiled=True)  55.2 us
    ppermute x24, waiting for transfers between devices, fetch(): lax.ppermute(value, axis, [((i + shift) % size, i) for i in range(size)])  54.7 us
    reduce_scatter x1, waiting for transfers between devices, local(): lax.psum_scatter(reduce_near(paired), 'zh', scatter_dimension=0, tiled=True)  41.5 us
    all_gather x1, blocking collectives, local(): spread = spread_near(lax.all_gather(curved, 'zh', axis=0, tiled=True))  23.6 us
    ppermute x2, starting transfers between devices, swap_cores(): return lax.ppermute(value, 'c', [(0, 1), (1, 0)])  16.8 us
    another operation x8, other arithmetic, ring4(): return jnp.stack([value, after, jnp.concatenate([low, high], -2), before])  7.99 us
    ppermute x2, waiting for transfers between devices, swap_cores(): return lax.ppermute(value, 'c', [(0, 1), (1, 0)])  7.46 us
  transfers between devices with their start and end apart: 28, of which 12 were waited for; matrix products, arithmetic and copies ran while one was open for 4% of the time, Pallas kernels for 0%

profile of v3, /device:TPU:1, one launch (start us, length us, event | category | flops | bytes accessed | tf_op | source)
XLA Modules:
  0.0 345.5 jit_solution(12950448912951245103)
XLA Ops:
  13.0 4.0 %collective-permute-start.10 = (bf16[64,2304]{1,0:T(8,128)(2,1)S(1)}, bf16[64,2304]{1,0:T(8,128)(2,1)S(1)}, u32[]{:S(2)}, u32[]{:S(2)}) collective-permute-start(bf16[64,2304]{1,0:T(8,128)(2,1)S(1)} %get-tuple-element.16), channel_id=1, source_target_pairs={{384,0},{0,128},{128,256},{256,384},{385,1},{1,129},{129,257},{257... | collective-permute-start | bytes 884744 | tf_op jit(solution)/shard_map/ppermute | solution.py:11
  17.0 3.4 collective-permute-start.8
  20.4 4.4 %collective-permute-start = (bf16[64,2304]{1,0:T(8,128)(2,1)S(1)}, bf16[64,2304]{1,0:T(8,128)(2,1)S(1)}, u32[]{:S(2)}, u32[]{:S(2)}) collective-permute-start(bf16[64,2304]{1,0:T(8,128)(2,1)S(1)} %get-tuple-element.17), channel_id=1, source_target_pairs={{32,0},{64,32},{96,64},{0,96},{33,1},{65,33},{97,65},{1,97},{34,2}... | collective-permute-start | bytes 884744 | tf_op jit(solution)/shard_map/ppermute | solution.py:11
  28.7 4.6 %collective-permute-start.9 = (bf16[32,2304]{1,0:T(8,128)(2,1)S(1)}, bf16[32,2304]{1,0:T(8,128)(2,1)S(1)}, u32[]{:S(2)}, u32[]{:S(2)}) collective-permute-start(bf16[32,2304]{1,0:T(8,128)(2,1)S(1)} %slice.86), channel_id=1, source_target_pairs={{128,0},{256,128},{384,256},{0,384},{129,1},{257,129},{385,257},{1... | collective-permute-start | bytes 442376 | tf_op jit(solution)/shard_map/ppermute | solution.py:11
  33.3 4.6 %collective-permute-start.1 = (bf16[32,2304]{1,0:T(8,128)(2,1)S(1)}, bf16[32,2304]{1,0:T(8,128)(2,1)S(1)}, u32[]{:S(2)}, u32[]{:S(2)}) collective-permute-start(bf16[32,2304]{1,0:T(8,128)(2,1)S(1)} %slice.81), channel_id=1, source_target_pairs={{32,0},{64,32},{96,64},{0,96},{33,1},{65,33},{97,65},{1,97},{34,2}... | collective-permute-start | bytes 442376 | tf_op jit(solution)/shard_map/ppermute | solution.py:11
  40.1 4.6 %collective-permute-start.12 = (bf16[4,64,2304]{2,1,0:T(8,128)(2,1)S(1)}, bf16[4,64,2304]{2,1,0:T(8,128)(2,1)S(1)}, u32[]{:S(2)}, u32[]{:S(2)}) collective-permute-start(bf16[4,64,2304]{2,1,0:T(8,128)(2,1)S(1)} %get-tuple-element.11), channel_id=1, source_target_pairs={{32,0},{64,32},{96,64},{0,96},{33,1},{65,33},{97,65},{1,97},{34,2}... | collective-permute-start | bytes 3538952 | tf_op jit(solution)/shard_map/ppermute | solution.py:11
  49.0 3.1 collective-permute-start.6
  52.2 14.6 %collective-permute-done.12 = bf16[4,64,2304]{2,1,0:T(8,128)(2,1)S(1)} collective-permute-done((bf16[4,64,2304]{2,1,0:T(8,128)(2,1)S(1)}, bf16[4,64,2304]{2,1,0:T(8,128)(2,1)S(1)}, u32[]{:S(2)}, u32[]{:S(2)}) %collective-permute-start.12) | collective-permute-done | bytes 1179680 | tf_op jit(solution)/shard_map/ppermute | solution.py:11
  67.6 3.4 collective-permute-start.13
  80.9 3.1 collective-permute-start.7
  88.0 5.1 %collective-permute-done.7 = bf16[4,32,2304]{2,1,0:T(8,128)(2,1)} collective-permute-done((bf16[4,32,2304]{2,1,0:T(8,128)(2,1)}, bf16[4,32,2304]{2,1,0:T(8,128)(2,1)}, u32[]{:S(2)}, u32[]{:S(2)}) %collective-permute-start.7) | collective-permute-done | bytes 589856 | tf_op jit(solution)/shard_map/ppermute | solution.py:11
  100.7 7.1 %fusion.2 = f32[1024,768]{1,0:T(8,128)S(1)} fusion(bf16[1024,2176]{1,0:T(8,128)(2,1)} %all-gather.2.cloned.1.call-done, bf16[1024,2304]{1,0:T(8,128)(2,1)} %bitcast.58, bf16[1024,2304]{1,0:T(8,128)(2,1)} %bitcast.52), kind=kOutput, calls=%fused_computation.10 | convolution fusion | flops 3227516928 | bytes 16777216 | tf_op jit(solution)/shard_map/dot_general | solution.py:109
  107.9 3.7 %multiply_convert_fusion = bf16[1024,768]{1,0:T(8,128)(2,1)S(1)} fusion(f32[1024,768]{1,0:T(8,128)S(1)} %fusion.2, f32[1024]{0:T(1024)S(1)} %select_reduce_fusion, bf16[1024,2304]{1,0:T(8,128)(2,1)S(1)} %bitcast.61, bf16[1024,2304]{1,0:T(8,128)(2,1)S(1)} %bitcast.55, bf16[1024,2176]{1,0:T(8,128)(2,1)S(1)} %bitcast.85), kind=kOutput, calls=%fused_computation.19 | convolution fusion | flops 3233021952 | bytes 18354176 | tf_op jit(solution)/shard_map/dot_general | solution.py:110
  114.1 9.5 %collective-permute-start.16 = (bf16[512,2048]{1,0:T(8,128)(2,1)S(1)}, bf16[512,2048]{1,0:T(8,128)(2,1)S(1)}, u32[]{:S(2)}, u32[]{:S(2)}) collective-permute-start(bf16[512,2048]{1,0:T(8,128)(2,1)S(1)} %convolution_convert_fusion), channel_id=1, source_target_pairs={{0,1},{1,0},{2,3},{3,2},{4,5},{5,4},{6,7},{7,6},{8,9},{9,8},{10,11... | collective-permute-start | bytes 6291464 | tf_op jit(solution)/shard_map/ppermute | solution.py:18
  123.7 3.7 %collective-permute-done.16 = bf16[512,2048]{1,0:T(8,128)(2,1)S(1)} collective-permute-done((bf16[512,2048]{1,0:T(8,128)(2,1)S(1)}, bf16[512,2048]{1,0:T(8,128)(2,1)S(1)}, u32[]{:S(2)}, u32[]{:S(2)}) %collective-permute-start.16) | collective-permute-done | bytes 2097184 | tf_op jit(solution)/shard_map/ppermute | solution.py:18
  129.4 5.0 %collective-permute-start.17 = (bf16[128,2048]{1,0:T(8,128)(2,1)S(1)}, bf16[128,2048]{1,0:T(8,128)(2,1)S(1)}, u32[]{:S(2)}, u32[]{:S(2)}) collective-permute-start(bf16[128,2048]{1,0:T(8,128)(2,1)S(1)} %get-tuple-element.6), channel_id=1, source_target_pairs={{30,0},{0,2},{2,4},{4,6},{6,8},{8,10},{10,12},{12,14},{14,16},{16,... | collective-permute-start | bytes 1572872 | tf_op jit(solution)/shard_map/ppermute | solution.py:11
  134.4 9.5 %collective-permute-start.18 = (bf16[128,2048]{1,0:T(8,128)(2,1)S(1)}, bf16[128,2048]{1,0:T(8,128)(2,1)S(1)}, u32[]{:S(2)}, u32[]{:S(2)}) collective-permute-start(bf16[128,2048]{1,0:T(8,128)(2,1)S(1)} %get-tuple-element.7), channel_id=1, source_target_pairs={{2,0},{4,2},{6,4},{8,6},{10,8},{12,10},{14,12},{16,14},{18,16},{20... | collective-permute-start | bytes 1572872 | tf_op jit(solution)/shard_map/ppermute | solution.py:11
  145.9 5.7 %collective-permute-start.20 = (bf16[64,2048]{1,0:T(8,128)(2,1)S(1)}, bf16[64,2048]{1,0:T(8,128)(2,1)S(1)}, u32[]{:S(2)}, u32[]{:S(2)}) collective-permute-start(bf16[64,2048]{1,0:T(8,128)(2,1)S(1)} %get-tuple-element.5), channel_id=1, source_target_pairs={{4,0},{6,2},{8,4},{10,6},{12,8},{14,10},{16,12},{18,14},{20,16},{2... | collective-permute-start | bytes 786440 | tf_op jit(solution)/shard_map/ppermute | solution.py:11
  151.6 10.4 %collective-permute-done.19 = bf16[64,2048]{1,0:T(8,128)(2,1)S(1)} collective-permute-done((bf16[64,2048]{1,0:T(8,128)(2,1)S(1)}, bf16[64,2048]{1,0:T(8,128)(2,1)S(1)}, u32[]{:S(2)}, u32[]{:S(2)}) %collective-permute-start.19) | collective-permute-done | bytes 262176 | tf_op jit(solution)/shard_map/ppermute | solution.py:11
  162.0 4.1 %collective-permute-done.20 = bf16[64,2048]{1,0:T(8,128)(2,1)S(1)} collective-permute-done((bf16[64,2048]{1,0:T(8,128)(2,1)S(1)}, bf16[64,2048]{1,0:T(8,128)(2,1)S(1)}, u32[]{:S(2)}, u32[]{:S(2)}) %collective-permute-start.20) | collective-permute-done | bytes 262176 | tf_op jit(solution)/shard_map/ppermute | solution.py:11
  167.2 41.5 %reduce-scatter.2.cloned.1.call-done = bf16[32,2048]{1,0:T(8,128)(2,1)} async-done(((bf16[128,2048]{1,0:T(8,128)(2,1)}), bf16[32,2048]{1,0:T(8,128)(2,1)}) %reduce-scatter.2.cloned.1.call-update) | async-done | bytes 131088 | tf_op jit(solution)/shard_map/reduce_scatter | solution.py:137
  211.2 23.6 %all_gather.7 = bf16[128,2048]{1,0:T(8,128)(2,1)S(1)} all-gather(bf16[32,2048]{1,0:T(8,128)(2,1)S(1)} %multiply_convert_fusion.1), channel_id=1, replica_groups=mesh['y'=4,'x'=4,'zh'=4,'zl'=4,'c'=2] {'zh'}, dimensions={0}, use_global_device_ids=true | all-gather | bytes 655360 | tf_op jit(solution)/shard_map/all_gather | solution.py:140
  234.7 5.1 %collective-permute-start.21 = (bf16[128,2048]{1,0:T(8,128)(2,1)S(1)}, bf16[128,2048]{1,0:T(8,128)(2,1)S(1)}, u32[]{:S(2)}, u32[]{:S(2)}) collective-permute-start(bf16[128,2048]{1,0:T(8,128)(2,1)S(1)} %all_gather.7), channel_id=1, source_target_pairs={{2,0},{4,2},{6,4},{8,6},{10,8},{12,10},{14,12},{16,14},{18,16},{20... | collective-permute-start | bytes 1572872 | tf_op jit(solution)/shard_map/ppermute | solution.py:11
  241.8 3.1 collective-permute-start.24
  244.9 3.1 collective-permute-start.23
  248.0 5.2 %collective-permute-done.21 = bf16[128,2048]{1,0:T(8,128)(2,1)S(1)} collective-permute-done((bf16[128,2048]{1,0:T(8,128)(2,1)S(1)}, bf16[128,2048]{1,0:T(8,128)(2,1)S(1)}, u32[]{:S(2)}, u32[]{:S(2)}) %collective-permute-start.21) | collective-permute-done | bytes 524320 | tf_op jit(solution)/shard_map/ppermute | solution.py:11
  253.3 4.0 %collective-permute-done.22 = bf16[64,2048]{1,0:T(8,128)(2,1)S(1)} collective-permute-done((bf16[64,2048]{1,0:T(8,128)(2,1)S(1)}, bf16[64,2048]{1,0:T(8,128)(2,1)S(1)}, u32[]{:S(2)}, u32[]{:S(2)}) %collective-permute-start.22) | collective-permute-done | bytes 262176 | tf_op jit(solution)/shard_map/ppermute | solution.py:11
  257.3 8.8 %collective-permute-done.23 = bf16[64,2048]{1,0:T(8,128)(2,1)S(1)} collective-permute-done((bf16[64,2048]{1,0:T(8,128)(2,1)S(1)}, bf16[64,2048]{1,0:T(8,128)(2,1)S(1)}, u32[]{:S(2)}, u32[]{:S(2)}) %collective-permute-start.23) | collective-permute-done | bytes 262176 | tf_op jit(solution)/shard_map/ppermute | solution.py:11
  266.1 7.3 %collective-permute-start.25 = (bf16[512,2048]{1,0:T(8,128)(2,1)S(1)}, bf16[512,2048]{1,0:T(8,128)(2,1)S(1)}, u32[]{:S(2)}, u32[]{:S(2)}) collective-permute-start(bf16[512,2048]{1,0:T(8,128)(2,1)S(1)} %constant_dynamic-update-slice_fusion), channel_id=1, source_target_pairs={{0,1},{1,0},{2,3},{3,2},{4,5},{5,4},{6,7},{7,6},{8,9},{9,8},{10,11... | collective-permute-start | bytes 6291464 | tf_op jit(solution)/shard_map/ppermute | solution.py:18
  273.5 3.8 %collective-permute-done.25 = bf16[512,2048]{1,0:T(8,128)(2,1)S(1)} collective-permute-done((bf16[512,2048]{1,0:T(8,128)(2,1)S(1)}, bf16[512,2048]{1,0:T(8,128)(2,1)S(1)}, u32[]{:S(2)}, u32[]{:S(2)}) %collective-permute-start.25) | collective-permute-done | bytes 2097184 | tf_op jit(solution)/shard_map/ppermute | solution.py:18
  281.1 39.8 %all_to_all.10 = bf16[4,512,768]{2,1,0:T(8,128)(2,1)S(1)} all-to-all(bf16[4,512,768]{2,1,0:T(8,128)(2,1)S(1)} %bitcast.64), channel_id=1, replica_groups=mesh['y'=4,'x'=4,'zh'=4,'zl'=4,'c'=2] {'y'}, dimensions={0} | all-to-all | bytes 6291456 | tf_op jit(solution)/shard_map/all_to_all | solution.py:152
  322.5 15.4 %all_to_all.11 = bf16[4,128,768]{2,1,0:T(8,128)(2,1)S(1)} all-to-all(bf16[4,128,768]{2,1,0:T(8,128)(2,1)} %bitcast.69), channel_id=1, replica_groups=mesh['y'=4,'x'=4,'zh'=4,'zl'=4,'c'=2] {'x'}, dimensions={0} | all-to-all | bytes 1572864 | tf_op jit(solution)/shard_map/all_to_all | solution.py:152
  (123 shorter events, 56.5 us)
Async XLA Ops:
  7.2 92.2 %all-gather.2.cloned.1.call-start = ((), (), s32[]{:S(2)}) async-start(), calls=%async_computation.3 | async-start | bytes 4595712 | tf_op jit(solution)/shard_map/all_gather | solution.py:93
  11.7 197.1 %reduce-scatter.2.cloned.1.call-start = ((), (), s32[]{:S(2)}) async-start(), calls=%async_computation.4 | async-start | bytes 655360 | tf_op jit(solution)/shard_map/reduce_scatter | solution.py:137
  13.0 13.7 %collective-permute-start.10 = (bf16[64,2304]{1,0:T(8,128)(2,1)S(1)}, bf16[64,2304]{1,0:T(8,128)(2,1)S(1)}, u32[]{:S(2)}, u32[]{:S(2)}) collective-permute-start(bf16[64,2304]{1,0:T(8,128)(2,1)S(1)} %get-tuple-element.16), channel_id=1, source_target_pairs={{384,0},{0,128},{128,256},{256,384},{385,1},{1,129},{129,257},{257... | collective-permute-start | bytes 884744 | tf_op jit(solution)/shard_map/ppermute | solution.py:11
  17.0 11.7 %collective-permute-start.8 = (bf16[64,2304]{1,0:T(8,128)(2,1)S(1)}, bf16[64,2304]{1,0:T(8,128)(2,1)S(1)}, u32[]{:S(2)}, u32[]{:S(2)}) collective-permute-start(bf16[64,2304]{1,0:T(8,128)(2,1)S(1)} %get-tuple-element.16), channel_id=1, source_target_pairs={{128,0},{256,128},{384,256},{0,384},{129,1},{257,129},{385,257},{1... | collective-permute-start | bytes 884744 | tf_op jit(solution)/shard_map/ppermute | solution.py:11
  20.4 12.9 %collective-permute-start = (bf16[64,2304]{1,0:T(8,128)(2,1)S(1)}, bf16[64,2304]{1,0:T(8,128)(2,1)S(1)}, u32[]{:S(2)}, u32[]{:S(2)}) collective-permute-start(bf16[64,2304]{1,0:T(8,128)(2,1)S(1)} %get-tuple-element.17), channel_id=1, source_target_pairs={{32,0},{64,32},{96,64},{0,96},{33,1},{65,33},{97,65},{1,97},{34,2}... | collective-permute-start | bytes 884744 | tf_op jit(solution)/shard_map/ppermute | solution.py:11
  24.8 13.1 %collective-permute-start.2 = (bf16[64,2304]{1,0:T(8,128)(2,1)S(1)}, bf16[64,2304]{1,0:T(8,128)(2,1)S(1)}, u32[]{:S(2)}, u32[]{:S(2)}) collective-permute-start(bf16[64,2304]{1,0:T(8,128)(2,1)S(1)} %get-tuple-element.17), channel_id=1, source_target_pairs={{96,0},{0,32},{32,64},{64,96},{97,1},{1,33},{33,65},{65,97},{98,2}... | collective-permute-start | bytes 884744 | tf_op jit(solution)/shard_map/ppermute | solution.py:11
  26.7 13.1 %collective-permute-start.11 = (bf16[32,2304]{1,0:T(8,128)(2,1)S(1)}, bf16[32,2304]{1,0:T(8,128)(2,1)S(1)}, u32[]{:S(2)}, u32[]{:S(2)}) collective-permute-start(bf16[32,2304]{1,0:T(8,128)(2,1)S(1)} %slice.87), channel_id=1, source_target_pairs={{384,0},{0,128},{128,256},{256,384},{385,1},{1,129},{129,257},{257... | collective-permute-start | bytes 442376 | tf_op jit(solution)/shard_map/ppermute | solution.py:11
  28.7 11.2 %collective-permute-start.9 = (bf16[32,2304]{1,0:T(8,128)(2,1)S(1)}, bf16[32,2304]{1,0:T(8,128)(2,1)S(1)}, u32[]{:S(2)}, u32[]{:S(2)}) collective-permute-start(bf16[32,2304]{1,0:T(8,128)(2,1)S(1)} %slice.86), channel_id=1, source_target_pairs={{128,0},{256,128},{384,256},{0,384},{129,1},{257,129},{385,257},{1... | collective-permute-start | bytes 442376 | tf_op jit(solution)/shard_map/ppermute | solution.py:11
  33.3 13.3 %collective-permute-start.1 = (bf16[32,2304]{1,0:T(8,128)(2,1)S(1)}, bf16[32,2304]{1,0:T(8,128)(2,1)S(1)}, u32[]{:S(2)}, u32[]{:S(2)}) collective-permute-start(bf16[32,2304]{1,0:T(8,128)(2,1)S(1)} %slice.81), channel_id=1, source_target_pairs={{32,0},{64,32},{96,64},{0,96},{33,1},{65,33},{97,65},{1,97},{34,2}... | collective-permute-start | bytes 442376 | tf_op jit(solution)/shard_map/ppermute | solution.py:11
  37.9 8.7 %collective-permute-start.3 = (bf16[32,2304]{1,0:T(8,128)(2,1)S(1)}, bf16[32,2304]{1,0:T(8,128)(2,1)S(1)}, u32[]{:S(2)}, u32[]{:S(2)}) collective-permute-start(bf16[32,2304]{1,0:T(8,128)(2,1)S(1)} %slice.82), channel_id=1, source_target_pairs={{96,0},{0,32},{32,64},{64,96},{97,1},{1,33},{33,65},{65,97},{98,2}... | collective-permute-start | bytes 442376 | tf_op jit(solution)/shard_map/ppermute | solution.py:11
  40.1 26.6 %collective-permute-start.12 = (bf16[4,64,2304]{2,1,0:T(8,128)(2,1)S(1)}, bf16[4,64,2304]{2,1,0:T(8,128)(2,1)S(1)}, u32[]{:S(2)}, u32[]{:S(2)}) collective-permute-start(bf16[4,64,2304]{2,1,0:T(8,128)(2,1)S(1)} %get-tuple-element.11), channel_id=1, source_target_pairs={{32,0},{64,32},{96,64},{0,96},{33,1},{65,33},{97,65},{1,97},{34,2}... | collective-permute-start | bytes 3538952 | tf_op jit(solution)/shard_map/ppermute | solution.py:11
  44.7 26.3 %collective-permute-start.14 = (bf16[4,64,2304]{2,1,0:T(8,128)(2,1)S(1)}, bf16[4,64,2304]{2,1,0:T(8,128)(2,1)S(1)}, u32[]{:S(2)}, u32[]{:S(2)}) collective-permute-start(bf16[4,64,2304]{2,1,0:T(8,128)(2,1)S(1)} %get-tuple-element.11), channel_id=1, source_target_pairs={{96,0},{0,32},{32,64},{64,96},{97,1},{1,33},{33,65},{65,97},{98,2}... | collective-permute-start | bytes 3538952 | tf_op jit(solution)/shard_map/ppermute | solution.py:11
  46.9 28.0 %collective-permute-start.4 = (bf16[4,64,2304]{2,1,0:T(8,128)(2,1)S(1)}, bf16[4,64,2304]{2,1,0:T(8,128)(2,1)S(1)}, u32[]{:S(2)}, u32[]{:S(2)}) collective-permute-start(bf16[4,64,2304]{2,1,0:T(8,128)(2,1)S(1)} %get-tuple-element.13), channel_id=1, source_target_pairs={{128,0},{256,128},{384,256},{0,384},{129,1},{257,129},{385,257},{1... | collective-permute-start | bytes 3538952 | tf_op jit(solution)/shard_map/ppermute | solution.py:11
  49.0 30.1 %collective-permute-start.6 = (bf16[4,64,2304]{2,1,0:T(8,128)(2,1)S(1)}, bf16[4,64,2304]{2,1,0:T(8,128)(2,1)S(1)}, u32[]{:S(2)}, u32[]{:S(2)}) collective-permute-start(bf16[4,64,2304]{2,1,0:T(8,128)(2,1)S(1)} %get-tuple-element.13), channel_id=1, source_target_pairs={{384,0},{0,128},{128,256},{256,384},{385,1},{1,129},{129,257},{257... | collective-permute-start | bytes 3538952 | tf_op jit(solution)/shard_map/ppermute | solution.py:11
  67.6 16.5 %collective-permute-start.13 = (bf16[4,32,2304]{2,1,0:T(8,128)(2,1)}, bf16[4,32,2304]{2,1,0:T(8,128)(2,1)}, u32[]{:S(2)}, u32[]{:S(2)}) collective-permute-start(bf16[4,32,2304]{2,1,0:T(8,128)(2,1)} %slice.88), channel_id=1, source_target_pairs={{32,0},{64,32},{96,64},{0,96},{33,1},{65,33},{97,65},{1,97},{34,2}... | collective-permute-start | bytes 1769480 | tf_op jit(solution)/shard_map/ppermute | solution.py:11
  72.9 12.3 %collective-permute-start.15 = (bf16[4,32,2304]{2,1,0:T(8,128)(2,1)}, bf16[4,32,2304]{2,1,0:T(8,128)(2,1)}, u32[]{:S(2)}, u32[]{:S(2)}) collective-permute-start(bf16[4,32,2304]{2,1,0:T(8,128)(2,1)} %slice.89), channel_id=1, source_target_pairs={{96,0},{0,32},{32,64},{64,96},{97,1},{1,33},{33,65},{65,97},{98,2}... | collective-permute-start | bytes 1769480 | tf_op jit(solution)/shard_map/ppermute | solution.py:11
  76.8 11.2 %collective-permute-start.5 = (bf16[4,32,2304]{2,1,0:T(8,128)(2,1)}, bf16[4,32,2304]{2,1,0:T(8,128)(2,1)}, u32[]{:S(2)}, u32[]{:S(2)}) collective-permute-start(bf16[4,32,2304]{2,1,0:T(8,128)(2,1)} %slice.83), channel_id=1, source_target_pairs={{128,0},{256,128},{384,256},{0,384},{129,1},{257,129},{385,257},{1... | collective-permute-start | bytes 1769480 | tf_op jit(solution)/shard_map/ppermute | solution.py:11
  80.9 12.1 %collective-permute-start.7 = (bf16[4,32,2304]{2,1,0:T(8,128)(2,1)}, bf16[4,32,2304]{2,1,0:T(8,128)(2,1)}, u32[]{:S(2)}, u32[]{:S(2)}) collective-permute-start(bf16[4,32,2304]{2,1,0:T(8,128)(2,1)} %slice.84), channel_id=1, source_target_pairs={{384,0},{0,128},{128,256},{256,384},{385,1},{1,129},{129,257},{257... | collective-permute-start | bytes 1769480 | tf_op jit(solution)/shard_map/ppermute | solution.py:11
  84.1 10.3 %copy-start.1 = (bf16[4,64,2304]{2,1,0:T(8,128)(2,1)S(1)}, bf16[4,64,2304]{2,1,0:T(8,128)(2,1)}, u32[]{:S(2)}) copy-start(bf16[4,64,2304]{2,1,0:T(8,128)(2,1)} %copy-done) | copy-start | bytes 3538948
  96.9 10.9 %slice-start = ((s8[4718592]{0:T(1024)(128)(4,1)}), s8[524288]{0:T(1024)(128)(4,1)S(1)}, s32[]{:S(2)}) async-start(s8[4718592]{0:T(1024)(128)(4,1)} %bitcast.53), calls=%async_computation.5 | async-start | bytes 1048576
  114.1 13.3 %collective-permute-start.16 = (bf16[512,2048]{1,0:T(8,128)(2,1)S(1)}, bf16[512,2048]{1,0:T(8,128)(2,1)S(1)}, u32[]{:S(2)}, u32[]{:S(2)}) collective-permute-start(bf16[512,2048]{1,0:T(8,128)(2,1)S(1)} %convolution_convert_fusion), channel_id=1, source_target_pairs={{0,1},{1,0},{2,3},{3,2},{4,5},{5,4},{6,7},{7,6},{8,9},{9,8},{10,11... | collective-permute-start | bytes 6291464 | tf_op jit(solution)/shard_map/ppermute | solution.py:18
  129.4 36.7 %collective-permute-start.17 = (bf16[128,2048]{1,0:T(8,128)(2,1)S(1)}, bf16[128,2048]{1,0:T(8,128)(2,1)S(1)}, u32[]{:S(2)}, u32[]{:S(2)}) collective-permute-start(bf16[128,2048]{1,0:T(8,128)(2,1)S(1)} %get-tuple-element.6), channel_id=1, source_target_pairs={{30,0},{0,2},{2,4},{4,6},{6,8},{8,10},{10,12},{12,14},{14,16},{16,... | collective-permute-start | bytes 1572872 | tf_op jit(solution)/shard_map/ppermute | solution.py:11
  134.4 76.7 %copy-start.7 = (f32[32]{0:T(128)S(1)}, f32[32]{0:T(128)}, u32[]{:S(2)}) copy-start(f32[32]{0:T(128)} %param.10) | copy-start | bytes 388
  134.4 31.7 %collective-permute-start.18 = (bf16[128,2048]{1,0:T(8,128)(2,1)S(1)}, bf16[128,2048]{1,0:T(8,128)(2,1)S(1)}, u32[]{:S(2)}, u32[]{:S(2)}) collective-permute-start(bf16[128,2048]{1,0:T(8,128)(2,1)S(1)} %get-tuple-element.7), channel_id=1, source_target_pairs={{2,0},{4,2},{6,4},{8,6},{10,8},{12,10},{14,12},{16,14},{18,16},{20... | collective-permute-start | bytes 1572872 | tf_op jit(solution)/shard_map/ppermute | solution.py:11
  143.9 18.0 %collective-permute-start.19 = (bf16[64,2048]{1,0:T(8,128)(2,1)S(1)}, bf16[64,2048]{1,0:T(8,128)(2,1)S(1)}, u32[]{:S(2)}, u32[]{:S(2)}) collective-permute-start(bf16[64,2048]{1,0:T(8,128)(2,1)S(1)} %get-tuple-element.4), channel_id=1, source_target_pairs={{28,0},{30,2},{0,4},{2,6},{4,8},{6,10},{8,12},{10,14},{12,16},{14,... | collective-permute-start | bytes 786440 | tf_op jit(solution)/shard_map/ppermute | solution.py:11
  145.9 20.2 %collective-permute-start.20 = (bf16[64,2048]{1,0:T(8,128)(2,1)S(1)}, bf16[64,2048]{1,0:T(8,128)(2,1)S(1)}, u32[]{:S(2)}, u32[]{:S(2)}) collective-permute-start(bf16[64,2048]{1,0:T(8,128)(2,1)S(1)} %get-tuple-element.5), channel_id=1, source_target_pairs={{4,0},{6,2},{8,4},{10,6},{12,8},{14,10},{16,12},{18,14},{20,16},{2... | collective-permute-start | bytes 786440 | tf_op jit(solution)/shard_map/ppermute | solution.py:11
  211.0 68.1 %copy-start.6 = (bf16[32,2048]{1,0:T(8,128)(2,1)}, bf16[32,2048]{1,0:T(8,128)(2,1)S(1)}, u32[]{:S(2)}) copy-start(bf16[32,2048]{1,0:T(8,128)(2,1)S(1)} %reshape.68) | copy-start | bytes 393220
  234.7 18.5 %collective-permute-start.21 = (bf16[128,2048]{1,0:T(8,128)(2,1)S(1)}, bf16[128,2048]{1,0:T(8,128)(2,1)S(1)}, u32[]{:S(2)}, u32[]{:S(2)}) collective-permute-start(bf16[128,2048]{1,0:T(8,128)(2,1)S(1)} %all_gather.7), channel_id=1, source_target_pairs={{2,0},{4,2},{6,4},{8,6},{10,8},{12,10},{14,12},{16,14},{18,16},{20... | collective-permute-start | bytes 1572872 | tf_op jit(solution)/shard_map/ppermute | solution.py:11
  239.8 17.4 %collective-permute-start.22 = (bf16[64,2048]{1,0:T(8,128)(2,1)S(1)}, bf16[64,2048]{1,0:T(8,128)(2,1)S(1)}, u32[]{:S(2)}, u32[]{:S(2)}) collective-permute-start(bf16[64,2048]{1,0:T(8,128)(2,1)S(1)} %get-tuple-element.19), channel_id=1, source_target_pairs={{4,0},{6,2},{8,4},{10,6},{12,8},{14,10},{16,12},{18,14},{20,16},{2... | collective-permute-start | bytes 786440 | tf_op jit(solution)/shard_map/ppermute | solution.py:11
  241.8 24.3 %collective-permute-start.24 = (bf16[128,2048]{1,0:T(8,128)(2,1)S(1)}, bf16[128,2048]{1,0:T(8,128)(2,1)S(1)}, u32[]{:S(2)}, u32[]{:S(2)}) collective-permute-start(bf16[128,2048]{1,0:T(8,128)(2,1)S(1)} %all_gather.7), channel_id=1, source_target_pairs={{30,0},{0,2},{2,4},{4,6},{6,8},{8,10},{10,12},{12,14},{14,16},{16,... | collective-permute-start | bytes 1572872 | tf_op jit(solution)/shard_map/ppermute | solution.py:11
  244.9 21.1 %collective-permute-start.23 = (bf16[64,2048]{1,0:T(8,128)(2,1)S(1)}, bf16[64,2048]{1,0:T(8,128)(2,1)S(1)}, u32[]{:S(2)}, u32[]{:S(2)}) collective-permute-start(bf16[64,2048]{1,0:T(8,128)(2,1)S(1)} %get-tuple-element.18), channel_id=1, source_target_pairs={{28,0},{30,2},{0,4},{2,6},{4,8},{6,10},{8,12},{10,14},{12,16},{14,... | collective-permute-start | bytes 786440 | tf_op jit(solution)/shard_map/ppermute | solution.py:11
  266.1 11.1 %collective-permute-start.25 = (bf16[512,2048]{1,0:T(8,128)(2,1)S(1)}, bf16[512,2048]{1,0:T(8,128)(2,1)S(1)}, u32[]{:S(2)}, u32[]{:S(2)}) collective-permute-start(bf16[512,2048]{1,0:T(8,128)(2,1)S(1)} %constant_dynamic-update-slice_fusion), channel_id=1, source_target_pairs={{0,1},{1,0},{2,3},{3,2},{4,5},{5,4},{6,7},{7,6},{8,9},{9,8},{10,11... | collective-permute-start | bytes 6291464 | tf_op jit(solution)/shard_map/ppermute | solution.py:18
  (10 other events, 46.6 us)
Sparse Core Ops, SparseCore 0:
  11.8 80.2 all-gather.1
  167.3 41.4 reduce-scatter.1

commit v4 on v1

--- a/solution.py
+++ b/solution.py
@@ -101,18 +101,24 @@
     paired = (tangent(home) + other.astype(F32)).astype(BF)
     jv = lax.psum_scatter(paired, "z", scatter_dimension=0, tiled=True)
     output_tangent = to_absolute(jv, y, x)
-    curved = (curvature[:, None] * output_tangent.astype(F32)).astype(BF)
-    spread = lax.all_gather(curved, ("z", "c"), axis=0, tiled=True)
+    curved = curvature[:, None] * output_tangent.astype(F32)
+    peak = jnp.max(jnp.abs(curved), axis=1, keepdims=True)
+    power = jnp.floor(jnp.log2(jnp.maximum(peak, 1e-30)))
+    scaled = jnp.concatenate(
+        [curved * jnp.exp2(-power), jnp.broadcast_to(power, (rows, 128))], 1
+    ).astype(jnp.float16)
+    spread = lax.all_gather(scaled, ("z", "c"), axis=0, tiled=True)
+    lifted = hidden.astype(F32) * jnp.exp2(spread[:, width : width + 1].astype(F32))
     part = lax.dot_general(
-        spread, hidden, (((0,), (0,)), ((), ())), preferred_element_type=F32
+        spread[:, :width].astype(BF),
+        lifted.astype(BF),
+        (((0,), (0,)), ((), ())),
+        preferred_element_type=F32,
     ).astype(BF)
-
-    def add_over(value, axis):
-        value = value.reshape(4, -1, hidden_width)
-        moved = lax.all_to_all(value, axis, 0, 0, tiled=True)
-        return jnp.sum(moved.astype(F32), axis=0).astype(BF)
-
-    product = add_over(add_over(part, "y"), "x")
+    moved = lax.all_to_all(
+        part.reshape(16, -1, hidden_width), ("y", "x"), 0, 0, tiled=True
+    )
+    product = jnp.sum(moved.astype(F32), axis=0).astype(BF)
     return output_tangent, product[None]
 
 

time: 354 us -> 312 us (0.88)
  waiting for transfers between devices: 174 us -> 91.9 us
  blocking collectives: 55.8 us -> 100 us
    all_gather x1 -> x0, waiting for transfers between devices: 82.8 us -> none  [local(): spread = lax.all_gather(curved, ('z', 'c'), axis=0, tiled=True)]
    all_gather x0 -> x1, blocking collectives: none -> 54.8 us  [local(): spread = lax.all_gather(scaled, ('z', 'c'), axis=0, tiled=True)]
    all_to_all x2 -> x1, blocking collectives: 55.8 us -> 45.2 us  [local(): lax.all_to_all(part.reshape(16, -1, hidden_width), ('y', 'x'), 0, 0, tile...]
  transfers between devices with their start and end apart: 20 -> 19, of which waited for: 7 -> 6; matrix products, arithmetic and copies ran while one was open for 4% -> 4% of each run, Pallas kernels for 0% -> 0%
where the time goes in v4:
time: 312 us; the launch traced here: 311 us
  blocking collectives  100 us (32%)
  waiting for transfers between devices  91.9 us (29%)
  starting transfers between devices  58.8 us (19%)
  matrix products  20.1 us (6%)
  between operations  14.7 us (5%)
  other arithmetic  13.7 us (4%)
  local copies, waits for them, and re-layouts  12.2 us (4%)
    reduce_scatter x1, waiting for transfers between devices, local(): jv = lax.psum_scatter(paired, 'z', scatter_dimension=0, tiled=True)  65.9 us
    all_gather x1, blocking collectives, local(): spread = lax.all_gather(scaled, ('z', 'c'), axis=0, tiled=True)  54.8 us
    ppermute x16, starting transfers between devices, fetch(): lax.ppermute(value, axis, [((i + shift) % size, i) for i in range(size)])  49.2 us
    all_to_all x1, blocking collectives, local(): lax.all_to_all(part.reshape(16, -1, hidden_width), ('y', 'x'), 0, 0, tile...  45.2 us
    ppermute x16, waiting for transfers between devices, fetch(): lax.ppermute(value, axis, [((i + shift) % size, i) for i in range(size)])  22.2 us
    ppermute x1, starting transfers between devices, local(): other = lax.ppermute(tangent(away).astype(BF), 'c', [(0, 1), (1, 0)])  9.5 us
    another operation x8, other arithmetic, ring4(): return jnp.stack([value, after, jnp.concatenate([low, high], -2), before])  7.98 us
    dot_general x1, matrix products, local(): jnp.dot(group, weights[:, :hidden_width], preferred_element_type=F32)  7.14 us
  transfers between devices with their start and end apart: 19, of which 6 were waited for; matrix products, arithmetic and copies ran while one was open for 4% of the time, Pallas kernels for 0%

profile of v4, /device:TPU:1, one launch (start us, length us, event | category | flops | bytes accessed | tf_op | source)
XLA Modules:
  0.0 311.3 jit_solution(12614923203611955186)
XLA Ops:
  13.0 4.0 %collective-permute-start.10 = (bf16[64,2304]{1,0:T(8,128)(2,1)S(1)}, bf16[64,2304]{1,0:T(8,128)(2,1)S(1)}, u32[]{:S(2)}, u32[]{:S(2)}) collective-permute-start(bf16[64,2304]{1,0:T(8,128)(2,1)S(1)} %get-tuple-element.14), channel_id=1, source_target_pairs={{384,0},{0,128},{128,256},{256,384},{385,1},{1,129},{129,257},{257... | collective-permute-start | bytes 884744 | tf_op jit(solution)/shard_map/ppermute | solution.py:11
  17.0 3.4 %collective-permute-start.8 = (bf16[64,2304]{1,0:T(8,128)(2,1)S(1)}, bf16[64,2304]{1,0:T(8,128)(2,1)S(1)}, u32[]{:S(2)}, u32[]{:S(2)}) collective-permute-start(bf16[64,2304]{1,0:T(8,128)(2,1)S(1)} %get-tuple-element.14), channel_id=1, source_target_pairs={{128,0},{256,128},{384,256},{0,384},{129,1},{257,129},{385,257},{1... | collective-permute-start | bytes 884744 | tf_op jit(solution)/shard_map/ppermute | solution.py:11
  20.4 4.4 %collective-permute-start = (bf16[64,2304]{1,0:T(8,128)(2,1)S(1)}, bf16[64,2304]{1,0:T(8,128)(2,1)S(1)}, u32[]{:S(2)}, u32[]{:S(2)}) collective-permute-start(bf16[64,2304]{1,0:T(8,128)(2,1)S(1)} %get-tuple-element.15), channel_id=1, source_target_pairs={{32,0},{64,32},{96,64},{0,96},{33,1},{65,33},{97,65},{1,97},{34,2}... | collective-permute-start | bytes 884744 | tf_op jit(solution)/shard_map/ppermute | solution.py:11
  24.8 1.9 collective-permute-start.2
  26.7 1.9 collective-permute-start.11
  28.7 4.6 %collective-permute-start.9 = (bf16[32,2304]{1,0:T(8,128)(2,1)S(1)}, bf16[32,2304]{1,0:T(8,128)(2,1)S(1)}, u32[]{:S(2)}, u32[]{:S(2)}) collective-permute-start(bf16[32,2304]{1,0:T(8,128)(2,1)S(1)} %slice.76), channel_id=1, source_target_pairs={{128,0},{256,128},{384,256},{0,384},{129,1},{257,129},{385,257},{1... | collective-permute-start | bytes 442376 | tf_op jit(solution)/shard_map/ppermute | solution.py:11
  33.3 4.6 %collective-permute-start.1 = (bf16[32,2304]{1,0:T(8,128)(2,1)S(1)}, bf16[32,2304]{1,0:T(8,128)(2,1)S(1)}, u32[]{:S(2)}, u32[]{:S(2)}) collective-permute-start(bf16[32,2304]{1,0:T(8,128)(2,1)S(1)} %slice.71), channel_id=1, source_target_pairs={{32,0},{64,32},{96,64},{0,96},{33,1},{65,33},{97,65},{1,97},{34,2}... | collective-permute-start | bytes 442376 | tf_op jit(solution)/shard_map/ppermute | solution.py:11
  37.9 1.9 collective-permute-start.3
  40.1 4.6 %collective-permute-start.12 = (bf16[4,64,2304]{2,1,0:T(8,128)(2,1)S(1)}, bf16[4,64,2304]{2,1,0:T(8,128)(2,1)S(1)}, u32[]{:S(2)}, u32[]{:S(2)}) collective-permute-start(bf16[4,64,2304]{2,1,0:T(8,128)(2,1)S(1)} %get-tuple-element.9), channel_id=1, source_target_pairs={{32,0},{64,32},{96,64},{0,96},{33,1},{65,33},{97,65},{1,97},{34,2}... | collective-permute-start | bytes 3538952 | tf_op jit(solution)/shard_map/ppermute | solution.py:11
  44.7 1.9 collective-permute-start.14
  46.9 2.2 collective-permute-start.4
  49.0 3.1 %collective-permute-start.6 = (bf16[4,64,2304]{2,1,0:T(8,128)(2,1)S(1)}, bf16[4,64,2304]{2,1,0:T(8,128)(2,1)S(1)}, u32[]{:S(2)}, u32[]{:S(2)}) collective-permute-start(bf16[4,64,2304]{2,1,0:T(8,128)(2,1)S(1)} %get-tuple-element.11), channel_id=1, source_target_pairs={{384,0},{0,128},{128,256},{256,384},{385,1},{1,129},{129,257},{257... | collective-permute-start | bytes 3538952 | tf_op jit(solution)/shard_map/ppermute | solution.py:11
  52.2 14.6 %collective-permute-done.12 = bf16[4,64,2304]{2,1,0:T(8,128)(2,1)S(1)} collective-permute-done((bf16[4,64,2304]{2,1,0:T(8,128)(2,1)S(1)}, bf16[4,64,2304]{2,1,0:T(8,128)(2,1)S(1)}, u32[]{:S(2)}, u32[]{:S(2)}) %collective-permute-start.12) | collective-permute-done | bytes 1179680 | tf_op jit(solution)/shard_map/ppermute | solution.py:11
  67.6 3.4 %collective-permute-start.13 = (bf16[4,32,2304]{2,1,0:T(8,128)(2,1)}, bf16[4,32,2304]{2,1,0:T(8,128)(2,1)}, u32[]{:S(2)}, u32[]{:S(2)}) collective-permute-start(bf16[4,32,2304]{2,1,0:T(8,128)(2,1)} %slice.78), channel_id=1, source_target_pairs={{32,0},{64,32},{96,64},{0,96},{33,1},{65,33},{97,65},{1,97},{34,2}... | collective-permute-start | bytes 1769480 | tf_op jit(solution)/shard_map/ppermute | solution.py:11
  73.0 1.9 collective-permute-start.15
  76.8 2.3 collective-permute-start.5
  81.0 3.1 %collective-permute-start.7 = (bf16[4,32,2304]{2,1,0:T(8,128)(2,1)}, bf16[4,32,2304]{2,1,0:T(8,128)(2,1)}, u32[]{:S(2)}, u32[]{:S(2)}) collective-permute-start(bf16[4,32,2304]{2,1,0:T(8,128)(2,1)} %slice.74), channel_id=1, source_target_pairs={{384,0},{0,128},{128,256},{256,384},{385,1},{1,129},{129,257},{257... | collective-permute-start | bytes 1769480 | tf_op jit(solution)/shard_map/ppermute | solution.py:11
  85.3 1.3 maximum_bitcast_fusion.1
  86.6 1.4 collective-permute-done.5
  88.0 5.1 %collective-permute-done.7 = bf16[4,32,2304]{2,1,0:T(8,128)(2,1)} collective-permute-done((bf16[4,32,2304]{2,1,0:T(8,128)(2,1)}, bf16[4,32,2304]{2,1,0:T(8,128)(2,1)}, u32[]{:S(2)}, u32[]{:S(2)}) %collective-permute-start.7) | collective-permute-done | bytes 589856 | tf_op jit(solution)/shard_map/ppermute | solution.py:11
  94.5 2.5 pad_maximum_fusion.1
  97.0 2.5 pad_maximum_fusion
  100.7 7.1 %fusion.3 = f32[1024,768]{1,0:T(8,128)S(1)} fusion(bf16[1024,2176]{1,0:T(8,128)(2,1)} %all-gather.3.cloned.1.call-done, bf16[1024,2304]{1,0:T(8,128)(2,1)} %bitcast.45, bf16[1024,2304]{1,0:T(8,128)(2,1)} %bitcast.39), kind=kOutput, calls=%fused_computation.11 | convolution fusion | flops 3227516928 | bytes 16777216 | tf_op jit(solution)/shard_map/dot_general | solution.py:82
  108.0 3.7 %multiply_convert_fusion.1 = bf16[1024,768]{1,0:T(8,128)(2,1)S(1)} fusion(f32[1024,768]{1,0:T(8,128)S(1)} %fusion.3, f32[1024]{0:T(1024)S(1)} %select_reduce_fusion, bf16[1024,2304]{1,0:T(8,128)(2,1)S(1)} %bitcast.48, bf16[1024,2304]{1,0:T(8,128)(2,1)S(1)} %bitcast.42, bf16[1024,2176]{1,0:T(8,128)(2,1)S(1)} %bitcast.69), kind=kOutput, calls=%fused_computation.18 | convolution fusion | flops 3233021952 | bytes 18354176 | tf_op jit(solution)/shard_map/dot_general | solution.py:83
  111.8 1.8 convolution_convert_fusion
  113.7 9.5 %collective-permute-start.16 = (bf16[512,2048]{1,0:T(8,128)(2,1)S(1)}, bf16[512,2048]{1,0:T(8,128)(2,1)S(1)}, u32[]{:S(2)}, u32[]{:S(2)}) collective-permute-start(bf16[512,2048]{1,0:T(8,128)(2,1)S(1)} %convolution_convert_fusion), channel_id=1, source_target_pairs={{0,1},{1,0},{2,3},{3,2},{4,5},{5,4},{6,7},{7,6},{8,9},{9,8},{10,11... | collective-permute-start | bytes 6291464 | tf_op jit(solution)/shard_map/ppermute | solution.py:100
  123.2 3.8 %collective-permute-done.16 = bf16[512,2048]{1,0:T(8,128)(2,1)S(1)} collective-permute-done((bf16[512,2048]{1,0:T(8,128)(2,1)S(1)}, bf16[512,2048]{1,0:T(8,128)(2,1)S(1)}, u32[]{:S(2)}, u32[]{:S(2)}) %collective-permute-start.16) | collective-permute-done | bytes 2097184 | tf_op jit(solution)/shard_map/ppermute | solution.py:100
  126.9 3.2 %add_convert_fusion = bf16[512,2048]{1,0:T(8,128)(2,1)} fusion(bf16[512,2048]{1,0:T(8,128)(2,1)S(1)} %collective-permute-done.16, bf16[512,768]{1,0:T(8,128)(2,1)S(1)} %bitcast.51, bf16[1024,2304]{1,0:T(8,128)(2,1)S(1)} %bitcast.44, bf16[1024,2304]{1,0:T(8,128)(2,1)S(1)} %bitcast.50), kind=kOutput, calls=%fused_computation.8 | convolution fusion | flops 1620049920 | bytes 14417920 | tf_op jit(solution)/shard_map/dot_general | solution.py:93
  130.2 65.9 %reduce-scatter.2.cloned.1.call-done = bf16[32,2048]{1,0:T(8,128)(2,1)} async-done(((bf16[512,2048]{1,0:T(8,128)(2,1)}), bf16[32,2048]{1,0:T(8,128)(2,1)}) %reduce-scatter.2.cloned.1.call-update) | async-done | bytes 131088 | tf_op jit(solution)/shard_map/reduce_scatter | solution.py:102
  198.9 54.8 %all-gather.4 = f16[1024,2176]{1,0:T(8,128)(2,1)S(1)} all-gather(f16[32,2176]{1,0:T(8,128)(2,1)S(1)} %pad_maximum_fusion.6), channel_id=1, replica_groups=mesh['y'=4,'x'=4,'z'=16,'c'=2] {'z','c'}, dimensions={0}, use_global_device_ids=true | all-gather | bytes 4595712 | tf_op jit(solution)/shard_map/all_gather | solution.py:110
  253.9 4.2 %fusion.5 = bf16[2048,768]{1,0:T(8,128)(2,1)S(1)} fusion(f16[1024,2176]{1,0:T(8,128)(2,1)S(1)} %all-gather.4, bf16[1024,768]{1,0:T(8,128)(2,1)S(1)} %multiply_convert_fusion.1, f32[1024]{0:T(1024)S(1)} %exponential_reduce_fusion), kind=kOutput, calls=%fused_computation.13 | convolution fusion | flops 3227254784 | bytes 8916992 | tf_op jit(solution)/shard_map/dot_general | solution.py:112
  258.1 45.2 %all_to_all.5 = bf16[16,128,768]{2,1,0:T(8,128)(2,1)S(1)} all-to-all(bf16[16,128,768]{2,1,0:T(8,128)(2,1)S(1)} %bitcast.52), channel_id=1, replica_groups=mesh['y'=4,'x'=4,'z'=16,'c'=2] {'y','x'}, dimensions={0} | all-to-all | bytes 6291456 | tf_op jit(solution)/shard_map/all_to_all | solution.py:118
  (95 shorter events, 20.8 us)
Async XLA Ops:
  7.2 92.3 %all-gather.3.cloned.1.call-start = ((), (), s32[]{:S(2)}) async-start(), calls=%async_computation.2 | async-start | bytes 4595712 | tf_op jit(solution)/shard_map/all_gather | solution.py:66
  11.7 184.4 %reduce-scatter.2.cloned.1.call-start = ((), (), s32[]{:S(2)}) async-start(), calls=%async_computation.3 | async-start | bytes 2228224 | tf_op jit(solution)/shard_map/reduce_scatter | solution.py:102
  13.0 13.7 %collective-permute-start.10 = (bf16[64,2304]{1,0:T(8,128)(2,1)S(1)}, bf16[64,2304]{1,0:T(8,128)(2,1)S(1)}, u32[]{:S(2)}, u32[]{:S(2)}) collective-permute-start(bf16[64,2304]{1,0:T(8,128)(2,1)S(1)} %get-tuple-element.14), channel_id=1, source_target_pairs={{384,0},{0,128},{128,256},{256,384},{385,1},{1,129},{129,257},{257... | collective-permute-start | bytes 884744 | tf_op jit(solution)/shard_map/ppermute | solution.py:11
  17.0 11.7 %collective-permute-start.8 = (bf16[64,2304]{1,0:T(8,128)(2,1)S(1)}, bf16[64,2304]{1,0:T(8,128)(2,1)S(1)}, u32[]{:S(2)}, u32[]{:S(2)}) collective-permute-start(bf16[64,2304]{1,0:T(8,128)(2,1)S(1)} %get-tuple-element.14), channel_id=1, source_target_pairs={{128,0},{256,128},{384,256},{0,384},{129,1},{257,129},{385,257},{1... | collective-permute-start | bytes 884744 | tf_op jit(solution)/shard_map/ppermute | solution.py:11
  20.4 12.9 %collective-permute-start = (bf16[64,2304]{1,0:T(8,128)(2,1)S(1)}, bf16[64,2304]{1,0:T(8,128)(2,1)S(1)}, u32[]{:S(2)}, u32[]{:S(2)}) collective-permute-start(bf16[64,2304]{1,0:T(8,128)(2,1)S(1)} %get-tuple-element.15), channel_id=1, source_target_pairs={{32,0},{64,32},{96,64},{0,96},{33,1},{65,33},{97,65},{1,97},{34,2}... | collective-permute-start | bytes 884744 | tf_op jit(solution)/shard_map/ppermute | solution.py:11
  24.8 13.1 %collective-permute-start.2 = (bf16[64,2304]{1,0:T(8,128)(2,1)S(1)}, bf16[64,2304]{1,0:T(8,128)(2,1)S(1)}, u32[]{:S(2)}, u32[]{:S(2)}) collective-permute-start(bf16[64,2304]{1,0:T(8,128)(2,1)S(1)} %get-tuple-element.15), channel_id=1, source_target_pairs={{96,0},{0,32},{32,64},{64,96},{97,1},{1,33},{33,65},{65,97},{98,2}... | collective-permute-start | bytes 884744 | tf_op jit(solution)/shard_map/ppermute | solution.py:11
  26.7 13.1 %collective-permute-start.11 = (bf16[32,2304]{1,0:T(8,128)(2,1)S(1)}, bf16[32,2304]{1,0:T(8,128)(2,1)S(1)}, u32[]{:S(2)}, u32[]{:S(2)}) collective-permute-start(bf16[32,2304]{1,0:T(8,128)(2,1)S(1)} %slice.77), channel_id=1, source_target_pairs={{384,0},{0,128},{128,256},{256,384},{385,1},{1,129},{129,257},{257... | collective-permute-start | bytes 442376 | tf_op jit(solution)/shard_map/ppermute | solution.py:11
  28.7 11.2 %collective-permute-start.9 = (bf16[32,2304]{1,0:T(8,128)(2,1)S(1)}, bf16[32,2304]{1,0:T(8,128)(2,1)S(1)}, u32[]{:S(2)}, u32[]{:S(2)}) collective-permute-start(bf16[32,2304]{1,0:T(8,128)(2,1)S(1)} %slice.76), channel_id=1, source_target_pairs={{128,0},{256,128},{384,256},{0,384},{129,1},{257,129},{385,257},{1... | collective-permute-start | bytes 442376 | tf_op jit(solution)/shard_map/ppermute | solution.py:11
  33.3 13.3 %collective-permute-start.1 = (bf16[32,2304]{1,0:T(8,128)(2,1)S(1)}, bf16[32,2304]{1,0:T(8,128)(2,1)S(1)}, u32[]{:S(2)}, u32[]{:S(2)}) collective-permute-start(bf16[32,2304]{1,0:T(8,128)(2,1)S(1)} %slice.71), channel_id=1, source_target_pairs={{32,0},{64,32},{96,64},{0,96},{33,1},{65,33},{97,65},{1,97},{34,2}... | collective-permute-start | bytes 442376 | tf_op jit(solution)/shard_map/ppermute | solution.py:11
  37.9 8.7 %collective-permute-start.3 = (bf16[32,2304]{1,0:T(8,128)(2,1)S(1)}, bf16[32,2304]{1,0:T(8,128)(2,1)S(1)}, u32[]{:S(2)}, u32[]{:S(2)}) collective-permute-start(bf16[32,2304]{1,0:T(8,128)(2,1)S(1)} %slice.72), channel_id=1, source_target_pairs={{96,0},{0,32},{32,64},{64,96},{97,1},{1,33},{33,65},{65,97},{98,2}... | collective-permute-start | bytes 442376 | tf_op jit(solution)/shard_map/ppermute | solution.py:11
  40.1 26.6 %collective-permute-start.12 = (bf16[4,64,2304]{2,1,0:T(8,128)(2,1)S(1)}, bf16[4,64,2304]{2,1,0:T(8,128)(2,1)S(1)}, u32[]{:S(2)}, u32[]{:S(2)}) collective-permute-start(bf16[4,64,2304]{2,1,0:T(8,128)(2,1)S(1)} %get-tuple-element.9), channel_id=1, source_target_pairs={{32,0},{64,32},{96,64},{0,96},{33,1},{65,33},{97,65},{1,97},{34,2}... | collective-permute-start | bytes 3538952 | tf_op jit(solution)/shard_map/ppermute | solution.py:11
  44.7 26.4 %collective-permute-start.14 = (bf16[4,64,2304]{2,1,0:T(8,128)(2,1)S(1)}, bf16[4,64,2304]{2,1,0:T(8,128)(2,1)S(1)}, u32[]{:S(2)}, u32[]{:S(2)}) collective-permute-start(bf16[4,64,2304]{2,1,0:T(8,128)(2,1)S(1)} %get-tuple-element.9), channel_id=1, source_target_pairs={{96,0},{0,32},{32,64},{64,96},{97,1},{1,33},{33,65},{65,97},{98,2}... | collective-permute-start | bytes 3538952 | tf_op jit(solution)/shard_map/ppermute | solution.py:11
  46.9 28.0 %collective-permute-start.4 = (bf16[4,64,2304]{2,1,0:T(8,128)(2,1)S(1)}, bf16[4,64,2304]{2,1,0:T(8,128)(2,1)S(1)}, u32[]{:S(2)}, u32[]{:S(2)}) collective-permute-start(bf16[4,64,2304]{2,1,0:T(8,128)(2,1)S(1)} %get-tuple-element.11), channel_id=1, source_target_pairs={{128,0},{256,128},{384,256},{0,384},{129,1},{257,129},{385,257},{1... | collective-permute-start | bytes 3538952 | tf_op jit(solution)/shard_map/ppermute | solution.py:11
  49.0 30.1 %collective-permute-start.6 = (bf16[4,64,2304]{2,1,0:T(8,128)(2,1)S(1)}, bf16[4,64,2304]{2,1,0:T(8,128)(2,1)S(1)}, u32[]{:S(2)}, u32[]{:S(2)}) collective-permute-start(bf16[4,64,2304]{2,1,0:T(8,128)(2,1)S(1)} %get-tuple-element.11), channel_id=1, source_target_pairs={{384,0},{0,128},{128,256},{256,384},{385,1},{1,129},{129,257},{257... | collective-permute-start | bytes 3538952 | tf_op jit(solution)/shard_map/ppermute | solution.py:11
  67.6 16.5 %collective-permute-start.13 = (bf16[4,32,2304]{2,1,0:T(8,128)(2,1)}, bf16[4,32,2304]{2,1,0:T(8,128)(2,1)}, u32[]{:S(2)}, u32[]{:S(2)}) collective-permute-start(bf16[4,32,2304]{2,1,0:T(8,128)(2,1)} %slice.78), channel_id=1, source_target_pairs={{32,0},{64,32},{96,64},{0,96},{33,1},{65,33},{97,65},{1,97},{34,2}... | collective-permute-start | bytes 1769480 | tf_op jit(solution)/shard_map/ppermute | solution.py:11
  73.0 12.3 %collective-permute-start.15 = (bf16[4,32,2304]{2,1,0:T(8,128)(2,1)}, bf16[4,32,2304]{2,1,0:T(8,128)(2,1)}, u32[]{:S(2)}, u32[]{:S(2)}) collective-permute-start(bf16[4,32,2304]{2,1,0:T(8,128)(2,1)} %slice.79), channel_id=1, source_target_pairs={{96,0},{0,32},{32,64},{64,96},{97,1},{1,33},{33,65},{65,97},{98,2}... | collective-permute-start | bytes 1769480 | tf_op jit(solution)/shard_map/ppermute | solution.py:11
  74.9 1.1 copy-start.2
  76.8 11.2 %collective-permute-start.5 = (bf16[4,32,2304]{2,1,0:T(8,128)(2,1)}, bf16[4,32,2304]{2,1,0:T(8,128)(2,1)}, u32[]{:S(2)}, u32[]{:S(2)}) collective-permute-start(bf16[4,32,2304]{2,1,0:T(8,128)(2,1)} %slice.73), channel_id=1, source_target_pairs={{128,0},{256,128},{384,256},{0,384},{129,1},{257,129},{385,257},{1... | collective-permute-start | bytes 1769480 | tf_op jit(solution)/shard_map/ppermute | solution.py:11
  79.1 1.0 copy-start.4
  81.0 12.1 %collective-permute-start.7 = (bf16[4,32,2304]{2,1,0:T(8,128)(2,1)}, bf16[4,32,2304]{2,1,0:T(8,128)(2,1)}, u32[]{:S(2)}, u32[]{:S(2)}) collective-permute-start(bf16[4,32,2304]{2,1,0:T(8,128)(2,1)} %slice.74), channel_id=1, source_target_pairs={{384,0},{0,128},{128,256},{256,384},{385,1},{1,129},{129,257},{257... | collective-permute-start | bytes 1769480 | tf_op jit(solution)/shard_map/ppermute | solution.py:11
  84.2 10.3 %copy-start.1 = (bf16[4,64,2304]{2,1,0:T(8,128)(2,1)S(1)}, bf16[4,64,2304]{2,1,0:T(8,128)(2,1)}, u32[]{:S(2)}) copy-start(bf16[4,64,2304]{2,1,0:T(8,128)(2,1)} %copy-done) | copy-start | bytes 3538948
  94.5 2.5 copy-start.3
  94.5 2.5 copy-start.5
  97.0 10.9 %slice-start = ((s8[4718592]{0:T(1024)(128)(4,1)}), s8[524288]{0:T(1024)(128)(4,1)S(1)}, s32[]{:S(2)}) async-start(s8[4718592]{0:T(1024)(128)(4,1)} %bitcast.40), calls=%async_computation.4 | async-start | bytes 1048576
  99.5 8.4 %slice-start.2 = ((s8[4718592]{0:T(1024)(128)(4,1)}), s8[4194304]{0:T(1024)(128)(4,1)S(1)}, s32[]{:S(2)}) async-start(s8[4718592]{0:T(1024)(128)(4,1)} %bitcast.46), calls=%async_computation.6 | async-start | bytes 8388608
  99.5 8.5 %slice-start.4 = ((s8[4456448]{0:T(1024)(128)(4,1)}), s8[4194304]{0:T(1024)(128)(4,1)S(1)}, s32[]{:S(2)}) async-start(s8[4456448]{0:T(1024)(128)(4,1)} %bitcast.68), calls=%async_computation.8 | async-start | bytes 8388608
  100.7 7.2 %slice-start.1 = ((s8[4718592]{0:T(1024)(128)(4,1)}), s8[4194304]{0:T(1024)(128)(4,1)S(1)}, s32[]{:S(2)}) async-start(s8[4718592]{0:T(1024)(128)(4,1)} %bitcast.40), calls=%async_computation.5 | async-start | bytes 8388608
  100.7 7.2 %slice-start.3 = ((s8[4718592]{0:T(1024)(128)(4,1)}), s8[524288]{0:T(1024)(128)(4,1)S(1)}, s32[]{:S(2)}) async-start(s8[4718592]{0:T(1024)(128)(4,1)} %bitcast.46), calls=%async_computation.7 | async-start | bytes 1048576
  100.7 7.2 %slice-start.5 = ((s8[4456448]{0:T(1024)(128)(4,1)}), s8[262144]{0:T(1024)(128)(4,1)S(1)}, s32[]{:S(2)}) async-start(s8[4456448]{0:T(1024)(128)(4,1)} %bitcast.68), calls=%async_computation.9 | async-start | bytes 524288
  113.7 13.3 %collective-permute-start.16 = (bf16[512,2048]{1,0:T(8,128)(2,1)S(1)}, bf16[512,2048]{1,0:T(8,128)(2,1)S(1)}, u32[]{:S(2)}, u32[]{:S(2)}) collective-permute-start(bf16[512,2048]{1,0:T(8,128)(2,1)S(1)} %convolution_convert_fusion), channel_id=1, source_target_pairs={{0,1},{1,0},{2,3},{3,2},{4,5},{5,4},{6,7},{7,6},{8,9},{9,8},{10,11... | collective-permute-start | bytes 6291464 | tf_op jit(solution)/shard_map/ppermute | solution.py:100
  130.1 67.8 %copy-start.7 = (f32[32]{0:T(128)S(1)}, f32[32]{0:T(128)}, u32[]{:S(2)}) copy-start(f32[32]{0:T(128)} %param.10) | copy-start | bytes 388
  198.6 59.5 %copy-start.6 = (bf16[32,2048]{1,0:T(8,128)(2,1)}, bf16[32,2048]{1,0:T(8,128)(2,1)S(1)}, u32[]{:S(2)}) copy-start(bf16[32,2048]{1,0:T(8,128)(2,1)S(1)} %reshape.89) | copy-start | bytes 393220
  (1 other events, 1.0 us)
Sparse Core Ops, SparseCore 0:
  11.8 80.2 all-gather.2
  130.3 65.7 reduce-scatter.1

commit v5 on v4

v5 whole, which is shorter than its diff:
```python
import jax
import jax.numpy as jnp
from jax import lax
from jax.sharding import Mesh, PartitionSpec as P

BF = jnp.bfloat16
F32 = jnp.float32
HALF = jnp.float16


def to_half(value, lift):
    value = value.astype(F32)
    peak = jnp.max(jnp.abs(value), axis=1, keepdims=True)
    power = jnp.floor(jnp.log2(jnp.maximum(peak, 1e-30))) - lift
    return (value * jnp.exp2(-power)).astype(HALF), power


def local(tokens, routes, gates, curvature, w_gate, w_up, direction):
    rows, width = tokens.shape
    hidden_width = w_gate.shape[2]
    z_count, cores = lax.axis_size("z"), lax.axis_size("c")
    experts = z_count * cores
    core = lax.axis_index("c")
    me = lax.axis_index(("z", "c"))

    chosen = routes[:, :, None] == jnp.arange(experts, dtype=jnp.int32)
    table = jnp.sum(jnp.where(chosen, gates[:, :, None], 0.0), axis=1)
    table_high = table.astype(BF)
    table_low = (table - table_high.astype(F32)).astype(BF)
    sent = jnp.concatenate(
        [
            tokens,
            table_high,
            table_low,
            jnp.zeros((rows, 128 - 2 * experts), BF),
        ],
        1,
    )
    arrived = lax.all_gather(sent, ("z", "c"), axis=0, tiled=True)

    halves = [to_half(matrix[0], 13) for matrix in (w_gate, w_up, direction)]
    powers = jnp.concatenate([power for _, power in halves], 1)
    packed = jnp.concatenate(
        [half for half, _ in halves] + [jnp.pad(powers, ((0, 0), (0, 125))).astype(HALF)], 1
    )
    packed = lax.all_gather(packed, "x", axis=0, tiled=True)
    packed = lax.all_gather(packed, "y", axis=0, tiled=True)
    scales = jnp.exp2(packed[:, 3 * hidden_width :].astype(F32))

    def unpack(which):
        columns = packed[:, which * hidden_width : (which + 1) * hidden_width]
        return (columns.astype(F32) * scales[:, which : which + 1]).astype(BF)

    gate_matrix, up_matrix, back = lax.optimization_barrier(
        (unpack(0), unpack(1), unpack(2))
    )

    lanes = lax.broadcasted_iota(jnp.int32, (1, 128), 1)
    mine = (lanes == me) | (lanes == me + experts)
    share = jnp.sum(
        jnp.where(mine, arrived[:, width:].astype(F32), 0.0), axis=1, keepdims=True
    )
    group = arrived[:, :width]
    gate_pre = jnp.dot(group, gate_matrix, preferred_element_type=F32)
    up_pre = jnp.dot(group, up_matrix, preferred_element_type=F32)
    hidden = (jax.nn.silu(gate_pre) * up_pre * share).astype(BF)

    by_core = hidden.reshape(z_count, cores, rows, hidden_width)
    away = lax.dynamic_index_in_dim(by_core, 1 - core, 1, False).reshape(-1, hidden_width)
    home = lax.dynamic_index_in_dim(by_core, core, 1, False).reshape(-1, hidden_width)

    def tangent(part):
        return lax.dot_general(
            part, back, (((1,), (1,)), ((), ())), preferred_element_type=F32
        )

    other = lax.ppermute(tangent(away).astype(BF), "c", [(0, 1), (1, 0)])
    kept = lax.optimization_barrier(tangent(home))
    paired = (kept + other.astype(F32)).astype(BF)
    output_tangent = lax.psum_scatter(paired, "z", scatter_dimension=0, tiled=True)
    curved, power = to_half(curvature[:, None] * output_tangent.astype(F32), 13)
    scaled = jnp.concatenate(
        [curved, jnp.broadcast_to(power, (rows, 128)).astype(HALF)], 1
    )
    spread = lax.all_gather(scaled, ("z", "c"), axis=0, tiled=True)
    lifted = hidden.astype(F32) * jnp.exp2(spread[:, width : width + 1].astype(F32))
    part = lax.dot_general(
        spread[:, :width].astype(BF),
        lifted.astype(BF),
        (((0,), (0,)), ((), ())),
        preferred_element_type=F32,
    ).astype(BF)
    moved = lax.all_to_all(
        part.reshape(16, -1, hidden_width), ("y", "x"), 0, 0, tiled=True
    )
    product = jnp.sum(moved.astype(F32), axis=0).astype(BF)
    return output_tangent, product[None]


def solution(mesh):
    torus = Mesh(mesh.devices.reshape(4, 4, 16, 2), ("y", "x", "z", "c"))
    tokens = P(("y", "x", "z", "c"), None)
    matrix = P(("z", "c"), ("y", "x"), None)
    return jax.shard_map(
        local,
        mesh=torus,
        in_specs=(tokens, tokens, tokens, P(("y", "x", "z", "c")), matrix, matrix, matrix),
        out_specs=(tokens, matrix),
        check_vma=False,
    )
```

time: 312 us -> 335 us (1.074)
  blocking collectives: 100 us -> 207 us
  starting transfers between devices: 58.8 us -> 5.28 us
  waiting for transfers between devices: 91.9 us -> 67.7 us
  local copies, waits for them, and re-layouts: 12.2 us -> 5.98 us
    all_gather x0 -> x2, blocking collectives: none -> 107 us  [the longest x1 85.1 us: local(): packed = lax.all_gather(packed, 'y', axis=0, tiled=True)]
    ppermute x16 -> x0, starting transfers between devices: 49.2 us -> none  [fetch(): lax.ppermute(value, axis, [((i + shift) % size, i) for i in range(size)])]
    ppermute x16 -> x0, waiting for transfers between devices: 22.2 us -> none  [fetch(): lax.ppermute(value, axis, [((i + shift) % size, i) for i in range(size)])]
    convert_element_type x0 -> x6, other arithmetic: none -> 10.2 us  [the longest x4 4.14 us: to_half(): return ((value * jnp.exp2(-power)).astype(HALF), power)]
    another operation x9 -> x0, other arithmetic: 8.09 us -> none  [the longest x8 7.98 us: ring4(): return jnp.stack([value, after, jnp.concatenate([low, high], -2), before])]
    ppermute x1, starting transfers between devices: 9.5 us -> 5.2 us  [local(): other = lax.ppermute(tangent(away).astype(BF), 'c', [(0, 1), (1, 0)])]
    reduce_max x1 -> x4, other arithmetic: 0.5 us -> 4.24 us  [to_half(): peak = jnp.max(jnp.abs(value), axis=1, keepdims=True)]
  transfers between devices with their start and end apart: 19 -> 3, of which waited for: 6 -> 2; matrix products, arithmetic and copies ran while one was open for 4% -> 4% of each run, Pallas kernels for 0% -> 0%
where the time goes in v5:
time: 335 us
  blocking collectives  207 us (62%)
  waiting for transfers between devices  67.7 us (20%)
  matrix products  17.8 us (5%)
  other arithmetic  16.6 us (5%)
  between operations  14.3 us (4%)
  local copies, waits for them, and re-layouts  5.98 us (2%)
  starting transfers between devices  5.28 us (2%)
    all_gather x1, blocking collectives, local(): packed = lax.all_gather(packed, 'y', axis=0, tiled=True)  85.1 us
    reduce_scatter x1, waiting for transfers between devices, local(): lax.psum_scatter(paired, 'z', scatter_dimension=0, tiled=True)  65.7 us
    all_gather x1, blocking collectives, local(): spread = lax.all_gather(scaled, ('z', 'c'), axis=0, tiled=True)  54.4 us
    all_to_all x1, blocking collectives, local(): lax.all_to_all(part.reshape(16, -1, hidden_width), ('y', 'x'), 0, 0, tile...  45.6 us
    all_gather x1, blocking collectives, local(): packed = lax.all_gather(packed, 'x', axis=0, tiled=True)  21.8 us
  transfers between devices with their start and end apart: 3, of which 2 were waited for; matrix products, arithmetic and copies ran while one was open for 4% of the time, Pallas kernels for 0%

profile of v5, /device:TPU:1, one launch (start us, length us, event | category | flops | bytes accessed | tf_op | source)
XLA Modules:
  0.0 334.6 jit_solution(15974387684468855368)
XLA Ops:
  7.2 0.8 copy.15
  8.0 0.8 copy.16
  8.9 1.6 concatenate.13
  10.6 1.0 fusion.13
  11.7 1.0 fusion.15
  12.7 1.0 fusion.11
  14.0 1.0 fusion.14
  15.0 1.0 fusion.16
  16.1 1.0 fusion.12
  17.1 0.2 fusion.10
  17.3 21.8 %all-gather.6 = f16[512,2432]{1,0:T(8,128)(2,1)S(1)} all-gather(f16[128,2432]{1,0:T(8,128)(2,1)S(1)} %fusion.10), channel_id=1, replica_groups=mesh['y'=4,'x'=4,'z'=16,'c'=2] {'x'}, dimensions={0}, use_global_device_ids=true | all-gather | bytes 3112960 | tf_op jit(solution)/shard_map/all_gather | solution.py:46
  39.1 85.1 %all-gather.7 = f16[2048,2432]{1,0:T(8,128)(2,1)S(1)} all-gather(f16[512,2432]{1,0:T(8,128)(2,1)S(1)} %all-gather.6), channel_id=1, replica_groups=mesh['y'=4,'x'=4,'z'=16,'c'=2] {'y'}, dimensions={0}, use_global_device_ids=true | all-gather | bytes 12451840 | tf_op jit(solution)/shard_map/all_gather | solution.py:47
  124.2 0.2 multiply_exponential_fusion
  124.4 1.4 slice_reduce_fusion
  125.8 4.0 %multiply_convert_fusion = (bf16[2048,768]{1,0:T(8,128)(2,1)S(1)}, bf16[2048,768]{1,0:T(8,128)(2,1)}, bf16[2048,768]{1,0:T(8,128)(2,1)}) fusion(f16[2048,2432]{1,0:T(8,128)(2,1)S(1)} %all-gather.7, f32[2048]{0:T(1024)S(1)} %get-tuple-element.8, f32[2048]{0:T(1024)S(1)} %get-tuple-element.9, f32[2048]{0:T(1024)S(1)} %get-tuple-element.10), kind=kLoop, calls=%fused_computation | loop fusion | flops 14155776 | bytes 18898944 | tf_op jit(solution)/shard_map/convert_element_type | solution.py:52
  129.9 6.3 %fusion.1 = f32[1024,768]{1,0:T(8,128)S(1)} fusion(bf16[2048,768]{1,0:T(8,128)(2,1)} %get-tuple-element.6, bf16[1024,2176]{1,0:T(8,128)(2,1)} %all-gather.5.cloned.1.call-done), kind=kOutput, calls=%fused_computation.6 | convolution fusion | flops 3221225472 | bytes 10485760 | tf_op jit(solution)/shard_map/dot_general | solution.py:65
  136.2 0.1 select_reduce_fusion
  136.3 3.7 %multiply_convert_fusion.4 = bf16[1024,768]{1,0:T(8,128)(2,1)S(1)} fusion(f32[1024,768]{1,0:T(8,128)S(1)} %fusion.1, bf16[2048,768]{1,0:T(8,128)(2,1)S(1)} %copy-done, bf16[1024,2176]{1,0:T(8,128)(2,1)S(1)} %copy-done.3, f32[1024]{0:T(1024)S(1)} %select_reduce_fusion), kind=kOutput, calls=%fused_computation.12 | convolution fusion | flops 3226730496 | bytes 12062720 | tf_op jit(solution)/shard_map/dot_general | solution.py:64
  140.2 1.0 copy-done.1
  141.2 1.8 convolution_convert_fusion
  143.1 5.2 %collective-permute-start = (bf16[512,2048]{1,0:T(8,128)(2,1)S(1)}, bf16[512,2048]{1,0:T(8,128)(2,1)S(1)}, u32[]{:S(2)}, u32[]{:S(2)}) collective-permute-start(bf16[512,2048]{1,0:T(8,128)(2,1)S(1)} %convolution_convert_fusion), channel_id=1, source_target_pairs={{0,1},{1,0},{2,3},{3,2},{4,5},{5,4},{6,7},{7,6},{8,9},{9,8},{10,11... | collective-permute-start | bytes 6291464 | tf_op jit(solution)/shard_map/ppermute | solution.py:77
  148.3 1.8 fusion.18
  150.1 1.9 collective-permute-done
  152.0 2.1 add_convert_fusion
  154.2 65.7 %reduce-scatter.2.cloned.1.call-done = bf16[32,2048]{1,0:T(8,128)(2,1)} async-done(((bf16[512,2048]{1,0:T(8,128)(2,1)}), bf16[32,2048]{1,0:T(8,128)(2,1)}) %reduce-scatter.2.cloned.1.call-update) | async-done | bytes 131088 | tf_op jit(solution)/shard_map/reduce_scatter | solution.py:80
  219.9 1.1 abs_reduce_fusion
  221.0 1.0 multiply_convert_fusion.6
  222.2 54.4 %all-gather.8 = f16[1024,2176]{1,0:T(8,128)(2,1)S(1)} all-gather(f16[32,2176]{1,0:T(8,128)(2,1)S(1)} %pad_maximum_fusion), channel_id=1, replica_groups=mesh['y'=4,'x'=4,'z'=16,'c'=2] {'z','c'}, dimensions={0}, use_global_device_ids=true | all-gather | bytes 4595712 | tf_op jit(solution)/shard_map/all_gather | solution.py:85
  276.6 0.2 exponential_reduce_fusion
  276.8 4.2 %fusion.5 = bf16[2048,768]{1,0:T(8,128)(2,1)S(1)} fusion(f16[1024,2176]{1,0:T(8,128)(2,1)S(1)} %all-gather.8, bf16[1024,768]{1,0:T(8,128)(2,1)S(1)} %copy-done.2, f32[1024]{0:T(1024)S(1)} %exponential_reduce_fusion), kind=kOutput, calls=%fused_computation.10 | convolution fusion | flops 3227254784 | bytes 8916992 | tf_op jit(solution)/shard_map/dot_general | solution.py:87
  281.0 45.6 %all_to_all.5 = bf16[16,128,768]{2,1,0:T(8,128)(2,1)S(1)} all-to-all(bf16[16,128,768]{2,1,0:T(8,128)(2,1)S(1)} %bitcast.29), channel_id=1, replica_groups=mesh['y'=4,'x'=4,'z'=16,'c'=2] {'y','x'}, dimensions={0} | all-to-all | bytes 6291456 | tf_op jit(solution)/shard_map/all_to_all | solution.py:93
  326.7 1.1 reduce_sum.32
  (26 shorter events, 0.7 us)
Async XLA Ops:
  7.2 122.7 %all-gather.5.cloned.1.call-start = ((), (), s32[]{:S(2)}) async-start(), calls=%async_computation.2 | async-start | bytes 4595712 | tf_op jit(solution)/shard_map/all_gather | solution.py:39
  10.6 209.3 %reduce-scatter.2.cloned.1.call-start = ((), (), s32[]{:S(2)}) async-start(), calls=%async_computation.3 | async-start | bytes 2228224 | tf_op jit(solution)/shard_map/reduce_scatter | solution.py:80
  129.9 6.3 %copy-start.3 = (bf16[1024,2176]{1,0:T(8,128)(2,1)S(1)}, bf16[1024,2176]{1,0:T(8,128)(2,1)}, u32[]{:S(2)}) copy-start(bf16[1024,2176]{1,0:T(8,128)(2,1)} %all-gather.5.cloned.1.call-done) | copy-start | bytes 13369348
  129.9 6.5 %copy-start = (bf16[2048,768]{1,0:T(8,128)(2,1)S(1)}, bf16[2048,768]{1,0:T(8,128)(2,1)}, u32[]{:S(2)}) copy-start(bf16[2048,768]{1,0:T(8,128)(2,1)} %get-tuple-element.5) | copy-start | bytes 9437188
  140.1 1.2 copy-start.1
  143.1 9.0 %collective-permute-start = (bf16[512,2048]{1,0:T(8,128)(2,1)S(1)}, bf16[512,2048]{1,0:T(8,128)(2,1)S(1)}, u32[]{:S(2)}, u32[]{:S(2)}) collective-permute-start(bf16[512,2048]{1,0:T(8,128)(2,1)S(1)} %convolution_convert_fusion), channel_id=1, source_target_pairs={{0,1},{1,0},{2,3},{3,2},{4,5},{5,4},{6,7},{7,6},{8,9},{9,8},{10,11... | collective-permute-start | bytes 6291464 | tf_op jit(solution)/shard_map/ppermute | solution.py:77
  150.1 69.8 %copy-start.4 = (f32[32]{0:T(128)S(1)}, f32[32]{0:T(128)}, u32[]{:S(2)}) copy-start(f32[32]{0:T(128)} %param.10) | copy-start | bytes 388
  154.2 122.7 %copy-start.2 = (bf16[1024,768]{1,0:T(8,128)(2,1)S(1)}, bf16[1024,768]{1,0:T(8,128)(2,1)}, u32[]{:S(2)}) copy-start(bf16[1024,768]{1,0:T(8,128)(2,1)} %copy-done.1) | copy-start | bytes 4718596
Sparse Core Ops, SparseCore 0:
  10.7 79.8 all-gather.4
  154.3 65.5 reduce-scatter.1

commit v6 on v4

--- a/solution.py
+++ b/solution.py
@@ -17,7 +17,12 @@
     before = fetch(value, axis, -1, 4)
     low = fetch(after[..., :half, :], axis, 1, 4)
     high = fetch(before[..., half:, :], axis, -1, 4)
-    return jnp.stack([value, after, jnp.concatenate([low, high], -2), before])
+    return [value, after, before], [low, high]
+
+
+def ring4_stack(value, axis):
+    soon, late = ring4(value, axis)
+    return jnp.stack([soon[0], soon[1], jnp.concatenate(late, -2), soon[2]])
 
 
 def turn(value, axis, start):
@@ -29,16 +34,22 @@
     rows, width = value.shape
     value = turn(turn(value.reshape(rows, 4, 4, width // 16), 1, y), 2, x)
     first, second = jnp.split(value, 2, axis=3)
-    second = second.swapaxes(1, 2)
-    return jnp.concatenate([first.reshape(rows, -1), second.reshape(rows, -1)], 1)
+    pieces = []
+    for part in (first, second.swapaxes(1, 2)):
+        pieces += [part[:, :2], part[:, 3:]]
+    pieces += [first[:, 2:3], second.swapaxes(1, 2)[:, 2:3]]
+    return jnp.concatenate([piece.reshape(rows, -1) for piece in pieces], 1)
 
 
 def to_absolute(value, y, x):
     rows, width = value.shape
-    first, second = jnp.split(value, 2, axis=1)
-    first = first.reshape(rows, 4, 4, width // 32)
-    second = second.reshape(rows, 4, 4, width // 32).swapaxes(1, 2)
-    both = jnp.concatenate([first, second], 3)
+    unit = width // 8
+    a, b, c, d, e, f = jnp.split(
+        value, [2 * unit, 3 * unit, 5 * unit, 6 * unit, 7 * unit], axis=1
+    )
+    first = jnp.concatenate([a, e, b], 1).reshape(rows, 4, 4, width // 32)
+    second = jnp.concatenate([c, f, d], 1).reshape(rows, 4, 4, width // 32)
+    both = jnp.concatenate([first, second.swapaxes(1, 2)], 3)
     return turn(turn(both, 1, (4 - y) % 4), 2, (4 - x) % 4).reshape(rows, width)
 
 
@@ -67,11 +78,10 @@
 
     stacked = jnp.concatenate([w_gate[0], w_up[0], direction[0]], 1)
     half = stacked.shape[0] // 2
-    first = ring4(ring4(stacked[:half], "x"), "y")
-    second = ring4(ring4(stacked[half:], "y"), "x")
-    weights = jnp.concatenate(
-        [first.reshape(width // 2, -1), second.reshape(width // 2, -1)], 0
-    )
+    first_soon, first_late = ring4(ring4_stack(stacked[:half], "x"), "y")
+    second_soon, second_late = ring4(ring4_stack(stacked[half:], "y"), "x")
+    columns = stacked.shape[1]
+    soon = jnp.concatenate([p.reshape(-1, columns) for p in first_soon + second_soon])
 
     lanes = lax.broadcasted_iota(jnp.int32, (1, 128), 1)
     mine = (lanes == me) | (lanes == me + experts)
@@ -79,10 +89,26 @@
         jnp.where(mine, arrived[:, width:].astype(F32), 0.0), axis=1, keepdims=True
     )
     group = arrived[:, :width]
-    gate_pre = jnp.dot(group, weights[:, :hidden_width], preferred_element_type=F32)
-    up_pre = jnp.dot(
-        group, weights[:, hidden_width : 2 * hidden_width], preferred_element_type=F32
+    early = soon.shape[0]
+
+    def times(left, right, which):
+        right = right[:, which * hidden_width : (which + 1) * hidden_width]
+        return jnp.dot(left, right, preferred_element_type=F32)
+
+    gate_soon = times(group[:, :early], soon, 0)
+    up_soon = times(group[:, :early], soon, 1)
+    low_1, high_1, low_2, high_2, gate_soon, up_soon = lax.optimization_barrier(
+        (*first_late, *second_late, gate_soon, up_soon)
     )
+    late = jnp.concatenate(
+        [
+            jnp.concatenate(pair, -2).reshape(-1, columns)
+            for pair in ((low_1, high_1), (low_2, high_2))
+        ]
+    )
+    back = jnp.concatenate([soon[:, 2 * hidden_width :], late[:, 2 * hidden_width :]])
+    gate_pre = gate_soon + times(group[:, early:], late, 0)
+    up_pre = up_soon + times(group[:, early:], late, 1)
     hidden = (jax.nn.silu(gate_pre) * up_pre * share).astype(BF)
 
     by_core = hidden.reshape(z_count, cores, rows, hidden_width)
@@ -91,14 +117,12 @@
 
     def tangent(part):
         return lax.dot_general(
-            part,
-            weights[:, 2 * hidden_width :],
-            (((1,), (1,)), ((), ())),
-            preferred_element_type=F32,
+            part, back, (((1,), (1,)), ((), ())), preferred_element_type=F32
         )
 
     other = lax.ppermute(tangent(away).astype(BF), "c", [(0, 1), (1, 0)])
-    paired = (tangent(home) + other.astype(F32)).astype(BF)
+    kept = lax.optimization_barrier(tangent(home))
+    paired = (kept + other.astype(F32)).astype(BF)
     jv = lax.psum_scatter(paired, "z", scatter_dimension=0, tiled=True)
     output_tangent = to_absolute(jv, y, x)
     curved = curvature[:, None] * output_tangent.astype(F32)

time: 312 us -> 310 us (level)
  local copies, waits for them, and re-layouts: 12.2 us -> 23.1 us
  waiting for transfers between devices: 91.9 us -> 82.8 us
  other arithmetic: 13.7 us -> 8.48 us
    ppermute x16, waiting for transfers between devices: 22.2 us -> 14.5 us  [fetch(): lax.ppermute(value, axis, [((i + shift) % size, i) for i in range(size)])]
    another operation x9 -> x5, other arithmetic: 8.09 us -> 0.45 us  [the longest x4 0.34 us: ring4_stack(): return jnp.stack([soon[0], soon[1], jnp.concatenate(late, -2), soon[2]])]
    unnamed x30 -> x23, local copies, waits for them, and re-layouts: 4.7 us -> 8.88 us
    dot_general x4 -> x6, matrix products: 15.9 us -> 17.6 us  [the longest x4 11.6 us: times(): return jnp.dot(left, right, preferred_element_type=F32)]
  transfers between devices with their start and end apart: 19 -> 19, of which waited for: 6 -> 4; matrix products, arithmetic and copies ran while one was open for 4% -> 8% of each run, Pallas kernels for 0% -> 0%
where the time goes in v6:
time: 310 us; the launch traced here: 308 us
  blocking collectives  99.9 us (32%)
  waiting for transfers between devices  82.8 us (27%)
  starting transfers between devices  57.6 us (19%)
  local copies, waits for them, and re-layouts  23.1 us (7%)
  matrix products  21.8 us (7%)
  between operations  14.8 us (5%)
  other arithmetic  8.48 us (3%)
    reduce_scatter x1, waiting for transfers between devices, local(): jv = lax.psum_scatter(paired, 'z', scatter_dimension=0, tiled=True)  65.6 us
    all_gather x1, blocking collectives, local(): spread = lax.all_gather(scaled, ('z', 'c'), axis=0, tiled=True)  54.2 us
    ppermute x16, starting transfers between devices, fetch(): lax.ppermute(value, axis, [((i + shift) % size, i) for i in range(size)])  49.4 us
    all_to_all x1, blocking collectives, local(): lax.all_to_all(part.reshape(16, -1, hidden_width), ('y', 'x'), 0, 0, tile...  45.7 us
    ppermute x16, waiting for transfers between devices, fetch(): lax.ppermute(value, axis, [((i + shift) % size, i) for i in range(size)])  14.5 us
    dot_general x4, matrix products, times(): return jnp.dot(left, right, preferred_element_type=F32)  11.6 us
    unnamed x23, local copies, waits for them, and re-layouts  8.88 us
    ppermute x1, starting transfers between devices, local(): other = lax.ppermute(tangent(away).astype(BF), 'c', [(0, 1), (1, 0)])  8.12 us
  transfers between devices with their start and end apart: 19, of which 4 were waited for; matrix products, arithmetic and copies ran while one was open for 8% of the time, Pallas kernels for 0%

profile of v6, /device:TPU:1, one launch (start us, length us, event | category | flops | bytes accessed | tf_op | source)
XLA Modules:
  0.0 308.5 jit_solution(8237579307963218192)
XLA Ops:
  12.8 4.0 %collective-permute-start.10 = (bf16[64,2304]{1,0:T(8,128)(2,1)S(1)}, bf16[64,2304]{1,0:T(8,128)(2,1)S(1)}, u32[]{:S(2)}, u32[]{:S(2)}) collective-permute-start(bf16[64,2304]{1,0:T(8,128)(2,1)S(1)} %get-tuple-element.22), channel_id=1, source_target_pairs={{384,0},{0,128},{128,256},{256,384},{385,1},{1,129},{129,257},{257... | collective-permute-start | bytes 884744 | tf_op jit(solution)/shard_map/ppermute | solution.py:11
  16.8 3.4 %collective-permute-start.8 = (bf16[64,2304]{1,0:T(8,128)(2,1)S(1)}, bf16[64,2304]{1,0:T(8,128)(2,1)S(1)}, u32[]{:S(2)}, u32[]{:S(2)}) collective-permute-start(bf16[64,2304]{1,0:T(8,128)(2,1)S(1)} %get-tuple-element.22), channel_id=1, source_target_pairs={{128,0},{256,128},{384,256},{0,384},{129,1},{257,129},{385,257},{1... | collective-permute-start | bytes 884744 | tf_op jit(solution)/shard_map/ppermute | solution.py:11
  20.2 4.4 %collective-permute-start = (bf16[64,2304]{1,0:T(8,128)(2,1)S(1)}, bf16[64,2304]{1,0:T(8,128)(2,1)S(1)}, u32[]{:S(2)}, u32[]{:S(2)}) collective-permute-start(bf16[64,2304]{1,0:T(8,128)(2,1)S(1)} %get-tuple-element.23), channel_id=1, source_target_pairs={{32,0},{64,32},{96,64},{0,96},{33,1},{65,33},{97,65},{1,97},{34,2}... | collective-permute-start | bytes 884744 | tf_op jit(solution)/shard_map/ppermute | solution.py:11
  24.6 1.9 collective-permute-start.2
  26.5 1.9 collective-permute-start.11
  28.5 4.6 %collective-permute-start.9 = (bf16[32,2304]{1,0:T(8,128)(2,1)S(1)}, bf16[32,2304]{1,0:T(8,128)(2,1)S(1)}, u32[]{:S(2)}, u32[]{:S(2)}) collective-permute-start(bf16[32,2304]{1,0:T(8,128)(2,1)S(1)} %slice.122), channel_id=1, source_target_pairs={{128,0},{256,128},{384,256},{0,384},{129,1},{257,129},{385,257},{1... | collective-permute-start | bytes 442376 | tf_op jit(solution)/shard_map/ppermute | solution.py:11
  33.1 4.6 %collective-permute-start.1 = (bf16[32,2304]{1,0:T(8,128)(2,1)S(1)}, bf16[32,2304]{1,0:T(8,128)(2,1)S(1)}, u32[]{:S(2)}, u32[]{:S(2)}) collective-permute-start(bf16[32,2304]{1,0:T(8,128)(2,1)S(1)} %slice.117), channel_id=1, source_target_pairs={{32,0},{64,32},{96,64},{0,96},{33,1},{65,33},{97,65},{1,97},{34,2}... | collective-permute-start | bytes 442376 | tf_op jit(solution)/shard_map/ppermute | solution.py:11
  37.7 1.9 collective-permute-start.3
  39.8 4.6 %collective-permute-start.12 = (bf16[4,64,2304]{2,1,0:T(8,128)(2,1)S(1)}, bf16[4,64,2304]{2,1,0:T(8,128)(2,1)S(1)}, u32[]{:S(2)}, u32[]{:S(2)}) collective-permute-start(bf16[4,64,2304]{2,1,0:T(8,128)(2,1)S(1)} %pad_maximum_fusion.2), channel_id=1, source_target_pairs={{32,0},{64,32},{96,64},{0,96},{33,1},{65,33},{97,65},{1,97},{34,2}... | collective-permute-start | bytes 3538952 | tf_op jit(solution)/shard_map/ppermute | solution.py:11
  44.4 1.9 collective-permute-start.14
  46.6 2.2 collective-permute-start.4
  48.7 3.1 %collective-permute-start.6 = (bf16[4,64,2304]{2,1,0:T(8,128)(2,1)S(1)}, bf16[4,64,2304]{2,1,0:T(8,128)(2,1)}, u32[]{:S(2)}, u32[]{:S(2)}) collective-permute-start(bf16[4,64,2304]{2,1,0:T(8,128)(2,1)S(1)} %pad_maximum_fusion.1), channel_id=1, source_target_pairs={{384,0},{0,128},{128,256},{256,384},{385,1},{1,129},{129,257},{257... | collective-permute-start | bytes 3538952 | tf_op jit(solution)/shard_map/ppermute | solution.py:11
  52.0 14.5 %collective-permute-done.12 = bf16[4,64,2304]{2,1,0:T(8,128)(2,1)S(1)} collective-permute-done((bf16[4,64,2304]{2,1,0:T(8,128)(2,1)S(1)}, bf16[4,64,2304]{2,1,0:T(8,128)(2,1)S(1)}, u32[]{:S(2)}, u32[]{:S(2)}) %collective-permute-start.12) | collective-permute-done | bytes 1179680 | tf_op jit(solution)/shard_map/ppermute | solution.py:11
  67.4 3.5 %collective-permute-start.13 = (bf16[4,32,2304]{2,1,0:T(8,128)(2,1)}, bf16[4,32,2304]{2,1,0:T(8,128)(2,1)}, u32[]{:S(2)}, u32[]{:S(2)}) collective-permute-start(bf16[4,32,2304]{2,1,0:T(8,128)(2,1)} %slice.124), channel_id=1, source_target_pairs={{32,0},{64,32},{96,64},{0,96},{33,1},{65,33},{97,65},{1,97},{34,2}... | collective-permute-start | bytes 1769480 | tf_op jit(solution)/shard_map/ppermute | solution.py:11
  70.9 1.9 slice.125
  72.8 1.9 collective-permute-start.15
  74.8 2.0 slice.119
  76.7 2.2 collective-permute-start.5
  80.1 3.2 %collective-permute-start.7 = (bf16[4,32,2304]{2,1,0:T(8,128)(2,1)S(1)}, bf16[4,32,2304]{2,1,0:T(8,128)(2,1)S(1)}, u32[]{:S(2)}, u32[]{:S(2)}) collective-permute-start(bf16[4,32,2304]{2,1,0:T(8,128)(2,1)S(1)} %slice.120), channel_id=1, source_target_pairs={{384,0},{0,128},{128,256},{256,384},{385,1},{1,129},{129,257},{257... | collective-permute-start | bytes 1769480 | tf_op jit(solution)/shard_map/ppermute | solution.py:11
  87.5 2.9 copy-done.2
  90.4 1.6 slice.141
  93.0 5.4 %fusion.3 = f32[1024,768]{1,0:T(8,128)S(1)} fusion(bf16[1024,2176]{1,0:T(8,128)(2,1)} %all-gather.3.cloned.1.call-done, bf16[1536,2304]{1,0:T(8,128)(2,1)} %copy-done.2), kind=kOutput, calls=%fused_computation.9 | convolution fusion | flops 2415919104 | bytes 8650752 | tf_op jit(solution)/shard_map/dot_general | solution.py:96
  98.3 4.3 %fusion.5 = f32[1024,768]{1,0:T(8,128)S(1)} fusion(bf16[1024,2176]{1,0:T(8,128)(2,1)S(1)} %copy-done, bf16[1536,2304]{1,0:T(8,128)(2,1)} %copy-done.2), kind=kOutput, calls=%fused_computation.11 | convolution fusion | flops 2415919104 | bytes 8650752 | tf_op jit(solution)/shard_map/dot_general | solution.py:96
  109.0 4.2 %convolution_convert_fusion = bf16[512,2048]{1,0:T(8,128)(2,1)S(1)} fusion(bf16[512,768]{1,0:T(8,128)(2,1)S(1)} %bitcast.55, bf16[256,2304]{1,0:T(8,128)(2,1)S(1)} %bitcast.47, bf16[256,2304]{1,0:T(8,128)(2,1)S(1)} %bitcast.43, bf16[1536,768]{1,0:T(8,128)(2,1)S(1)} %copy-done.1), kind=kOutput, calls=%fused_computation.8 | convolution fusion | flops 1621098496 | bytes 7602176 | tf_op jit(solution)/shard_map/dot_general | solution.py:119
  113.3 8.1 %collective-permute-start.16 = (bf16[512,2048]{1,0:T(8,128)(2,1)S(1)}, bf16[512,2048]{1,0:T(8,128)(2,1)S(1)}, u32[]{:S(2)}, u32[]{:S(2)}) collective-permute-start(bf16[512,2048]{1,0:T(8,128)(2,1)S(1)} %convolution_convert_fusion), channel_id=1, source_target_pairs={{0,1},{1,0},{2,3},{3,2},{4,5},{5,4},{6,7},{7,6},{8,9},{9,8},{10,11... | collective-permute-start | bytes 6291464 | tf_op jit(solution)/shard_map/ppermute | solution.py:123
  121.4 1.8 fusion.19
  123.2 1.7 collective-permute-done.16
  124.9 2.1 add_convert_fusion
  127.1 65.6 %reduce-scatter.2.cloned.1.call-done = bf16[32,2048]{1,0:T(8,128)(2,1)} async-done(((bf16[512,2048]{1,0:T(8,128)(2,1)}), bf16[32,2048]{1,0:T(8,128)(2,1)}) %reduce-scatter.2.cloned.1.call-update) | async-done | bytes 131088 | tf_op jit(solution)/shard_map/reduce_scatter | solution.py:126
  196.2 54.2 %all-gather.4 = f16[1024,2176]{1,0:T(8,128)(2,1)S(1)} all-gather(f16[32,2176]{1,0:T(8,128)(2,1)S(1)} %pad_maximum_fusion.6), channel_id=1, replica_groups=mesh['y'=4,'x'=4,'z'=16,'c'=2] {'z','c'}, dimensions={0}, use_global_device_ids=true | all-gather | bytes 4595712 | tf_op jit(solution)/shard_map/all_gather | solution.py:134
  250.6 4.2 %fusion.1 = bf16[2048,768]{1,0:T(8,128)(2,1)S(1)} fusion(f16[1024,2176]{1,0:T(8,128)(2,1)S(1)} %all-gather.4, bf16[1024,768]{1,0:T(8,128)(2,1)S(1)} %multiply_convert_fusion.1, f32[1024]{0:T(1024)S(1)} %exponential_reduce_fusion), kind=kOutput, calls=%fused_computation.3 | convolution fusion | flops 3227254784 | bytes 8916992 | tf_op jit(solution)/shard_map/dot_general | solution.py:136
  254.8 45.7 %all_to_all.5 = bf16[16,128,768]{2,1,0:T(8,128)(2,1)S(1)} all-to-all(bf16[16,128,768]{2,1,0:T(8,128)(2,1)S(1)} %bitcast.52), channel_id=1, replica_groups=mesh['y'=4,'x'=4,'z'=16,'c'=2] {'y','x'}, dimensions={0} | all-to-all | bytes 6291456 | tf_op jit(solution)/shard_map/all_to_all | solution.py:142
  (102 shorter events, 24.2 us)
Async XLA Ops:
  7.2 5.4 %copy-start.6 = (bf16[1,128,768]{2,1,0:T(8,128)(2,1)S(1)}, bf16[1,128,768]{2,1,0:T(8,128)(2,1)}, u32[]{:S(2)}) copy-start(bf16[1,128,768]{2,1,0:T(8,128)(2,1)} %param.11) | copy-start | bytes 589828
  7.2 5.4 %copy-start.5 = (bf16[1,128,768]{2,1,0:T(8,128)(2,1)S(1)}, bf16[1,128,768]{2,1,0:T(8,128)(2,1)}, u32[]{:S(2)}) copy-start(bf16[1,128,768]{2,1,0:T(8,128)(2,1)} %param.12) | copy-start | bytes 589828
  7.2 5.4 %copy-start.4 = (bf16[1,128,768]{2,1,0:T(8,128)(2,1)S(1)}, bf16[1,128,768]{2,1,0:T(8,128)(2,1)}, u32[]{:S(2)}) copy-start(bf16[1,128,768]{2,1,0:T(8,128)(2,1)} %param.13) | copy-start | bytes 589828
  7.2 85.8 %all-gather.3.cloned.1.call-start = ((), (), s32[]{:S(2)}) async-start(), calls=%async_computation.2 | async-start | bytes 4595712 | tf_op jit(solution)/shard_map/all_gather | solution.py:77
  12.6 180.1 %reduce-scatter.2.cloned.1.call-start = ((), (), s32[]{:S(2)}) async-start(), calls=%async_computation.3 | async-start | bytes 2228224 | tf_op jit(solution)/shard_map/reduce_scatter | solution.py:126
  12.8 13.7 %collective-permute-start.10 = (bf16[64,2304]{1,0:T(8,128)(2,1)S(1)}, bf16[64,2304]{1,0:T(8,128)(2,1)S(1)}, u32[]{:S(2)}, u32[]{:S(2)}) collective-permute-start(bf16[64,2304]{1,0:T(8,128)(2,1)S(1)} %get-tuple-element.22), channel_id=1, source_target_pairs={{384,0},{0,128},{128,256},{256,384},{385,1},{1,129},{129,257},{257... | collective-permute-start | bytes 884744 | tf_op jit(solution)/shard_map/ppermute | solution.py:11
  16.8 11.7 %collective-permute-start.8 = (bf16[64,2304]{1,0:T(8,128)(2,1)S(1)}, bf16[64,2304]{1,0:T(8,128)(2,1)S(1)}, u32[]{:S(2)}, u32[]{:S(2)}) collective-permute-start(bf16[64,2304]{1,0:T(8,128)(2,1)S(1)} %get-tuple-element.22), channel_id=1, source_target_pairs={{128,0},{256,128},{384,256},{0,384},{129,1},{257,129},{385,257},{1... | collective-permute-start | bytes 884744 | tf_op jit(solution)/shard_map/ppermute | solution.py:11
  20.2 12.9 %collective-permute-start = (bf16[64,2304]{1,0:T(8,128)(2,1)S(1)}, bf16[64,2304]{1,0:T(8,128)(2,1)S(1)}, u32[]{:S(2)}, u32[]{:S(2)}) collective-permute-start(bf16[64,2304]{1,0:T(8,128)(2,1)S(1)} %get-tuple-element.23), channel_id=1, source_target_pairs={{32,0},{64,32},{96,64},{0,96},{33,1},{65,33},{97,65},{1,97},{34,2}... | collective-permute-start | bytes 884744 | tf_op jit(solution)/shard_map/ppermute | solution.py:11
  24.6 13.1 %collective-permute-start.2 = (bf16[64,2304]{1,0:T(8,128)(2,1)S(1)}, bf16[64,2304]{1,0:T(8,128)(2,1)S(1)}, u32[]{:S(2)}, u32[]{:S(2)}) collective-permute-start(bf16[64,2304]{1,0:T(8,128)(2,1)S(1)} %get-tuple-element.23), channel_id=1, source_target_pairs={{96,0},{0,32},{32,64},{64,96},{97,1},{1,33},{33,65},{65,97},{98,2}... | collective-permute-start | bytes 884744 | tf_op jit(solution)/shard_map/ppermute | solution.py:11
  26.5 13.1 %collective-permute-start.11 = (bf16[32,2304]{1,0:T(8,128)(2,1)S(1)}, bf16[32,2304]{1,0:T(8,128)(2,1)S(1)}, u32[]{:S(2)}, u32[]{:S(2)}) collective-permute-start(bf16[32,2304]{1,0:T(8,128)(2,1)S(1)} %slice.123), channel_id=1, source_target_pairs={{384,0},{0,128},{128,256},{256,384},{385,1},{1,129},{129,257},{257... | collective-permute-start | bytes 442376 | tf_op jit(solution)/shard_map/ppermute | solution.py:11
  28.5 11.2 %collective-permute-start.9 = (bf16[32,2304]{1,0:T(8,128)(2,1)S(1)}, bf16[32,2304]{1,0:T(8,128)(2,1)S(1)}, u32[]{:S(2)}, u32[]{:S(2)}) collective-permute-start(bf16[32,2304]{1,0:T(8,128)(2,1)S(1)} %slice.122), channel_id=1, source_target_pairs={{128,0},{256,128},{384,256},{0,384},{129,1},{257,129},{385,257},{1... | collective-permute-start | bytes 442376 | tf_op jit(solution)/shard_map/ppermute | solution.py:11
  33.1 13.3 %collective-permute-start.1 = (bf16[32,2304]{1,0:T(8,128)(2,1)S(1)}, bf16[32,2304]{1,0:T(8,128)(2,1)S(1)}, u32[]{:S(2)}, u32[]{:S(2)}) collective-permute-start(bf16[32,2304]{1,0:T(8,128)(2,1)S(1)} %slice.117), channel_id=1, source_target_pairs={{32,0},{64,32},{96,64},{0,96},{33,1},{65,33},{97,65},{1,97},{34,2}... | collective-permute-start | bytes 442376 | tf_op jit(solution)/shard_map/ppermute | solution.py:11
  37.7 8.7 %collective-permute-start.3 = (bf16[32,2304]{1,0:T(8,128)(2,1)S(1)}, bf16[32,2304]{1,0:T(8,128)(2,1)S(1)}, u32[]{:S(2)}, u32[]{:S(2)}) collective-permute-start(bf16[32,2304]{1,0:T(8,128)(2,1)S(1)} %slice.118), channel_id=1, source_target_pairs={{96,0},{0,32},{32,64},{64,96},{97,1},{1,33},{33,65},{65,97},{98,2}... | collective-permute-start | bytes 442376 | tf_op jit(solution)/shard_map/ppermute | solution.py:11
  39.8 26.6 %collective-permute-start.12 = (bf16[4,64,2304]{2,1,0:T(8,128)(2,1)S(1)}, bf16[4,64,2304]{2,1,0:T(8,128)(2,1)S(1)}, u32[]{:S(2)}, u32[]{:S(2)}) collective-permute-start(bf16[4,64,2304]{2,1,0:T(8,128)(2,1)S(1)} %pad_maximum_fusion.2), channel_id=1, source_target_pairs={{32,0},{64,32},{96,64},{0,96},{33,1},{65,33},{97,65},{1,97},{34,2}... | collective-permute-start | bytes 3538952 | tf_op jit(solution)/shard_map/ppermute | solution.py:11
  44.4 26.5 %collective-permute-start.14 = (bf16[4,64,2304]{2,1,0:T(8,128)(2,1)S(1)}, bf16[4,64,2304]{2,1,0:T(8,128)(2,1)}, u32[]{:S(2)}, u32[]{:S(2)}) collective-permute-start(bf16[4,64,2304]{2,1,0:T(8,128)(2,1)S(1)} %pad_maximum_fusion.2), channel_id=1, source_target_pairs={{96,0},{0,32},{32,64},{64,96},{97,1},{1,33},{33,65},{65,97},{98,2}... | collective-permute-start | bytes 3538952 | tf_op jit(solution)/shard_map/ppermute | solution.py:11
  46.6 28.2 %collective-permute-start.4 = (bf16[4,64,2304]{2,1,0:T(8,128)(2,1)S(1)}, bf16[4,64,2304]{2,1,0:T(8,128)(2,1)}, u32[]{:S(2)}, u32[]{:S(2)}) collective-permute-start(bf16[4,64,2304]{2,1,0:T(8,128)(2,1)S(1)} %pad_maximum_fusion.1), channel_id=1, source_target_pairs={{128,0},{256,128},{384,256},{0,384},{129,1},{257,129},{385,257},{1... | collective-permute-start | bytes 3538952 | tf_op jit(solution)/shard_map/ppermute | solution.py:11
  48.7 30.3 %collective-permute-start.6 = (bf16[4,64,2304]{2,1,0:T(8,128)(2,1)S(1)}, bf16[4,64,2304]{2,1,0:T(8,128)(2,1)}, u32[]{:S(2)}, u32[]{:S(2)}) collective-permute-start(bf16[4,64,2304]{2,1,0:T(8,128)(2,1)S(1)} %pad_maximum_fusion.1), channel_id=1, source_target_pairs={{384,0},{0,128},{128,256},{256,384},{385,1},{1,129},{129,257},{257... | collective-permute-start | bytes 3538952 | tf_op jit(solution)/shard_map/ppermute | solution.py:11
  67.4 35.3 %collective-permute-start.13 = (bf16[4,32,2304]{2,1,0:T(8,128)(2,1)}, bf16[4,32,2304]{2,1,0:T(8,128)(2,1)}, u32[]{:S(2)}, u32[]{:S(2)}) collective-permute-start(bf16[4,32,2304]{2,1,0:T(8,128)(2,1)} %slice.124), channel_id=1, source_target_pairs={{32,0},{64,32},{96,64},{0,96},{33,1},{65,33},{97,65},{1,97},{34,2}... | collective-permute-start | bytes 1769480 | tf_op jit(solution)/shard_map/ppermute | solution.py:11
  72.8 29.8 %collective-permute-start.15 = (bf16[4,32,2304]{2,1,0:T(8,128)(2,1)}, bf16[4,32,2304]{2,1,0:T(8,128)(2,1)}, u32[]{:S(2)}, u32[]{:S(2)}) collective-permute-start(bf16[4,32,2304]{2,1,0:T(8,128)(2,1)} %slice.125), channel_id=1, source_target_pairs={{96,0},{0,32},{32,64},{64,96},{97,1},{1,33},{33,65},{65,97},{98,2}... | collective-permute-start | bytes 1769480 | tf_op jit(solution)/shard_map/ppermute | solution.py:11
  76.7 25.9 %collective-permute-start.5 = (bf16[4,32,2304]{2,1,0:T(8,128)(2,1)}, bf16[4,32,2304]{2,1,0:T(8,128)(2,1)}, u32[]{:S(2)}, u32[]{:S(2)}) collective-permute-start(bf16[4,32,2304]{2,1,0:T(8,128)(2,1)} %slice.119), channel_id=1, source_target_pairs={{128,0},{256,128},{384,256},{0,384},{129,1},{257,129},{385,257},{1... | collective-permute-start | bytes 1769480 | tf_op jit(solution)/shard_map/ppermute | solution.py:11
  80.1 22.6 %collective-permute-start.7 = (bf16[4,32,2304]{2,1,0:T(8,128)(2,1)S(1)}, bf16[4,32,2304]{2,1,0:T(8,128)(2,1)S(1)}, u32[]{:S(2)}, u32[]{:S(2)}) collective-permute-start(bf16[4,32,2304]{2,1,0:T(8,128)(2,1)S(1)} %slice.120), channel_id=1, source_target_pairs={{384,0},{0,128},{128,256},{256,384},{385,1},{1,129},{129,257},{257... | collective-permute-start | bytes 1769480 | tf_op jit(solution)/shard_map/ppermute | solution.py:11
  87.5 2.9 copy-start.2
  93.0 5.4 %copy-start = (bf16[1024,2176]{1,0:T(8,128)(2,1)S(1)}, bf16[1024,2176]{1,0:T(8,128)(2,1)}, u32[]{:S(2)}) copy-start(bf16[1024,2176]{1,0:T(8,128)(2,1)} %all-gather.3.cloned.1.call-done) | copy-start | bytes 13369348
  107.4 1.7 copy-start.1
  113.3 11.7 %collective-permute-start.16 = (bf16[512,2048]{1,0:T(8,128)(2,1)S(1)}, bf16[512,2048]{1,0:T(8,128)(2,1)S(1)}, u32[]{:S(2)}, u32[]{:S(2)}) collective-permute-start(bf16[512,2048]{1,0:T(8,128)(2,1)S(1)} %convolution_convert_fusion), channel_id=1, source_target_pairs={{0,1},{1,0},{2,3},{3,2},{4,5},{5,4},{6,7},{7,6},{8,9},{9,8},{10,11... | collective-permute-start | bytes 6291464 | tf_op jit(solution)/shard_map/ppermute | solution.py:123
  127.0 68.2 %copy-start.7 = (f32[32]{0:T(128)S(1)}, f32[32]{0:T(128)}, u32[]{:S(2)}) copy-start(f32[32]{0:T(128)} %param.10) | copy-start | bytes 388
  195.9 58.9 %copy-start.3 = (bf16[32,2048]{1,0:T(8,128)(2,1)}, bf16[32,2048]{1,0:T(8,128)(2,1)S(1)}, u32[]{:S(2)}) copy-start(bf16[32,2048]{1,0:T(8,128)(2,1)S(1)} %reshape.129) | copy-start | bytes 393220
Sparse Core Ops, SparseCore 0:
  12.7 80.2 all-gather.2
  127.1 65.4 reduce-scatter.1

commit v7 on v6

--- a/solution.py
+++ b/solution.py
@@ -5,6 +5,7 @@
 
 BF = jnp.bfloat16
 F32 = jnp.float32
+Z = ("zh", "zl")
 
 
 def fetch(value, axis, shift, size):
@@ -53,13 +54,30 @@
     return turn(turn(both, 1, (4 - y) % 4), 2, (4 - x) % 4).reshape(rows, width)
 
 
+def reduce_near(parts):
+    own, ahead, across, behind = jnp.split(parts, 4)
+    half = across.shape[0] // 2
+    low = fetch(across[:half], Z, -2, 16)
+    high = fetch(across[half:], Z, 2, 16)
+    ahead = fetch(ahead, Z, -1, 16)
+    behind = fetch(behind, Z, 1, 16)
+    across = jnp.concatenate([low, high])
+    return sum(p.astype(F32) for p in (own, ahead, behind, across)).astype(BF)
+
+
+def reduce_far(total, rows):
+    moved = lax.all_to_all(total.reshape(-1, rows, total.shape[1]), "zh", 0, 0, tiled=True)
+    return jnp.sum(moved.astype(F32), axis=0)
+
+
 def local(tokens, routes, gates, curvature, w_gate, w_up, direction):
     rows, width = tokens.shape
     hidden_width = w_gate.shape[2]
-    z_count, cores = lax.axis_size("z"), lax.axis_size("c")
+    z_far, z_near, cores = (lax.axis_size(name) for name in ("zh", "zl", "c"))
+    z_count = z_far * z_near
     experts = z_count * cores
     y, x, core = lax.axis_index("y"), lax.axis_index("x"), lax.axis_index("c")
-    me = lax.axis_index(("z", "c"))
+    me = lax.axis_index(("zh", "zl", "c"))
 
     chosen = routes[:, :, None] == jnp.arange(experts, dtype=jnp.int32)
     table = jnp.sum(jnp.where(chosen, gates[:, :, None], 0.0), axis=1)
@@ -74,7 +92,7 @@
         ],
         1,
     )
-    arrived = lax.all_gather(sent, ("z", "c"), axis=0, tiled=True)
+    arrived = lax.all_gather(sent, ("zh", "zl", "c"), axis=0, tiled=True)
 
     stacked = jnp.concatenate([w_gate[0], w_up[0], direction[0]], 1)
     half = stacked.shape[0] // 2
@@ -123,7 +141,16 @@
     other = lax.ppermute(tangent(away).astype(BF), "c", [(0, 1), (1, 0)])
     kept = lax.optimization_barrier(tangent(home))
     paired = (kept + other.astype(F32)).astype(BF)
-    jv = lax.psum_scatter(paired, "z", scatter_dimension=0, tiled=True)
+    middle = width // 2
+    one = lax.psum_scatter(paired[:, :middle], Z, scatter_dimension=0, tiled=True)
+    turned = turn(
+        paired[:, middle:].reshape(z_far, z_near, rows, width - middle),
+        1,
+        lax.axis_index("zl"),
+    )
+    turned = turned.swapaxes(0, 1).reshape(-1, width - middle)
+    two = reduce_far(reduce_near(turned), rows).astype(BF)
+    jv = jnp.concatenate([one, two], 1)
     output_tangent = to_absolute(jv, y, x)
     curved = curvature[:, None] * output_tangent.astype(F32)
     peak = jnp.max(jnp.abs(curved), axis=1, keepdims=True)
@@ -131,7 +158,7 @@
     scaled = jnp.concatenate(
         [curved * jnp.exp2(-power), jnp.broadcast_to(power, (rows, 128))], 1
     ).astype(jnp.float16)
-    spread = lax.all_gather(scaled, ("z", "c"), axis=0, tiled=True)
+    spread = lax.all_gather(scaled, ("zh", "zl", "c"), axis=0, tiled=True)
     lifted = hidden.astype(F32) * jnp.exp2(spread[:, width : width + 1].astype(F32))
     part = lax.dot_general(
         spread[:, :width].astype(BF),
@@ -147,13 +174,13 @@
 
 
 def solution(mesh):
-    torus = Mesh(mesh.devices.reshape(4, 4, 16, 2), ("y", "x", "z", "c"))
-    tokens = P(("y", "x", "z", "c"), None)
-    matrix = P(("z", "c"), ("y", "x"), None)
+    torus = Mesh(mesh.devices.reshape(4, 4, 4, 4, 2), ("y", "x", "zh", "zl", "c"))
+    tokens = P(("y", "x", "zh", "zl", "c"), None)
+    matrix = P(("zh", "zl", "c"), ("y", "x"), None)
     return jax.shard_map(
         local,
         mesh=torus,
-        in_specs=(tokens, tokens, tokens, P(("y", "x", "z", "c")), matrix, matrix, matrix),
+        in_specs=(tokens, tokens, tokens, P(("y", "x", "zh", "zl", "c")), matrix, matrix, matrix),
         out_specs=(tokens, matrix),
         check_vma=False,
     )

time: 310 us -> 315 us (1.016)
  starting transfers between devices: 57.6 us -> 86.9 us
  waiting for transfers between devices: 82.8 us -> 56.7 us
    reduce_scatter x1, waiting for transfers between devices: 65.6 us -> 18.1 us  [local(): lax.psum_scatter(paired[:, :middle], Z, scatter_dimension=0, tiled=True)]
    ppermute x16 -> x20, starting transfers between devices: 49.4 us -> 69.6 us  [fetch(): lax.ppermute(value, axis, [((i + shift) % size, i) for i in range(size)])]
    all_to_all x0 -> x1, waiting for transfers between devices: none -> 16.4 us  [reduce_far(): lax.all_to_all(total.reshape(-1, rows, total.shape[1]), 'zh', 0, 0, tiled...]
    all_to_all x0 -> x1, starting transfers between devices: none -> 9.08 us  [reduce_far(): lax.all_to_all(total.reshape(-1, rows, total.shape[1]), 'zh', 0, 0, tiled...]
    ppermute x16 -> x20, waiting for transfers between devices: 14.5 us -> 19.5 us  [fetch(): lax.ppermute(value, axis, [((i + shift) % size, i) for i in range(size)])]
  transfers between devices with their start and end apart: 19 -> 24, of which waited for: 4 -> 7; matrix products, arithmetic and copies ran while one was open for 8% -> 8% of each run, Pallas kernels for 0% -> 0%
where the time goes in v7:
time: 315 us; the launch traced here: 314 us
  blocking collectives  100 us (32%)
  starting transfers between devices  86.9 us (28%)
  waiting for transfers between devices  56.7 us (18%)
  local copies, waits for them, and re-layouts  24.4 us (8%)
  matrix products  21.8 us (7%)
  between operations  14.8 us (5%)
  other arithmetic  9.17 us (3%)
    ppermute x20, starting transfers between devices, fetch(): lax.ppermute(value, axis, [((i + shift) % size, i) for i in range(size)])  69.6 us
    all_gather x1, blocking collectives, local(): spread = lax.all_gather(scaled, ('zh', 'zl', 'c'), axis=0, tiled=True)  54.6 us
    all_to_all x1, blocking collectives, local(): lax.all_to_all(part.reshape(16, -1, hidden_width), ('y', 'x'), 0, 0, tile...  45.5 us
    ppermute x20, waiting for transfers between devices, fetch(): lax.ppermute(value, axis, [((i + shift) % size, i) for i in range(size)])  19.5 us
    reduce_scatter x1, waiting for transfers between devices, local(): lax.psum_scatter(paired[:, :middle], Z, scatter_dimension=0, tiled=True)  18.1 us
    all_to_all x1, waiting for transfers between devices, reduce_far(): lax.all_to_all(total.reshape(-1, rows, total.shape[1]), 'zh', 0, 0, tiled...  16.4 us
    dot_general x4, matrix products, times(): return jnp.dot(left, right, preferred_element_type=F32)  11.6 us
    all_to_all x1, starting transfers between devices, reduce_far(): lax.all_to_all(total.reshape(-1, rows, total.shape[1]), 'zh', 0, 0, tiled...  9.08 us
  transfers between devices with their start and end apart: 24, of which 7 were waited for; matrix products, arithmetic and copies ran while one was open for 8% of the time, Pallas kernels for 0%

profile of v7, /device:TPU:1, one launch (start us, length us, event | category | flops | bytes accessed | tf_op | source)
XLA Modules:
  0.0 313.8 jit_solution(16505331610961355239)
XLA Ops:
  12.8 4.0 %collective-permute-start.10 = (bf16[64,2304]{1,0:T(8,128)(2,1)S(1)}, bf16[64,2304]{1,0:T(8,128)(2,1)S(1)}, u32[]{:S(2)}, u32[]{:S(2)}) collective-permute-start(bf16[64,2304]{1,0:T(8,128)(2,1)S(1)} %get-tuple-element.29), channel_id=1, source_target_pairs={{384,0},{0,128},{128,256},{256,384},{385,1},{1,129},{129,257},{257... | collective-permute-start | bytes 884744 | tf_op jit(solution)/shard_map/ppermute | solution.py:12
  16.8 3.4 %collective-permute-start.8 = (bf16[64,2304]{1,0:T(8,128)(2,1)S(1)}, bf16[64,2304]{1,0:T(8,128)(2,1)S(1)}, u32[]{:S(2)}, u32[]{:S(2)}) collective-permute-start(bf16[64,2304]{1,0:T(8,128)(2,1)S(1)} %get-tuple-element.29), channel_id=1, source_target_pairs={{128,0},{256,128},{384,256},{0,384},{129,1},{257,129},{385,257},{1... | collective-permute-start | bytes 884744 | tf_op jit(solution)/shard_map/ppermute | solution.py:12
  20.2 4.4 %collective-permute-start = (bf16[64,2304]{1,0:T(8,128)(2,1)S(1)}, bf16[64,2304]{1,0:T(8,128)(2,1)S(1)}, u32[]{:S(2)}, u32[]{:S(2)}) collective-permute-start(bf16[64,2304]{1,0:T(8,128)(2,1)S(1)} %get-tuple-element.30), channel_id=1, source_target_pairs={{32,0},{64,32},{96,64},{0,96},{33,1},{65,33},{97,65},{1,97},{34,2}... | collective-permute-start | bytes 884744 | tf_op jit(solution)/shard_map/ppermute | solution.py:12
  24.6 1.9 collective-permute-start.2
  26.5 1.9 collective-permute-start.11
  28.5 4.6 %collective-permute-start.9 = (bf16[32,2304]{1,0:T(8,128)(2,1)S(1)}, bf16[32,2304]{1,0:T(8,128)(2,1)S(1)}, u32[]{:S(2)}, u32[]{:S(2)}) collective-permute-start(bf16[32,2304]{1,0:T(8,128)(2,1)S(1)} %slice.152), channel_id=1, source_target_pairs={{128,0},{256,128},{384,256},{0,384},{129,1},{257,129},{385,257},{1... | collective-permute-start | bytes 442376 | tf_op jit(solution)/shard_map/ppermute | solution.py:12
  33.1 4.6 %collective-permute-start.1 = (bf16[32,2304]{1,0:T(8,128)(2,1)S(1)}, bf16[32,2304]{1,0:T(8,128)(2,1)S(1)}, u32[]{:S(2)}, u32[]{:S(2)}) collective-permute-start(bf16[32,2304]{1,0:T(8,128)(2,1)S(1)} %slice.147), channel_id=1, source_target_pairs={{32,0},{64,32},{96,64},{0,96},{33,1},{65,33},{97,65},{1,97},{34,2}... | collective-permute-start | bytes 442376 | tf_op jit(solution)/shard_map/ppermute | solution.py:12
  39.8 4.6 %collective-permute-start.12 = (bf16[4,64,2304]{2,1,0:T(8,128)(2,1)S(1)}, bf16[4,64,2304]{2,1,0:T(8,128)(2,1)S(1)}, u32[]{:S(2)}, u32[]{:S(2)}) collective-permute-start(bf16[4,64,2304]{2,1,0:T(8,128)(2,1)S(1)} %pad_maximum_fusion.2), channel_id=1, source_target_pairs={{32,0},{64,32},{96,64},{0,96},{33,1},{65,33},{97,65},{1,97},{34,2}... | collective-permute-start | bytes 3538952 | tf_op jit(solution)/shard_map/ppermute | solution.py:12
  44.4 1.9 collective-permute-start.14
  46.6 2.2 collective-permute-start.4
  48.7 3.1 collective-permute-start.6
  52.0 14.5 %collective-permute-done.12 = bf16[4,64,2304]{2,1,0:T(8,128)(2,1)S(1)} collective-permute-done((bf16[4,64,2304]{2,1,0:T(8,128)(2,1)S(1)}, bf16[4,64,2304]{2,1,0:T(8,128)(2,1)S(1)}, u32[]{:S(2)}, u32[]{:S(2)}) %collective-permute-start.12) | collective-permute-done | bytes 1179680 | tf_op jit(solution)/shard_map/ppermute | solution.py:12
  67.4 3.5 %collective-permute-start.13 = (bf16[4,32,2304]{2,1,0:T(8,128)(2,1)}, bf16[4,32,2304]{2,1,0:T(8,128)(2,1)}, u32[]{:S(2)}, u32[]{:S(2)}) collective-permute-start(bf16[4,32,2304]{2,1,0:T(8,128)(2,1)} %slice.154), channel_id=1, source_target_pairs={{32,0},{64,32},{96,64},{0,96},{33,1},{65,33},{97,65},{1,97},{34,2}... | collective-permute-start | bytes 1769480 | tf_op jit(solution)/shard_map/ppermute | solution.py:12
  70.9 1.9 slice.155
  74.8 1.9 slice.149
  76.7 2.3 collective-permute-start.5
  80.1 3.2 %collective-permute-start.7 = (bf16[4,32,2304]{2,1,0:T(8,128)(2,1)S(1)}, bf16[4,32,2304]{2,1,0:T(8,128)(2,1)S(1)}, u32[]{:S(2)}, u32[]{:S(2)}) collective-permute-start(bf16[4,32,2304]{2,1,0:T(8,128)(2,1)S(1)} %slice.150), channel_id=1, source_target_pairs={{384,0},{0,128},{128,256},{256,384},{385,1},{1,129},{129,257},{257... | collective-permute-start | bytes 1769480 | tf_op jit(solution)/shard_map/ppermute | solution.py:12
  87.5 2.9 copy-done.2
  93.0 5.4 %fusion.3 = f32[1024,768]{1,0:T(8,128)S(1)} fusion(bf16[1024,2176]{1,0:T(8,128)(2,1)} %all-gather.3.cloned.1.call-done, bf16[1536,2304]{1,0:T(8,128)(2,1)} %copy-done.2), kind=kOutput, calls=%fused_computation.9 | convolution fusion | flops 2415919104 | bytes 8650752 | tf_op jit(solution)/shard_map/dot_general | solution.py:114
  98.3 4.3 %fusion.5 = f32[1024,768]{1,0:T(8,128)S(1)} fusion(bf16[1024,2176]{1,0:T(8,128)(2,1)S(1)} %copy-done, bf16[1536,2304]{1,0:T(8,128)(2,1)} %copy-done.2), kind=kOutput, calls=%fused_computation.11 | convolution fusion | flops 2415919104 | bytes 8650752 | tf_op jit(solution)/shard_map/dot_general | solution.py:114
  109.0 4.2 %convolution_convert_fusion = bf16[512,2048]{1,0:T(8,128)(2,1)S(1)} fusion(bf16[512,768]{1,0:T(8,128)(2,1)S(1)} %bitcast.67, bf16[256,2304]{1,0:T(8,128)(2,1)S(1)} %bitcast.58, bf16[256,2304]{1,0:T(8,128)(2,1)S(1)} %bitcast.54, bf16[1536,768]{1,0:T(8,128)(2,1)S(1)} %copy-done.1), kind=kOutput, calls=%fused_computation.8 | convolution fusion | flops 1621098496 | bytes 7602176 | tf_op jit(solution)/shard_map/dot_general | solution.py:137
  113.3 8.1 %collective-permute-start.16 = (bf16[512,2048]{1,0:T(8,128)(2,1)S(1)}, bf16[512,2048]{1,0:T(8,128)(2,1)S(1)}, u32[]{:S(2)}, u32[]{:S(2)}) collective-permute-start(bf16[512,2048]{1,0:T(8,128)(2,1)S(1)} %convolution_convert_fusion), channel_id=1, source_target_pairs={{0,1},{1,0},{2,3},{3,2},{4,5},{5,4},{6,7},{7,6},{8,9},{9,8},{10,11... | collective-permute-start | bytes 6291464 | tf_op jit(solution)/shard_map/ppermute | solution.py:141
  127.4 3.4 %collective-permute-start.17 = (bf16[128,1024]{1,0:T(8,128)(2,1)S(1)}, bf16[128,1024]{1,0:T(8,128)(2,1)S(1)}, u32[]{:S(2)}, u32[]{:S(2)}) collective-permute-start(bf16[128,1024]{1,0:T(8,128)(2,1)S(1)} %bitcast.74), channel_id=1, source_target_pairs={{30,0},{0,2},{2,4},{4,6},{6,8},{8,10},{10,12},{12,14},{14,16},{16,... | collective-permute-start | bytes 786440 | tf_op jit(solution)/shard_map/ppermute | solution.py:12
  130.8 9.5 %collective-permute-start.18 = (bf16[128,1024]{1,0:T(8,128)(2,1)S(1)}, bf16[128,1024]{1,0:T(8,128)(2,1)S(1)}, u32[]{:S(2)}, u32[]{:S(2)}) collective-permute-start(bf16[128,1024]{1,0:T(8,128)(2,1)S(1)} %bitcast.73), channel_id=1, source_target_pairs={{2,0},{4,2},{6,4},{8,6},{10,8},{12,10},{14,12},{16,14},{18,16},{20... | collective-permute-start | bytes 786440 | tf_op jit(solution)/shard_map/ppermute | solution.py:12
  142.2 5.5 %collective-permute-start.20 = (bf16[64,1024]{1,0:T(8,128)(2,1)S(1)}, bf16[64,1024]{1,0:T(8,128)(2,1)S(1)}, u32[]{:S(2)}, u32[]{:S(2)}) collective-permute-start(bf16[64,1024]{1,0:T(8,128)(2,1)S(1)} %bitcast.79), channel_id=1, source_target_pairs={{4,0},{6,2},{8,4},{10,6},{12,8},{14,10},{16,12},{18,14},{20,16},{2... | collective-permute-start | bytes 393224 | tf_op jit(solution)/shard_map/ppermute | solution.py:12
  147.7 3.9 %collective-permute-done.19 = bf16[64,1024]{1,0:T(8,128)(2,1)S(1)} collective-permute-done((bf16[64,1024]{1,0:T(8,128)(2,1)S(1)}, bf16[64,1024]{1,0:T(8,128)(2,1)S(1)}, u32[]{:S(2)}, u32[]{:S(2)}) %collective-permute-start.19) | collective-permute-done | bytes 131104 | tf_op jit(solution)/shard_map/ppermute | solution.py:12
  153.6 9.1 %all-to-all-start = ((bf16[4,32,1024]{2,1,0:T(8,128)(2,1)}), bf16[4,32,1024]{2,1,0:T(8,128)(2,1)S(1)}, u32[]{:S(2)}, u32[]{:S(2)}) async-start(bf16[4,32,1024]{2,1,0:T(8,128)(2,1)} %bitcast.30), calls=%async_computation.1 | async-start | bytes 524288 | tf_op jit(solution)/shard_map/all_to_all | solution.py:69
  162.7 16.4 %all-to-all-done = bf16[4,32,1024]{2,1,0:T(8,128)(2,1)S(1)} async-done(((bf16[4,32,1024]{2,1,0:T(8,128)(2,1)}), bf16[4,32,1024]{2,1,0:T(8,128)(2,1)S(1)}, u32[]{:S(2)}, u32[]{:S(2)}) %all-to-all-start) | async-done | bytes 262176 | tf_op jit(solution)/shard_map/all_to_all | solution.py:69
  179.1 18.1 %reduce-scatter.2.cloned.1.call-done = bf16[32,1024]{1,0:T(8,128)(2,1)} async-done(((bf16[512,1024]{1,0:T(8,128)(2,1)}), bf16[32,1024]{1,0:T(8,128)(2,1)}) %reduce-scatter.2.cloned.1.call-update) | async-done | bytes 65552 | tf_op jit(solution)/shard_map/reduce_scatter | solution.py:145
  201.4 54.6 %all-gather.4 = f16[1024,2176]{1,0:T(8,128)(2,1)S(1)} all-gather(f16[32,2176]{1,0:T(8,128)(2,1)S(1)} %pad_maximum_fusion.6), channel_id=1, replica_groups=mesh['y'=4,'x'=4,'zh'=4,'zl'=4,'c'=2] {'zh','zl','c'}, dimensions={0}, use_global_device_ids=true | all-gather | bytes 4595712 | tf_op jit(solution)/shard_map/all_gather | solution.py:161
  256.2 4.2 %fusion.1 = bf16[2048,768]{1,0:T(8,128)(2,1)S(1)} fusion(f16[1024,2176]{1,0:T(8,128)(2,1)S(1)} %all-gather.4, bf16[1024,768]{1,0:T(8,128)(2,1)S(1)} %multiply_convert_fusion.1, f32[1024]{0:T(1024)S(1)} %exponential_reduce_fusion), kind=kOutput, calls=%fused_computation.3 | convolution fusion | flops 3227254784 | bytes 8916992 | tf_op jit(solution)/shard_map/dot_general | solution.py:163
  260.4 45.5 %all_to_all.10 = bf16[16,128,768]{2,1,0:T(8,128)(2,1)S(1)} all-to-all(bf16[16,128,768]{2,1,0:T(8,128)(2,1)S(1)} %bitcast.64), channel_id=1, replica_groups=mesh['y'=4,'x'=4,'zh'=4,'zl'=4,'c'=2] {'y','x'}, dimensions={0} | all-to-all | bytes 6291456 | tf_op jit(solution)/shard_map/all_to_all | solution.py:169
  (119 shorter events, 40.3 us)
Async XLA Ops:
  7.2 5.4 %copy-start.6 = (bf16[1,128,768]{2,1,0:T(8,128)(2,1)S(1)}, bf16[1,128,768]{2,1,0:T(8,128)(2,1)}, u32[]{:S(2)}) copy-start(bf16[1,128,768]{2,1,0:T(8,128)(2,1)} %param.11) | copy-start | bytes 589828
  7.2 5.4 %copy-start.5 = (bf16[1,128,768]{2,1,0:T(8,128)(2,1)S(1)}, bf16[1,128,768]{2,1,0:T(8,128)(2,1)}, u32[]{:S(2)}) copy-start(bf16[1,128,768]{2,1,0:T(8,128)(2,1)} %param.12) | copy-start | bytes 589828
  7.2 5.4 %copy-start.4 = (bf16[1,128,768]{2,1,0:T(8,128)(2,1)S(1)}, bf16[1,128,768]{2,1,0:T(8,128)(2,1)}, u32[]{:S(2)}) copy-start(bf16[1,128,768]{2,1,0:T(8,128)(2,1)} %param.13) | copy-start | bytes 589828
  7.2 85.8 %all-gather.3.cloned.1.call-start = ((), (), s32[]{:S(2)}) async-start(), calls=%async_computation.3 | async-start | bytes 4595712 | tf_op jit(solution)/shard_map/all_gather | solution.py:95
  12.6 184.6 %reduce-scatter.2.cloned.1.call-start = ((), (), s32[]{:S(2)}) async-start(), calls=%async_computation.4 | async-start | bytes 1114112 | tf_op jit(solution)/shard_map/reduce_scatter | solution.py:145
  12.8 13.7 %collective-permute-start.10 = (bf16[64,2304]{1,0:T(8,128)(2,1)S(1)}, bf16[64,2304]{1,0:T(8,128)(2,1)S(1)}, u32[]{:S(2)}, u32[]{:S(2)}) collective-permute-start(bf16[64,2304]{1,0:T(8,128)(2,1)S(1)} %get-tuple-element.29), channel_id=1, source_target_pairs={{384,0},{0,128},{128,256},{256,384},{385,1},{1,129},{129,257},{257... | collective-permute-start | bytes 884744 | tf_op jit(solution)/shard_map/ppermute | solution.py:12
  16.8 11.7 %collective-permute-start.8 = (bf16[64,2304]{1,0:T(8,128)(2,1)S(1)}, bf16[64,2304]{1,0:T(8,128)(2,1)S(1)}, u32[]{:S(2)}, u32[]{:S(2)}) collective-permute-start(bf16[64,2304]{1,0:T(8,128)(2,1)S(1)} %get-tuple-element.29), channel_id=1, source_target_pairs={{128,0},{256,128},{384,256},{0,384},{129,1},{257,129},{385,257},{1... | collective-permute-start | bytes 884744 | tf_op jit(solution)/shard_map/ppermute | solution.py:12
  20.2 12.9 %collective-permute-start = (bf16[64,2304]{1,0:T(8,128)(2,1)S(1)}, bf16[64,2304]{1,0:T(8,128)(2,1)S(1)}, u32[]{:S(2)}, u32[]{:S(2)}) collective-permute-start(bf16[64,2304]{1,0:T(8,128)(2,1)S(1)} %get-tuple-element.30), channel_id=1, source_target_pairs={{32,0},{64,32},{96,64},{0,96},{33,1},{65,33},{97,65},{1,97},{34,2}... | collective-permute-start | bytes 884744 | tf_op jit(solution)/shard_map/ppermute | solution.py:12
  24.6 13.1 %collective-permute-start.2 = (bf16[64,2304]{1,0:T(8,128)(2,1)S(1)}, bf16[64,2304]{1,0:T(8,128)(2,1)S(1)}, u32[]{:S(2)}, u32[]{:S(2)}) collective-permute-start(bf16[64,2304]{1,0:T(8,128)(2,1)S(1)} %get-tuple-element.30), channel_id=1, source_target_pairs={{96,0},{0,32},{32,64},{64,96},{97,1},{1,33},{33,65},{65,97},{98,2}... | collective-permute-start | bytes 884744 | tf_op jit(solution)/shard_map/ppermute | solution.py:12
  26.5 13.1 %collective-permute-start.11 = (bf16[32,2304]{1,0:T(8,128)(2,1)S(1)}, bf16[32,2304]{1,0:T(8,128)(2,1)S(1)}, u32[]{:S(2)}, u32[]{:S(2)}) collective-permute-start(bf16[32,2304]{1,0:T(8,128)(2,1)S(1)} %slice.153), channel_id=1, source_target_pairs={{384,0},{0,128},{128,256},{256,384},{385,1},{1,129},{129,257},{257... | collective-permute-start | bytes 442376 | tf_op jit(solution)/shard_map/ppermute | solution.py:12
  28.5 11.2 %collective-permute-start.9 = (bf16[32,2304]{1,0:T(8,128)(2,1)S(1)}, bf16[32,2304]{1,0:T(8,128)(2,1)S(1)}, u32[]{:S(2)}, u32[]{:S(2)}) collective-permute-start(bf16[32,2304]{1,0:T(8,128)(2,1)S(1)} %slice.152), channel_id=1, source_target_pairs={{128,0},{256,128},{384,256},{0,384},{129,1},{257,129},{385,257},{1... | collective-permute-start | bytes 442376 | tf_op jit(solution)/shard_map/ppermute | solution.py:12
  33.1 13.3 %collective-permute-start.1 = (bf16[32,2304]{1,0:T(8,128)(2,1)S(1)}, bf16[32,2304]{1,0:T(8,128)(2,1)S(1)}, u32[]{:S(2)}, u32[]{:S(2)}) collective-permute-start(bf16[32,2304]{1,0:T(8,128)(2,1)S(1)} %slice.147), channel_id=1, source_target_pairs={{32,0},{64,32},{96,64},{0,96},{33,1},{65,33},{97,65},{1,97},{34,2}... | collective-permute-start | bytes 442376 | tf_op jit(solution)/shard_map/ppermute | solution.py:12
  37.7 8.7 %collective-permute-start.3 = (bf16[32,2304]{1,0:T(8,128)(2,1)S(1)}, bf16[32,2304]{1,0:T(8,128)(2,1)S(1)}, u32[]{:S(2)}, u32[]{:S(2)}) collective-permute-start(bf16[32,2304]{1,0:T(8,128)(2,1)S(1)} %slice.148), channel_id=1, source_target_pairs={{96,0},{0,32},{32,64},{64,96},{97,1},{1,33},{33,65},{65,97},{98,2}... | collective-permute-start | bytes 442376 | tf_op jit(solution)/shard_map/ppermute | solution.py:12
  39.8 26.6 %collective-permute-start.12 = (bf16[4,64,2304]{2,1,0:T(8,128)(2,1)S(1)}, bf16[4,64,2304]{2,1,0:T(8,128)(2,1)S(1)}, u32[]{:S(2)}, u32[]{:S(2)}) collective-permute-start(bf16[4,64,2304]{2,1,0:T(8,128)(2,1)S(1)} %pad_maximum_fusion.2), channel_id=1, source_target_pairs={{32,0},{64,32},{96,64},{0,96},{33,1},{65,33},{97,65},{1,97},{34,2}... | collective-permute-start | bytes 3538952 | tf_op jit(solution)/shard_map/ppermute | solution.py:12
  44.4 26.5 %collective-permute-start.14 = (bf16[4,64,2304]{2,1,0:T(8,128)(2,1)S(1)}, bf16[4,64,2304]{2,1,0:T(8,128)(2,1)}, u32[]{:S(2)}, u32[]{:S(2)}) collective-permute-start(bf16[4,64,2304]{2,1,0:T(8,128)(2,1)S(1)} %pad_maximum_fusion.2), channel_id=1, source_target_pairs={{96,0},{0,32},{32,64},{64,96},{97,1},{1,33},{33,65},{65,97},{98,2}... | collective-permute-start | bytes 3538952 | tf_op jit(solution)/shard_map/ppermute | solution.py:12
  46.6 28.2 %collective-permute-start.4 = (bf16[4,64,2304]{2,1,0:T(8,128)(2,1)S(1)}, bf16[4,64,2304]{2,1,0:T(8,128)(2,1)}, u32[]{:S(2)}, u32[]{:S(2)}) collective-permute-start(bf16[4,64,2304]{2,1,0:T(8,128)(2,1)S(1)} %pad_maximum_fusion.1), channel_id=1, source_target_pairs={{128,0},{256,128},{384,256},{0,384},{129,1},{257,129},{385,257},{1... | collective-permute-start | bytes 3538952 | tf_op jit(solution)/shard_map/ppermute | solution.py:12
  48.7 30.3 %collective-permute-start.6 = (bf16[4,64,2304]{2,1,0:T(8,128)(2,1)S(1)}, bf16[4,64,2304]{2,1,0:T(8,128)(2,1)}, u32[]{:S(2)}, u32[]{:S(2)}) collective-permute-start(bf16[4,64,2304]{2,1,0:T(8,128)(2,1)S(1)} %pad_maximum_fusion.1), channel_id=1, source_target_pairs={{384,0},{0,128},{128,256},{256,384},{385,1},{1,129},{129,257},{257... | collective-permute-start | bytes 3538952 | tf_op jit(solution)/shard_map/ppermute | solution.py:12
  67.4 35.3 %collective-permute-start.13 = (bf16[4,32,2304]{2,1,0:T(8,128)(2,1)}, bf16[4,32,2304]{2,1,0:T(8,128)(2,1)}, u32[]{:S(2)}, u32[]{:S(2)}) collective-permute-start(bf16[4,32,2304]{2,1,0:T(8,128)(2,1)} %slice.154), channel_id=1, source_target_pairs={{32,0},{64,32},{96,64},{0,96},{33,1},{65,33},{97,65},{1,97},{34,2}... | collective-permute-start | bytes 1769480 | tf_op jit(solution)/shard_map/ppermute | solution.py:12
  72.8 29.8 %collective-permute-start.15 = (bf16[4,32,2304]{2,1,0:T(8,128)(2,1)}, bf16[4,32,2304]{2,1,0:T(8,128)(2,1)}, u32[]{:S(2)}, u32[]{:S(2)}) collective-permute-start(bf16[4,32,2304]{2,1,0:T(8,128)(2,1)} %slice.155), channel_id=1, source_target_pairs={{96,0},{0,32},{32,64},{64,96},{97,1},{1,33},{33,65},{65,97},{98,2}... | collective-permute-start | bytes 1769480 | tf_op jit(solution)/shard_map/ppermute | solution.py:12
  76.7 25.9 %collective-permute-start.5 = (bf16[4,32,2304]{2,1,0:T(8,128)(2,1)}, bf16[4,32,2304]{2,1,0:T(8,128)(2,1)}, u32[]{:S(2)}, u32[]{:S(2)}) collective-permute-start(bf16[4,32,2304]{2,1,0:T(8,128)(2,1)} %slice.149), channel_id=1, source_target_pairs={{128,0},{256,128},{384,256},{0,384},{129,1},{257,129},{385,257},{1... | collective-permute-start | bytes 1769480 | tf_op jit(solution)/shard_map/ppermute | solution.py:12
  80.1 22.6 %collective-permute-start.7 = (bf16[4,32,2304]{2,1,0:T(8,128)(2,1)S(1)}, bf16[4,32,2304]{2,1,0:T(8,128)(2,1)S(1)}, u32[]{:S(2)}, u32[]{:S(2)}) collective-permute-start(bf16[4,32,2304]{2,1,0:T(8,128)(2,1)S(1)} %slice.150), channel_id=1, source_target_pairs={{384,0},{0,128},{128,256},{256,384},{385,1},{1,129},{129,257},{257... | collective-permute-start | bytes 1769480 | tf_op jit(solution)/shard_map/ppermute | solution.py:12
  87.5 2.9 copy-start.2
  93.0 5.4 %copy-start = (bf16[1024,2176]{1,0:T(8,128)(2,1)S(1)}, bf16[1024,2176]{1,0:T(8,128)(2,1)}, u32[]{:S(2)}) copy-start(bf16[1024,2176]{1,0:T(8,128)(2,1)} %all-gather.3.cloned.1.call-done) | copy-start | bytes 13369348
  107.4 1.7 copy-start.1
  113.3 11.7 %collective-permute-start.16 = (bf16[512,2048]{1,0:T(8,128)(2,1)S(1)}, bf16[512,2048]{1,0:T(8,128)(2,1)S(1)}, u32[]{:S(2)}, u32[]{:S(2)}) collective-permute-start(bf16[512,2048]{1,0:T(8,128)(2,1)S(1)} %convolution_convert_fusion), channel_id=1, source_target_pairs={{0,1},{1,0},{2,3},{3,2},{4,5},{5,4},{6,7},{7,6},{8,9},{9,8},{10,11... | collective-permute-start | bytes 6291464 | tf_op jit(solution)/shard_map/ppermute | solution.py:141
  127.3 73.1 %copy-start.7 = (f32[32]{0:T(128)S(1)}, f32[32]{0:T(128)}, u32[]{:S(2)}) copy-start(f32[32]{0:T(128)} %param.10) | copy-start | bytes 388
  127.4 25.3 %collective-permute-start.17 = (bf16[128,1024]{1,0:T(8,128)(2,1)S(1)}, bf16[128,1024]{1,0:T(8,128)(2,1)S(1)}, u32[]{:S(2)}, u32[]{:S(2)}) collective-permute-start(bf16[128,1024]{1,0:T(8,128)(2,1)S(1)} %bitcast.74), channel_id=1, source_target_pairs={{30,0},{0,2},{2,4},{4,6},{6,8},{8,10},{10,12},{12,14},{14,16},{16,... | collective-permute-start | bytes 786440 | tf_op jit(solution)/shard_map/ppermute | solution.py:12
  130.8 21.9 %collective-permute-start.18 = (bf16[128,1024]{1,0:T(8,128)(2,1)S(1)}, bf16[128,1024]{1,0:T(8,128)(2,1)S(1)}, u32[]{:S(2)}, u32[]{:S(2)}) collective-permute-start(bf16[128,1024]{1,0:T(8,128)(2,1)S(1)} %bitcast.73), channel_id=1, source_target_pairs={{2,0},{4,2},{6,4},{8,6},{10,8},{12,10},{14,12},{16,14},{18,16},{20... | collective-permute-start | bytes 786440 | tf_op jit(solution)/shard_map/ppermute | solution.py:12
  140.3 11.3 %collective-permute-start.19 = (bf16[64,1024]{1,0:T(8,128)(2,1)S(1)}, bf16[64,1024]{1,0:T(8,128)(2,1)S(1)}, u32[]{:S(2)}, u32[]{:S(2)}) collective-permute-start(bf16[64,1024]{1,0:T(8,128)(2,1)S(1)} %bitcast.80), channel_id=1, source_target_pairs={{28,0},{30,2},{0,4},{2,6},{4,8},{6,10},{8,12},{10,14},{12,16},{14,... | collective-permute-start | bytes 393224 | tf_op jit(solution)/shard_map/ppermute | solution.py:12
  142.2 10.5 %collective-permute-start.20 = (bf16[64,1024]{1,0:T(8,128)(2,1)S(1)}, bf16[64,1024]{1,0:T(8,128)(2,1)S(1)}, u32[]{:S(2)}, u32[]{:S(2)}) collective-permute-start(bf16[64,1024]{1,0:T(8,128)(2,1)S(1)} %bitcast.79), channel_id=1, source_target_pairs={{4,0},{6,2},{8,4},{10,6},{12,8},{14,10},{16,12},{18,14},{20,16},{2... | collective-permute-start | bytes 393224 | tf_op jit(solution)/shard_map/ppermute | solution.py:12
  153.6 25.4 %all-to-all-start = ((bf16[4,32,1024]{2,1,0:T(8,128)(2,1)}), bf16[4,32,1024]{2,1,0:T(8,128)(2,1)S(1)}, u32[]{:S(2)}, u32[]{:S(2)}) async-start(bf16[4,32,1024]{2,1,0:T(8,128)(2,1)} %bitcast.30), calls=%async_computation.1 | async-start | bytes 524288 | tf_op jit(solution)/shard_map/all_to_all | solution.py:69
  201.1 59.2 %copy-start.3 = (bf16[32,2048]{1,0:T(8,128)(2,1)}, bf16[32,2048]{1,0:T(8,128)(2,1)S(1)}, u32[]{:S(2)}) copy-start(bf16[32,2048]{1,0:T(8,128)(2,1)S(1)} %reshape.146) | copy-start | bytes 393220
Sparse Core Ops, SparseCore 0:
  12.7 80.2 all-gather.2
  127.0 70.1 reduce-scatter.1

commit v8 on v6

--- a/solution.py
+++ b/solution.py
@@ -1,6 +1,10 @@
+import functools
+
 import jax
 import jax.numpy as jnp
 from jax import lax
+from jax.experimental import pallas as pl
+from jax.experimental.pallas import tpu as pltpu
 from jax.sharding import Mesh, PartitionSpec as P
 
 BF = jnp.bfloat16
@@ -53,6 +57,34 @@
     return turn(turn(both, 1, (4 - y) % 4), 2, (4 - x) % 4).reshape(rows, width)
 
 
+def expert_kernel(size, group_ref, mask_ref, *refs):
+    pieces, hidden_ref, tangent_ref = refs[:-2], refs[-2], refs[-1]
+    gate = jnp.zeros((group_ref.shape[0], size), F32)
+    up = jnp.zeros((group_ref.shape[0], size), F32)
+    start = 0
+    for piece in pieces:
+        depth = piece.shape[0]
+        rows = group_ref[:, start : start + depth]
+        gate += jnp.dot(rows, piece[:, :size], preferred_element_type=F32)
+        up += jnp.dot(rows, piece[:, size : 2 * size], preferred_element_type=F32)
+        start += depth
+    share = jnp.sum(
+        group_ref[:, start:].astype(F32) * mask_ref[...], axis=1, keepdims=True
+    )
+    hidden = (jax.nn.silu(gate) * up * share).astype(BF)
+    hidden_ref[...] = hidden
+    start = 0
+    for piece in pieces:
+        depth = piece.shape[0]
+        tangent_ref[:, start : start + depth] = lax.dot_general(
+            hidden,
+            piece[:, 2 * size :],
+            (((1,), (1,)), ((), ())),
+            preferred_element_type=F32,
+        ).astype(BF)
+        start += depth
+
+
 def local(tokens, routes, gates, curvature, w_gate, w_up, direction):
     rows, width = tokens.shape
     hidden_width = w_gate.shape[2]
@@ -81,48 +113,47 @@
     first_soon, first_late = ring4(ring4_stack(stacked[:half], "x"), "y")
     second_soon, second_late = ring4(ring4_stack(stacked[half:], "y"), "x")
     columns = stacked.shape[1]
-    soon = jnp.concatenate([p.reshape(-1, columns) for p in first_soon + second_soon])
+    late = [
+        jnp.concatenate(pair, -2).reshape(-1, columns) for pair in (first_late, second_late)
+    ]
+    pieces = [p.reshape(-1, columns) for p in first_soon + second_soon] + late
 
     lanes = lax.broadcasted_iota(jnp.int32, (1, 128), 1)
-    mine = (lanes == me) | (lanes == me + experts)
-    share = jnp.sum(
-        jnp.where(mine, arrived[:, width:].astype(F32), 0.0), axis=1, keepdims=True
-    )
-    group = arrived[:, :width]
-    early = soon.shape[0]
+    mask = ((lanes == me) | (lanes == me + experts)).astype(F32)
+    count, wide = arrived.shape
+    block = count // 4
+    hidden, tangents = pl.pallas_call(
+        functools.partial(expert_kernel, hidden_width),
+        grid=(4,),
+        in_specs=[
+            pl.BlockSpec((block, wide), lambda i: (i, 0)),
+            pl.BlockSpec((1, 128), lambda i: (0, 0)),
+        ]
+        + [
+            pl.BlockSpec(p.shape, lambda i: (0, 0), pipeline_mode=pl.Buffered(1))
+            for p in pieces
+        ],
+        out_specs=[
+            pl.BlockSpec((block, hidden_width), lambda i: (i, 0)),
+            pl.BlockSpec((block, width), lambda i: (i, 0)),
+        ],
+        out_shape=[
+            jax.ShapeDtypeStruct((count, hidden_width), BF),
+            jax.ShapeDtypeStruct((count, width), BF),
+        ],
+        compiler_params=pltpu.CompilerParams(vmem_limit_bytes=52 * 1024 * 1024),
+        cost_estimate=pl.CostEstimate(
+            flops=6 * count * width * hidden_width,
+            bytes_accessed=2 * (count * (2 * width + hidden_width) + 3 * width * hidden_width),
+            transcendentals=count * hidden_width,
+        ),
+    )(arrived, mask, *pieces)
 
-    def times(left, right, which):
-        right = right[:, which * hidden_width : (which + 1) * hidden_width]
-        return jnp.dot(left, right, preferred_element_type=F32)
-
-    gate_soon = times(group[:, :early], soon, 0)
-    up_soon = times(group[:, :early], soon, 1)
-    low_1, high_1, low_2, high_2, gate_soon, up_soon = lax.optimization_barrier(
-        (*first_late, *second_late, gate_soon, up_soon)
-    )
-    late = jnp.concatenate(
-        [
-            jnp.concatenate(pair, -2).reshape(-1, columns)
-            for pair in ((low_1, high_1), (low_2, high_2))
-        ]
-    )
-    back = jnp.concatenate([soon[:, 2 * hidden_width :], late[:, 2 * hidden_width :]])
-    gate_pre = gate_soon + times(group[:, early:], late, 0)
-    up_pre = up_soon + times(group[:, early:], late, 1)
-    hidden = (jax.nn.silu(gate_pre) * up_pre * share).astype(BF)
-
-    by_core = hidden.reshape(z_count, cores, rows, hidden_width)
-    away = lax.dynamic_index_in_dim(by_core, 1 - core, 1, False).reshape(-1, hidden_width)
-    home = lax.dynamic_index_in_dim(by_core, core, 1, False).reshape(-1, hidden_width)
-
-    def tangent(part):
-        return lax.dot_general(
-            part, back, (((1,), (1,)), ((), ())), preferred_element_type=F32
-        )
-
-    other = lax.ppermute(tangent(away).astype(BF), "c", [(0, 1), (1, 0)])
-    kept = lax.optimization_barrier(tangent(home))
-    paired = (kept + other.astype(F32)).astype(BF)
+    by_core = tangents.reshape(z_count, cores, rows, width)
+    away = lax.dynamic_index_in_dim(by_core, 1 - core, 1, False).reshape(-1, width)
+    home = lax.dynamic_index_in_dim(by_core, core, 1, False).reshape(-1, width)
+    other = lax.ppermute(away, "c", [(0, 1), (1, 0)])
+    paired = (home.astype(F32) + other.astype(F32)).astype(BF)
     jv = lax.psum_scatter(paired, "z", scatter_dimension=0, tiled=True)
     output_tangent = to_absolute(jv, y, x)
     curved = curvature[:, None] * output_tangent.astype(F32)

time: 310 us -> 307 us (level)
  matrix products: 21.8 us -> 4.16 us
  Pallas kernels: 0 us -> 15.4 us
  local copies, waits for them, and re-layouts: 23.1 us -> 9.19 us
  waiting for transfers between devices: 82.8 us -> 91.1 us
  starting transfers between devices: 57.6 us -> 60.8 us
    dot_general x6 -> x0, matrix products: 17.6 us -> none  [the longest x4 11.6 us: times(): return jnp.dot(left, right, preferred_element_type=F32)]
    pallas_call x0 -> x1, Pallas kernels: none -> 15.4 us  [local(): pl.pallas_call(functools.partial(expert_kernel, hidden_width), grid=(4,),...]
    ppermute x16, waiting for transfers between devices: 14.5 us -> 23 us  [fetch(): lax.ppermute(value, axis, [((i + shift) % size, i) for i in range(size)])]
    unnamed x23 -> x28, local copies, waits for them, and re-layouts: 8.88 us -> 1.18 us
    ppermute x16, starting transfers between devices: 49.4 us -> 53.6 us  [fetch(): lax.ppermute(value, axis, [((i + shift) % size, i) for i in range(size)])]
    concatenate x1 -> x2, other arithmetic: 1.58 us -> 4.73 us  [local(): jnp.concatenate(pair, -2).reshape(-1, columns)]
  transfers between devices with their start and end apart: 19 -> 19, of which waited for: 4 -> 5; matrix products, arithmetic and copies ran while one was open for 8% -> 2% of each run, Pallas kernels for 0% -> 0%
where the time goes in v8:
time: 307 us; the launch traced here: 306 us
  blocking collectives  100 us (33%)
  waiting for transfers between devices  91.1 us (30%)
  starting transfers between devices  60.8 us (20%)
  Pallas kernels  15.4 us (5%)
  between operations  14.8 us (5%)
  other arithmetic  10.5 us (3%)
  local copies, waits for them, and re-layouts  9.19 us (3%)
  matrix products  4.16 us (1%)
    reduce_scatter x1, waiting for transfers between devices, local(): jv = lax.psum_scatter(paired, 'z', scatter_dimension=0, tiled=True)  64.3 us
    all_gather x1, blocking collectives, local(): spread = lax.all_gather(scaled, ('z', 'c'), axis=0, tiled=True)  54.7 us
    ppermute x16, starting transfers between devices, fetch(): lax.ppermute(value, axis, [((i + shift) % size, i) for i in range(size)])  53.6 us
    all_to_all x1, blocking collectives, local(): lax.all_to_all(part.reshape(16, -1, hidden_width), ('y', 'x'), 0, 0, tile...  45.5 us
    ppermute x16, waiting for transfers between devices, fetch(): lax.ppermute(value, axis, [((i + shift) % size, i) for i in range(size)])  23 us
    pallas_call x1, Pallas kernels, local(): pl.pallas_call(functools.partial(expert_kernel, hidden_width), grid=(4,),...  15.4 us
    ppermute x1, starting transfers between devices, local(): other = lax.ppermute(away, 'c', [(0, 1), (1, 0)])  7.13 us
  transfers between devices with their start and end apart: 19, of which 5 were waited for; matrix products, arithmetic and copies ran while one was open for 2% of the time, Pallas kernels for 0%

profile of v8, /device:TPU:1, one launch (start us, length us, event | category | flops | bytes accessed | tf_op | source)
XLA Modules:
  0.0 306.1 jit_solution(9680293671381109777)
XLA Ops:
  7.2 1.0 reshape.121
  11.3 5.5 %collective-permute-start.6 = (bf16[64,2304]{1,0:T(8,128)(2,1)S(1)}, bf16[64,2304]{1,0:T(8,128)(2,1)S(1)}, u32[]{:S(2)}, u32[]{:S(2)}) collective-permute-start(bf16[64,2304]{1,0:T(8,128)(2,1)S(1)} %get-tuple-element.14), channel_id=1, source_target_pairs={{128,0},{256,128},{384,256},{0,384},{129,1},{257,129},{385,257},{1... | collective-permute-start | bytes 884744 | tf_op jit(solution)/shard_map/ppermute | solution.py:15
  16.8 1.9 collective-permute-start.8
  18.7 4.4 %collective-permute-start = (bf16[64,2304]{1,0:T(8,128)(2,1)S(1)}, bf16[64,2304]{1,0:T(8,128)(2,1)S(1)}, u32[]{:S(2)}, u32[]{:S(2)}) collective-permute-start(bf16[64,2304]{1,0:T(8,128)(2,1)S(1)} %get-tuple-element.15), channel_id=1, source_target_pairs={{32,0},{64,32},{96,64},{0,96},{33,1},{65,33},{97,65},{1,97},{34,2}... | collective-permute-start | bytes 884744 | tf_op jit(solution)/shard_map/ppermute | solution.py:15
  23.1 1.9 collective-permute-start.2
  25.1 4.6 %collective-permute-start.7 = (bf16[32,2304]{1,0:T(8,128)(2,1)S(1)}, bf16[32,2304]{1,0:T(8,128)(2,1)S(1)}, u32[]{:S(2)}, u32[]{:S(2)}) collective-permute-start(bf16[32,2304]{1,0:T(8,128)(2,1)S(1)} %slice.85), channel_id=1, source_target_pairs={{128,0},{256,128},{384,256},{0,384},{129,1},{257,129},{385,257},{1... | collective-permute-start | bytes 442376 | tf_op jit(solution)/shard_map/ppermute | solution.py:15
  29.7 1.9 collective-permute-start.9
  31.6 4.6 %collective-permute-start.1 = (bf16[32,2304]{1,0:T(8,128)(2,1)S(1)}, bf16[32,2304]{1,0:T(8,128)(2,1)S(1)}, u32[]{:S(2)}, u32[]{:S(2)}) collective-permute-start(bf16[32,2304]{1,0:T(8,128)(2,1)S(1)} %slice.82), channel_id=1, source_target_pairs={{32,0},{64,32},{96,64},{0,96},{33,1},{65,33},{97,65},{1,97},{34,2}... | collective-permute-start | bytes 442376 | tf_op jit(solution)/shard_map/ppermute | solution.py:15
  36.3 1.9 collective-permute-start.3
  38.4 4.6 %collective-permute-start.10 = (bf16[4,64,2304]{2,1,0:T(8,128)(2,1)S(1)}, bf16[4,64,2304]{2,1,0:T(8,128)(2,1)S(1)}, u32[]{:S(2)}, u32[]{:S(2)}) collective-permute-start(bf16[4,64,2304]{2,1,0:T(8,128)(2,1)S(1)} %pad_maximum_fusion.1), channel_id=1, source_target_pairs={{32,0},{64,32},{96,64},{0,96},{33,1},{65,33},{97,65},{1,97},{34,2}... | collective-permute-start | bytes 3538952 | tf_op jit(solution)/shard_map/ppermute | solution.py:15
  43.0 1.9 collective-permute-start.11
  45.1 4.6 %collective-permute-start.4 = (bf16[4,64,2304]{2,1,0:T(8,128)(2,1)S(1)}, bf16[4,64,2304]{2,1,0:T(8,128)(2,1)S(1)}, u32[]{:S(2)}, u32[]{:S(2)}) collective-permute-start(bf16[4,64,2304]{2,1,0:T(8,128)(2,1)S(1)} %pad_maximum_fusion), channel_id=1, source_target_pairs={{128,0},{256,128},{384,256},{0,384},{129,1},{257,129},{385,257},{1... | collective-permute-start | bytes 3538952 | tf_op jit(solution)/shard_map/ppermute | solution.py:15
  49.7 1.9 collective-permute-start.5
  51.6 13.5 %collective-permute-done.10 = bf16[4,64,2304]{2,1,0:T(8,128)(2,1)S(1)} collective-permute-done((bf16[4,64,2304]{2,1,0:T(8,128)(2,1)S(1)}, bf16[4,64,2304]{2,1,0:T(8,128)(2,1)S(1)}, u32[]{:S(2)}, u32[]{:S(2)}) %collective-permute-start.10) | collective-permute-done | bytes 1179680 | tf_op jit(solution)/shard_map/ppermute | solution.py:15
  65.2 5.3 %collective-permute-start.14 = (bf16[4,32,2304]{2,1,0:T(8,128)(2,1)S(1)}, bf16[4,32,2304]{2,1,0:T(8,128)(2,1)}, u32[]{:S(2)}, u32[]{:S(2)}) collective-permute-start(bf16[4,32,2304]{2,1,0:T(8,128)(2,1)S(1)} %slice.89), channel_id=1, source_target_pairs={{32,0},{64,32},{96,64},{0,96},{33,1},{65,33},{97,65},{1,97},{34,2}... | collective-permute-start | bytes 1769480 | tf_op jit(solution)/shard_map/ppermute | solution.py:15
  70.6 1.9 collective-permute-start.15
  72.6 4.8 %collective-permute-start.12 = (bf16[4,32,2304]{2,1,0:T(8,128)(2,1)S(1)}, bf16[4,32,2304]{2,1,0:T(8,128)(2,1)}, u32[]{:S(2)}, u32[]{:S(2)}) collective-permute-start(bf16[4,32,2304]{2,1,0:T(8,128)(2,1)S(1)} %slice.87), channel_id=1, source_target_pairs={{128,0},{256,128},{384,256},{0,384},{129,1},{257,129},{385,257},{1... | collective-permute-start | bytes 1769480 | tf_op jit(solution)/shard_map/ppermute | solution.py:15
  78.5 1.9 collective-permute-start.13
  80.5 3.9 %collective-permute-done.15 = bf16[4,32,2304]{2,1,0:T(8,128)(2,1)} collective-permute-done((bf16[4,32,2304]{2,1,0:T(8,128)(2,1)S(1)}, bf16[4,32,2304]{2,1,0:T(8,128)(2,1)}, u32[]{:S(2)}, u32[]{:S(2)}) %collective-permute-start.15) | collective-permute-done | bytes 589856 | tf_op jit(solution)/shard_map/ppermute | solution.py:15
  84.4 2.3 pad_maximum_fusion.3
  86.8 5.5 %collective-permute-done.13 = bf16[4,32,2304]{2,1,0:T(8,128)(2,1)} collective-permute-done((bf16[4,32,2304]{2,1,0:T(8,128)(2,1)S(1)}, bf16[4,32,2304]{2,1,0:T(8,128)(2,1)}, u32[]{:S(2)}, u32[]{:S(2)}) %collective-permute-start.13) | collective-permute-done | bytes 589856 | tf_op jit(solution)/shard_map/ppermute | solution.py:15
  92.2 2.4 pad_maximum_fusion.2
  94.6 15.4 %shard_map.86 = (bf16[1024,768]{1,0:T(8,128)(2,1)}, bf16[1024,2048]{1,0:T(8,128)(2,1)}) custom-call(bf16[1024,2176]{1,0:T(8,128)(2,1)} %all-gather.3.cloned.1.call-done.group_ref, f32[1,128]{1,0:T(1,128)S(1)} %or_convert_fusion.mask_ref, bf16[256,2304]{1,0:T(8,128)(2,1)S(1)} %bitcast.43, bf16[256,2304]{1,0:T(8,128)(2,1)} %bitcast.57, ...), custom_call_target="tpu_custom_call" | custom-call | flops 9663676416 | bytes 19398656 | tf_op jit(solution)/shard_map/pallas_call | solution.py:125
  110.0 2.7 constant_dynamic-slice_fusion.1
  112.7 7.1 %collective-permute-start.16 = (bf16[512,2048]{1,0:T(8,128)(2,1)S(1)}, bf16[512,2048]{1,0:T(8,128)(2,1)S(1)}, u32[]{:S(2)}, u32[]{:S(2)}) collective-permute-start(bf16[512,2048]{1,0:T(8,128)(2,1)S(1)} %bitcast.46), channel_id=1, source_target_pairs={{0,1},{1,0},{2,3},{3,2},{4,5},{5,4},{6,7},{7,6},{8,9},{9,8},{10,11... | collective-permute-start | bytes 6291464 | tf_op jit(solution)/shard_map/ppermute | solution.py:155
  119.9 3.8 %collective-permute-done.16 = bf16[512,2048]{1,0:T(8,128)(2,1)S(1)} collective-permute-done((bf16[512,2048]{1,0:T(8,128)(2,1)S(1)}, bf16[512,2048]{1,0:T(8,128)(2,1)S(1)}, u32[]{:S(2)}, u32[]{:S(2)}) %collective-permute-start.16) | collective-permute-done | bytes 2097184 | tf_op jit(solution)/shard_map/ppermute | solution.py:155
  123.6 2.3 fusion.1
  125.9 64.3 %reduce-scatter.2.cloned.1.call-done = bf16[32,2048]{1,0:T(8,128)(2,1)} async-done(((bf16[512,2048]{1,0:T(8,128)(2,1)}), bf16[32,2048]{1,0:T(8,128)(2,1)}) %reduce-scatter.2.cloned.1.call-update) | async-done | bytes 131088 | tf_op jit(solution)/shard_map/reduce_scatter | solution.py:157
  193.5 54.7 %all-gather.4 = f16[1024,2176]{1,0:T(8,128)(2,1)S(1)} all-gather(f16[32,2176]{1,0:T(8,128)(2,1)S(1)} %pad_maximum_fusion.5), channel_id=1, replica_groups=mesh['y'=4,'x'=4,'z'=16,'c'=2] {'z','c'}, dimensions={0}, use_global_device_ids=true | all-gather | bytes 4595712 | tf_op jit(solution)/shard_map/all_gather | solution.py:165
  248.5 4.2 %fusion.2 = bf16[2048,768]{1,0:T(8,128)(2,1)S(1)} fusion(f16[1024,2176]{1,0:T(8,128)(2,1)S(1)} %all-gather.4, bf16[1024,768]{1,0:T(8,128)(2,1)S(1)} %copy-done.12, f32[1024]{0:T(1024)S(1)} %exponential_reduce_fusion), kind=kOutput, calls=%fused_computation.4 | convolution fusion | flops 3227254784 | bytes 8916992 | tf_op jit(solution)/shard_map/dot_general | solution.py:167
  252.7 45.5 %all_to_all.5 = bf16[16,128,768]{2,1,0:T(8,128)(2,1)S(1)} all-to-all(bf16[16,128,768]{2,1,0:T(8,128)(2,1)S(1)} %bitcast.45), channel_id=1, replica_groups=mesh['y'=4,'x'=4,'z'=16,'c'=2] {'y','x'}, dimensions={0} | all-to-all | bytes 6291456 | tf_op jit(solution)/shard_map/all_to_all | solution.py:173
  298.1 1.1 reduce_sum.22
  (97 shorter events, 8.0 us)
Async XLA Ops:
  7.2 2.8 copy-start.9
  7.2 2.9 copy-start.10
  7.2 87.4 %all-gather.3.cloned.1.call-start = ((), (), s32[]{:S(2)}) async-start(), calls=%async_computation.2 | async-start | bytes 4595712 | tf_op jit(solution)/shard_map/all_gather | solution.py:109
  8.2 2.9 copy-start.6
  8.2 2.9 copy-start.7
  8.2 2.9 copy-start.8
  11.1 179.2 %reduce-scatter.2.cloned.1.call-start = ((), (), s32[]{:S(2)}) async-start(), calls=%async_computation.3 | async-start | bytes 2228224 | tf_op jit(solution)/shard_map/reduce_scatter | solution.py:157
  11.3 13.7 %collective-permute-start.6 = (bf16[64,2304]{1,0:T(8,128)(2,1)S(1)}, bf16[64,2304]{1,0:T(8,128)(2,1)S(1)}, u32[]{:S(2)}, u32[]{:S(2)}) collective-permute-start(bf16[64,2304]{1,0:T(8,128)(2,1)S(1)} %get-tuple-element.14), channel_id=1, source_target_pairs={{128,0},{256,128},{384,256},{0,384},{129,1},{257,129},{385,257},{1... | collective-permute-start | bytes 884744 | tf_op jit(solution)/shard_map/ppermute | solution.py:15
  16.8 12.9 %collective-permute-start.8 = (bf16[64,2304]{1,0:T(8,128)(2,1)S(1)}, bf16[64,2304]{1,0:T(8,128)(2,1)S(1)}, u32[]{:S(2)}, u32[]{:S(2)}) collective-permute-start(bf16[64,2304]{1,0:T(8,128)(2,1)S(1)} %get-tuple-element.14), channel_id=1, source_target_pairs={{384,0},{0,128},{128,256},{256,384},{385,1},{1,129},{129,257},{257... | collective-permute-start | bytes 884744 | tf_op jit(solution)/shard_map/ppermute | solution.py:15
  18.7 12.9 %collective-permute-start = (bf16[64,2304]{1,0:T(8,128)(2,1)S(1)}, bf16[64,2304]{1,0:T(8,128)(2,1)S(1)}, u32[]{:S(2)}, u32[]{:S(2)}) collective-permute-start(bf16[64,2304]{1,0:T(8,128)(2,1)S(1)} %get-tuple-element.15), channel_id=1, source_target_pairs={{32,0},{64,32},{96,64},{0,96},{33,1},{65,33},{97,65},{1,97},{34,2}... | collective-permute-start | bytes 884744 | tf_op jit(solution)/shard_map/ppermute | solution.py:15
  23.1 13.1 %collective-permute-start.2 = (bf16[64,2304]{1,0:T(8,128)(2,1)S(1)}, bf16[64,2304]{1,0:T(8,128)(2,1)S(1)}, u32[]{:S(2)}, u32[]{:S(2)}) collective-permute-start(bf16[64,2304]{1,0:T(8,128)(2,1)S(1)} %get-tuple-element.15), channel_id=1, source_target_pairs={{96,0},{0,32},{32,64},{64,96},{97,1},{1,33},{33,65},{65,97},{98,2}... | collective-permute-start | bytes 884744 | tf_op jit(solution)/shard_map/ppermute | solution.py:15
  25.1 13.1 %collective-permute-start.7 = (bf16[32,2304]{1,0:T(8,128)(2,1)S(1)}, bf16[32,2304]{1,0:T(8,128)(2,1)S(1)}, u32[]{:S(2)}, u32[]{:S(2)}) collective-permute-start(bf16[32,2304]{1,0:T(8,128)(2,1)S(1)} %slice.85), channel_id=1, source_target_pairs={{128,0},{256,128},{384,256},{0,384},{129,1},{257,129},{385,257},{1... | collective-permute-start | bytes 442376 | tf_op jit(solution)/shard_map/ppermute | solution.py:15
  29.7 8.5 %collective-permute-start.9 = (bf16[32,2304]{1,0:T(8,128)(2,1)S(1)}, bf16[32,2304]{1,0:T(8,128)(2,1)S(1)}, u32[]{:S(2)}, u32[]{:S(2)}) collective-permute-start(bf16[32,2304]{1,0:T(8,128)(2,1)S(1)} %slice.86), channel_id=1, source_target_pairs={{384,0},{0,128},{128,256},{256,384},{385,1},{1,129},{129,257},{257... | collective-permute-start | bytes 442376 | tf_op jit(solution)/shard_map/ppermute | solution.py:15
  31.6 13.3 %collective-permute-start.1 = (bf16[32,2304]{1,0:T(8,128)(2,1)S(1)}, bf16[32,2304]{1,0:T(8,128)(2,1)S(1)}, u32[]{:S(2)}, u32[]{:S(2)}) collective-permute-start(bf16[32,2304]{1,0:T(8,128)(2,1)S(1)} %slice.82), channel_id=1, source_target_pairs={{32,0},{64,32},{96,64},{0,96},{33,1},{65,33},{97,65},{1,97},{34,2}... | collective-permute-start | bytes 442376 | tf_op jit(solution)/shard_map/ppermute | solution.py:15
  36.3 8.7 %collective-permute-start.3 = (bf16[32,2304]{1,0:T(8,128)(2,1)S(1)}, bf16[32,2304]{1,0:T(8,128)(2,1)S(1)}, u32[]{:S(2)}, u32[]{:S(2)}) collective-permute-start(bf16[32,2304]{1,0:T(8,128)(2,1)S(1)} %slice.83), channel_id=1, source_target_pairs={{96,0},{0,32},{32,64},{64,96},{97,1},{1,33},{33,65},{65,97},{98,2}... | collective-permute-start | bytes 442376 | tf_op jit(solution)/shard_map/ppermute | solution.py:15
  38.4 26.8 %copy-start = (bf16[4,64,2304]{2,1,0:T(8,128)(2,1)}, bf16[4,64,2304]{2,1,0:T(8,128)(2,1)S(1)}, u32[]{:S(2)}) copy-start(bf16[4,64,2304]{2,1,0:T(8,128)(2,1)S(1)} %pad_maximum_fusion.1) | copy-start | bytes 3538948
  38.4 26.8 %collective-permute-start.10 = (bf16[4,64,2304]{2,1,0:T(8,128)(2,1)S(1)}, bf16[4,64,2304]{2,1,0:T(8,128)(2,1)S(1)}, u32[]{:S(2)}, u32[]{:S(2)}) collective-permute-start(bf16[4,64,2304]{2,1,0:T(8,128)(2,1)S(1)} %pad_maximum_fusion.1), channel_id=1, source_target_pairs={{32,0},{64,32},{96,64},{0,96},{33,1},{65,33},{97,65},{1,97},{34,2}... | collective-permute-start | bytes 3538952 | tf_op jit(solution)/shard_map/ppermute | solution.py:15
  43.0 27.6 %collective-permute-start.11 = (bf16[4,64,2304]{2,1,0:T(8,128)(2,1)S(1)}, bf16[4,64,2304]{2,1,0:T(8,128)(2,1)S(1)}, u32[]{:S(2)}, u32[]{:S(2)}) collective-permute-start(bf16[4,64,2304]{2,1,0:T(8,128)(2,1)S(1)} %pad_maximum_fusion.1), channel_id=1, source_target_pairs={{96,0},{0,32},{32,64},{64,96},{97,1},{1,33},{33,65},{65,97},{98,2}... | collective-permute-start | bytes 3538952 | tf_op jit(solution)/shard_map/ppermute | solution.py:15
  45.1 27.4 %collective-permute-start.4 = (bf16[4,64,2304]{2,1,0:T(8,128)(2,1)S(1)}, bf16[4,64,2304]{2,1,0:T(8,128)(2,1)S(1)}, u32[]{:S(2)}, u32[]{:S(2)}) collective-permute-start(bf16[4,64,2304]{2,1,0:T(8,128)(2,1)S(1)} %pad_maximum_fusion), channel_id=1, source_target_pairs={{128,0},{256,128},{384,256},{0,384},{129,1},{257,129},{385,257},{1... | collective-permute-start | bytes 3538952 | tf_op jit(solution)/shard_map/ppermute | solution.py:15
  49.7 27.7 %collective-permute-start.5 = (bf16[4,64,2304]{2,1,0:T(8,128)(2,1)S(1)}, bf16[4,64,2304]{2,1,0:T(8,128)(2,1)S(1)}, u32[]{:S(2)}, u32[]{:S(2)}) collective-permute-start(bf16[4,64,2304]{2,1,0:T(8,128)(2,1)S(1)} %pad_maximum_fusion), channel_id=1, source_target_pairs={{384,0},{0,128},{128,256},{256,384},{385,1},{1,129},{129,257},{257... | collective-permute-start | bytes 3538952 | tf_op jit(solution)/shard_map/ppermute | solution.py:15
  65.2 7.5 %copy-start.2 = (bf16[4,64,2304]{2,1,0:T(8,128)(2,1)}, bf16[4,64,2304]{2,1,0:T(8,128)(2,1)S(1)}, u32[]{:S(2)}) copy-start(bf16[4,64,2304]{2,1,0:T(8,128)(2,1)S(1)} %collective-permute-done.10) | copy-start | bytes 3538948
  65.2 15.2 %collective-permute-start.14 = (bf16[4,32,2304]{2,1,0:T(8,128)(2,1)S(1)}, bf16[4,32,2304]{2,1,0:T(8,128)(2,1)}, u32[]{:S(2)}, u32[]{:S(2)}) collective-permute-start(bf16[4,32,2304]{2,1,0:T(8,128)(2,1)S(1)} %slice.89), channel_id=1, source_target_pairs={{32,0},{64,32},{96,64},{0,96},{33,1},{65,33},{97,65},{1,97},{34,2}... | collective-permute-start | bytes 1769480 | tf_op jit(solution)/shard_map/ppermute | solution.py:15
  70.6 7.0 %copy-start.3 = (bf16[4,64,2304]{2,1,0:T(8,128)(2,1)}, bf16[4,64,2304]{2,1,0:T(8,128)(2,1)S(1)}, u32[]{:S(2)}) copy-start(bf16[4,64,2304]{2,1,0:T(8,128)(2,1)S(1)} %collective-permute-done.11) | copy-start | bytes 3538948
  70.6 13.8 %collective-permute-start.15 = (bf16[4,32,2304]{2,1,0:T(8,128)(2,1)S(1)}, bf16[4,32,2304]{2,1,0:T(8,128)(2,1)}, u32[]{:S(2)}, u32[]{:S(2)}) collective-permute-start(bf16[4,32,2304]{2,1,0:T(8,128)(2,1)S(1)} %slice.90), channel_id=1, source_target_pairs={{96,0},{0,32},{32,64},{64,96},{97,1},{1,33},{33,65},{65,97},{98,2}... | collective-permute-start | bytes 1769480 | tf_op jit(solution)/shard_map/ppermute | solution.py:15
  72.6 4.9 %copy-start.4 = (bf16[4,64,2304]{2,1,0:T(8,128)(2,1)}, bf16[4,64,2304]{2,1,0:T(8,128)(2,1)S(1)}, u32[]{:S(2)}) copy-start(bf16[4,64,2304]{2,1,0:T(8,128)(2,1)S(1)} %collective-permute-done.4) | copy-start | bytes 3538948
  72.6 14.1 %collective-permute-start.12 = (bf16[4,32,2304]{2,1,0:T(8,128)(2,1)S(1)}, bf16[4,32,2304]{2,1,0:T(8,128)(2,1)}, u32[]{:S(2)}, u32[]{:S(2)}) collective-permute-start(bf16[4,32,2304]{2,1,0:T(8,128)(2,1)S(1)} %slice.87), channel_id=1, source_target_pairs={{128,0},{256,128},{384,256},{0,384},{129,1},{257,129},{385,257},{1... | collective-permute-start | bytes 1769480 | tf_op jit(solution)/shard_map/ppermute | solution.py:15
  77.5 1.0 copy-start.5
  78.5 13.7 %collective-permute-start.13 = (bf16[4,32,2304]{2,1,0:T(8,128)(2,1)S(1)}, bf16[4,32,2304]{2,1,0:T(8,128)(2,1)}, u32[]{:S(2)}, u32[]{:S(2)}) collective-permute-start(bf16[4,32,2304]{2,1,0:T(8,128)(2,1)S(1)} %slice.88), channel_id=1, source_target_pairs={{384,0},{0,128},{128,256},{256,384},{385,1},{1,129},{129,257},{257... | collective-permute-start | bytes 1769480 | tf_op jit(solution)/shard_map/ppermute | solution.py:15
  112.7 10.9 %collective-permute-start.16 = (bf16[512,2048]{1,0:T(8,128)(2,1)S(1)}, bf16[512,2048]{1,0:T(8,128)(2,1)S(1)}, u32[]{:S(2)}, u32[]{:S(2)}) collective-permute-start(bf16[512,2048]{1,0:T(8,128)(2,1)S(1)} %bitcast.46), channel_id=1, source_target_pairs={{0,1},{1,0},{2,3},{3,2},{4,5},{5,4},{6,7},{7,6},{8,9},{9,8},{10,11... | collective-permute-start | bytes 6291464 | tf_op jit(solution)/shard_map/ppermute | solution.py:155
  125.9 66.7 %copy-start.11 = (f32[32]{0:T(128)S(1)}, f32[32]{0:T(128)}, u32[]{:S(2)}) copy-start(f32[32]{0:T(128)} %param.10) | copy-start | bytes 388
  193.2 55.0 %copy-start.1 = (bf16[32,2048]{1,0:T(8,128)(2,1)}, bf16[32,2048]{1,0:T(8,128)(2,1)S(1)}, u32[]{:S(2)}) copy-start(bf16[32,2048]{1,0:T(8,128)(2,1)S(1)} %reshape.140) | copy-start | bytes 393220
  193.5 55.0 %copy-start.12 = (bf16[1024,768]{1,0:T(8,128)(2,1)S(1)}, bf16[1024,768]{1,0:T(8,128)(2,1)}, u32[]{:S(2)}) copy-start(bf16[1024,768]{1,0:T(8,128)(2,1)} %get-tuple-element.5) | copy-start | bytes 4718596
Sparse Core Ops, SparseCore 0:
  11.2 80.2 all-gather.2
  126.0 64.1 reduce-scatter.1

commit v9 on v8

--- a/solution.py
+++ b/solution.py
@@ -57,32 +57,41 @@
     return turn(turn(both, 1, (4 - y) % 4), 2, (4 - x) % 4).reshape(rows, width)
 
 
-def expert_kernel(size, group_ref, mask_ref, *refs):
-    pieces, hidden_ref, tangent_ref = refs[:-2], refs[-2], refs[-1]
+def expert_kernel(size, whole, group_ref, mask_ref, *refs):
+    hidden_ref, tangent_ref = refs[-2], refs[-1]
+    pieces = [(ref,) for ref in refs[:whole]]
+    pieces += [refs[i : i + 2] for i in range(whole, len(refs) - 2, 2)]
+    depth = pieces[0][0].shape[0]
+
+    def matrix(piece, which):
+        columns = slice(which * size, (which + 1) * size)
+        if len(piece) == 1:
+            return piece[0][:, columns]
+        step = depth // 8
+        return jnp.concatenate(
+            [ref[i * step : (i + 1) * step, columns] for i in range(4) for ref in piece]
+        )
+
     gate = jnp.zeros((group_ref.shape[0], size), F32)
     up = jnp.zeros((group_ref.shape[0], size), F32)
-    start = 0
-    for piece in pieces:
-        depth = piece.shape[0]
-        rows = group_ref[:, start : start + depth]
-        gate += jnp.dot(rows, piece[:, :size], preferred_element_type=F32)
-        up += jnp.dot(rows, piece[:, size : 2 * size], preferred_element_type=F32)
-        start += depth
+    for i, piece in enumerate(pieces):
+        rows = group_ref[:, i * depth : (i + 1) * depth]
+        gate += jnp.dot(rows, matrix(piece, 0), preferred_element_type=F32)
+        up += jnp.dot(rows, matrix(piece, 1), preferred_element_type=F32)
     share = jnp.sum(
-        group_ref[:, start:].astype(F32) * mask_ref[...], axis=1, keepdims=True
+        group_ref[:, len(pieces) * depth :].astype(F32) * mask_ref[...],
+        axis=1,
+        keepdims=True,
     )
     hidden = (jax.nn.silu(gate) * up * share).astype(BF)
     hidden_ref[...] = hidden
-    start = 0
-    for piece in pieces:
-        depth = piece.shape[0]
-        tangent_ref[:, start : start + depth] = lax.dot_general(
+    for i, piece in enumerate(pieces):
+        tangent_ref[:, i * depth : (i + 1) * depth] = lax.dot_general(
             hidden,
-            piece[:, 2 * size :],
+            matrix(piece, 2),
             (((1,), (1,)), ((), ())),
             preferred_element_type=F32,
         ).astype(BF)
-        start += depth
 
 
 def local(tokens, routes, gates, curvature, w_gate, w_up, direction):
@@ -113,17 +122,18 @@
     first_soon, first_late = ring4(ring4_stack(stacked[:half], "x"), "y")
     second_soon, second_late = ring4(ring4_stack(stacked[half:], "y"), "x")
     columns = stacked.shape[1]
-    late = [
-        jnp.concatenate(pair, -2).reshape(-1, columns) for pair in (first_late, second_late)
+    pieces = [
+        p.reshape(-1, columns)
+        for p in first_soon + second_soon + first_late + second_late
     ]
-    pieces = [p.reshape(-1, columns) for p in first_soon + second_soon] + late
+    whole = len(first_soon) + len(second_soon)
 
     lanes = lax.broadcasted_iota(jnp.int32, (1, 128), 1)
     mask = ((lanes == me) | (lanes == me + experts)).astype(F32)
     count, wide = arrived.shape
     block = count // 4
     hidden, tangents = pl.pallas_call(
-        functools.partial(expert_kernel, hidden_width),
+        functools.partial(expert_kernel, hidden_width, whole),
         grid=(4,),
         in_specs=[
             pl.BlockSpec((block, wide), lambda i: (i, 0)),

time: 307 us -> 304 us (level)
  other arithmetic: 10.5 us -> 5.74 us
    concatenate x2 -> x0, other arithmetic: 4.73 us -> none  [local(): jnp.concatenate(pair, -2).reshape(-1, columns)]
  transfers between devices with their start and end apart: 19 -> 19, of which waited for: 5 -> 6; matrix products, arithmetic and copies ran while one was open for 2% -> 1% of each run, Pallas kernels for 0% -> 0%
where the time goes in v9:
time: 304 us; the launch traced here: 303 us
  blocking collectives  99.7 us (33%)
  waiting for transfers between devices  93.5 us (31%)
  starting transfers between devices  60.8 us (20%)
  Pallas kernels  15.1 us (5%)
  between operations  14.8 us (5%)
  local copies, waits for them, and re-layouts  9.38 us (3%)
  other arithmetic  5.74 us (2%)
  matrix products  4.17 us (1%)
    reduce_scatter x1, waiting for transfers between devices, local(): jv = lax.psum_scatter(paired, 'z', scatter_dimension=0, tiled=True)  64.3 us
    all_gather x1, blocking collectives, local(): spread = lax.all_gather(scaled, ('z', 'c'), axis=0, tiled=True)  54.5 us
    ppermute x16, starting transfers between devices, fetch(): lax.ppermute(value, axis, [((i + shift) % size, i) for i in range(size)])  53.6 us
    all_to_all x1, blocking collectives, local(): lax.all_to_all(part.reshape(16, -1, hidden_width), ('y', 'x'), 0, 0, tile...  45.1 us
    ppermute x16, waiting for transfers between devices, fetch(): lax.ppermute(value, axis, [((i + shift) % size, i) for i in range(size)])  25.4 us
    pallas_call x1, Pallas kernels, local(): pl.pallas_call(functools.partial(expert_kernel, hidden_width, whole), gri...  15.1 us
    ppermute x1, starting transfers between devices, local(): other = lax.ppermute(away, 'c', [(0, 1), (1, 0)])  7.13 us
  transfers between devices with their start and end apart: 19, of which 6 were waited for; matrix products, arithmetic and copies ran while one was open for 1% of the time, Pallas kernels for 0%

profile of v9, /device:TPU:1, one launch (start us, length us, event | category | flops | bytes accessed | tf_op | source)
XLA Modules:
  0.0 303.3 jit_solution(13421663325291672277)
XLA Ops:
  7.2 1.0 reshape.127
  11.3 5.5 %collective-permute-start.6 = (bf16[64,2304]{1,0:T(8,128)(2,1)S(1)}, bf16[64,2304]{1,0:T(8,128)(2,1)S(1)}, u32[]{:S(2)}, u32[]{:S(2)}) collective-permute-start(bf16[64,2304]{1,0:T(8,128)(2,1)S(1)} %get-tuple-element.14), channel_id=1, source_target_pairs={{128,0},{256,128},{384,256},{0,384},{129,1},{257,129},{385,257},{1... | collective-permute-start | bytes 884744 | tf_op jit(solution)/shard_map/ppermute | solution.py:15
  16.8 1.9 collective-permute-start.8
  18.7 4.4 %collective-permute-start = (bf16[64,2304]{1,0:T(8,128)(2,1)S(1)}, bf16[64,2304]{1,0:T(8,128)(2,1)S(1)}, u32[]{:S(2)}, u32[]{:S(2)}) collective-permute-start(bf16[64,2304]{1,0:T(8,128)(2,1)S(1)} %get-tuple-element.15), channel_id=1, source_target_pairs={{32,0},{64,32},{96,64},{0,96},{33,1},{65,33},{97,65},{1,97},{34,2}... | collective-permute-start | bytes 884744 | tf_op jit(solution)/shard_map/ppermute | solution.py:15
  23.1 1.9 collective-permute-start.2
  25.1 4.6 %collective-permute-start.7 = (bf16[32,2304]{1,0:T(8,128)(2,1)S(1)}, bf16[32,2304]{1,0:T(8,128)(2,1)S(1)}, u32[]{:S(2)}, u32[]{:S(2)}) collective-permute-start(bf16[32,2304]{1,0:T(8,128)(2,1)S(1)} %slice.85), channel_id=1, source_target_pairs={{128,0},{256,128},{384,256},{0,384},{129,1},{257,129},{385,257},{1... | collective-permute-start | bytes 442376 | tf_op jit(solution)/shard_map/ppermute | solution.py:15
  29.7 1.9 collective-permute-start.9
  31.6 4.6 %collective-permute-start.1 = (bf16[32,2304]{1,0:T(8,128)(2,1)S(1)}, bf16[32,2304]{1,0:T(8,128)(2,1)S(1)}, u32[]{:S(2)}, u32[]{:S(2)}) collective-permute-start(bf16[32,2304]{1,0:T(8,128)(2,1)S(1)} %slice.82), channel_id=1, source_target_pairs={{32,0},{64,32},{96,64},{0,96},{33,1},{65,33},{97,65},{1,97},{34,2}... | collective-permute-start | bytes 442376 | tf_op jit(solution)/shard_map/ppermute | solution.py:15
  36.3 1.9 collective-permute-start.3
  38.4 4.6 %collective-permute-start.10 = (bf16[4,64,2304]{2,1,0:T(8,128)(2,1)S(1)}, bf16[4,64,2304]{2,1,0:T(8,128)(2,1)S(1)}, u32[]{:S(2)}, u32[]{:S(2)}) collective-permute-start(bf16[4,64,2304]{2,1,0:T(8,128)(2,1)S(1)} %pad_maximum_fusion.1), channel_id=1, source_target_pairs={{32,0},{64,32},{96,64},{0,96},{33,1},{65,33},{97,65},{1,97},{34,2}... | collective-permute-start | bytes 3538952 | tf_op jit(solution)/shard_map/ppermute | solution.py:15
  43.0 1.9 collective-permute-start.11
  45.1 4.6 %collective-permute-start.4 = (bf16[4,64,2304]{2,1,0:T(8,128)(2,1)S(1)}, bf16[4,64,2304]{2,1,0:T(8,128)(2,1)S(1)}, u32[]{:S(2)}, u32[]{:S(2)}) collective-permute-start(bf16[4,64,2304]{2,1,0:T(8,128)(2,1)S(1)} %pad_maximum_fusion), channel_id=1, source_target_pairs={{128,0},{256,128},{384,256},{0,384},{129,1},{257,129},{385,257},{1... | collective-permute-start | bytes 3538952 | tf_op jit(solution)/shard_map/ppermute | solution.py:15
  49.7 1.9 collective-permute-start.5
  51.6 13.5 %collective-permute-done.10 = bf16[4,64,2304]{2,1,0:T(8,128)(2,1)S(1)} collective-permute-done((bf16[4,64,2304]{2,1,0:T(8,128)(2,1)S(1)}, bf16[4,64,2304]{2,1,0:T(8,128)(2,1)S(1)}, u32[]{:S(2)}, u32[]{:S(2)}) %collective-permute-start.10) | collective-permute-done | bytes 1179680 | tf_op jit(solution)/shard_map/ppermute | solution.py:15
  65.2 5.3 %collective-permute-start.14 = (bf16[4,32,2304]{2,1,0:T(8,128)(2,1)S(1)}, bf16[4,32,2304]{2,1,0:T(8,128)(2,1)S(1)}, u32[]{:S(2)}, u32[]{:S(2)}) collective-permute-start(bf16[4,32,2304]{2,1,0:T(8,128)(2,1)S(1)} %slice.89), channel_id=1, source_target_pairs={{32,0},{64,32},{96,64},{0,96},{33,1},{65,33},{97,65},{1,97},{34,2}... | collective-permute-start | bytes 1769480 | tf_op jit(solution)/shard_map/ppermute | solution.py:15
  70.6 1.9 collective-permute-start.15
  72.7 4.8 %collective-permute-start.12 = (bf16[4,32,2304]{2,1,0:T(8,128)(2,1)S(1)}, bf16[4,32,2304]{2,1,0:T(8,128)(2,1)S(1)}, u32[]{:S(2)}, u32[]{:S(2)}) collective-permute-start(bf16[4,32,2304]{2,1,0:T(8,128)(2,1)S(1)} %slice.87), channel_id=1, source_target_pairs={{128,0},{256,128},{384,256},{0,384},{129,1},{257,129},{385,257},{1... | collective-permute-start | bytes 1769480 | tf_op jit(solution)/shard_map/ppermute | solution.py:15
  77.5 0.9 slice.88
  78.7 1.9 collective-permute-start.13
  80.6 3.8 %collective-permute-done.15 = bf16[4,32,2304]{2,1,0:T(8,128)(2,1)} collective-permute-done((bf16[4,32,2304]{2,1,0:T(8,128)(2,1)S(1)}, bf16[4,32,2304]{2,1,0:T(8,128)(2,1)}, u32[]{:S(2)}, u32[]{:S(2)}) %collective-permute-start.15) | collective-permute-done | bytes 589856 | tf_op jit(solution)/shard_map/ppermute | solution.py:15
  84.4 1.6 collective-permute-done.12
  86.0 6.5 %collective-permute-done.13 = bf16[4,32,2304]{2,1,0:T(8,128)(2,1)S(1)} collective-permute-done((bf16[4,32,2304]{2,1,0:T(8,128)(2,1)}, bf16[4,32,2304]{2,1,0:T(8,128)(2,1)S(1)}, u32[]{:S(2)}, u32[]{:S(2)}) %collective-permute-start.13) | collective-permute-done | bytes 589856 | tf_op jit(solution)/shard_map/ppermute | solution.py:15
  92.5 15.1 %shard_map.86 = (bf16[1024,768]{1,0:T(8,128)(2,1)}, bf16[1024,2048]{1,0:T(8,128)(2,1)}) custom-call(bf16[1024,2176]{1,0:T(8,128)(2,1)} %all-gather.3.cloned.1.call-done.group_ref, f32[1,128]{1,0:T(1,128)S(1)} %or_convert_fusion.mask_ref, bf16[256,2304]{1,0:T(8,128)(2,1)} %bitcast.52, bf16[256,2304]{1,0:T(8,128)(2,1)} %bitcast.60, ...), custom_call_target="tpu_custom_call" | custom-call | flops 9663676416 | bytes 19398656 | tf_op jit(solution)/shard_map/pallas_call | solution.py:135
  107.7 2.7 constant_dynamic-slice_fusion.1
  110.4 7.1 %collective-permute-start.16 = (bf16[512,2048]{1,0:T(8,128)(2,1)S(1)}, bf16[512,2048]{1,0:T(8,128)(2,1)S(1)}, u32[]{:S(2)}, u32[]{:S(2)}) collective-permute-start(bf16[512,2048]{1,0:T(8,128)(2,1)S(1)} %bitcast.50), channel_id=1, source_target_pairs={{0,1},{1,0},{2,3},{3,2},{4,5},{5,4},{6,7},{7,6},{8,9},{9,8},{10,11... | collective-permute-start | bytes 6291464 | tf_op jit(solution)/shard_map/ppermute | solution.py:165
  117.5 3.8 %collective-permute-done.16 = bf16[512,2048]{1,0:T(8,128)(2,1)S(1)} collective-permute-done((bf16[512,2048]{1,0:T(8,128)(2,1)S(1)}, bf16[512,2048]{1,0:T(8,128)(2,1)S(1)}, u32[]{:S(2)}, u32[]{:S(2)}) %collective-permute-start.16) | collective-permute-done | bytes 2097184 | tf_op jit(solution)/shard_map/ppermute | solution.py:165
  121.3 2.3 fusion.1
  123.6 64.3 %reduce-scatter.2.cloned.1.call-done = bf16[32,2048]{1,0:T(8,128)(2,1)} async-done(((bf16[512,2048]{1,0:T(8,128)(2,1)}), bf16[32,2048]{1,0:T(8,128)(2,1)}) %reduce-scatter.2.cloned.1.call-update) | async-done | bytes 131088 | tf_op jit(solution)/shard_map/reduce_scatter | solution.py:167
  191.2 54.5 %all-gather.4 = f16[1024,2176]{1,0:T(8,128)(2,1)S(1)} all-gather(f16[32,2176]{1,0:T(8,128)(2,1)S(1)} %pad_maximum_fusion.3), channel_id=1, replica_groups=mesh['y'=4,'x'=4,'z'=16,'c'=2] {'z','c'}, dimensions={0}, use_global_device_ids=true | all-gather | bytes 4595712 | tf_op jit(solution)/shard_map/all_gather | solution.py:175
  246.0 4.2 %fusion.2 = bf16[2048,768]{1,0:T(8,128)(2,1)S(1)} fusion(f16[1024,2176]{1,0:T(8,128)(2,1)S(1)} %all-gather.4, bf16[1024,768]{1,0:T(8,128)(2,1)S(1)} %copy-done.13, f32[1024]{0:T(1024)S(1)} %exponential_reduce_fusion), kind=kOutput, calls=%fused_computation.4 | convolution fusion | flops 3227254784 | bytes 8916992 | tf_op jit(solution)/shard_map/dot_general | solution.py:177
  250.2 45.1 %all_to_all.5 = bf16[16,128,768]{2,1,0:T(8,128)(2,1)S(1)} all-to-all(bf16[16,128,768]{2,1,0:T(8,128)(2,1)S(1)} %bitcast.49), channel_id=1, replica_groups=mesh['y'=4,'x'=4,'z'=16,'c'=2] {'y','x'}, dimensions={0} | all-to-all | bytes 6291456 | tf_op jit(solution)/shard_map/all_to_all | solution.py:183
  295.3 1.1 reduce_sum.22
  (97 shorter events, 7.2 us)
Async XLA Ops:
  7.2 2.8 copy-start.10
  7.2 2.9 copy-start.11
  7.2 85.3 %all-gather.3.cloned.1.call-start = ((), (), s32[]{:S(2)}) async-start(), calls=%async_computation.2 | async-start | bytes 4595712 | tf_op jit(solution)/shard_map/all_gather | solution.py:118
  8.2 2.9 copy-start.7
  8.2 2.9 copy-start.8
  8.2 2.9 copy-start.9
  11.1 176.8 %reduce-scatter.2.cloned.1.call-start = ((), (), s32[]{:S(2)}) async-start(), calls=%async_computation.3 | async-start | bytes 2228224 | tf_op jit(solution)/shard_map/reduce_scatter | solution.py:167
  11.3 13.7 %collective-permute-start.6 = (bf16[64,2304]{1,0:T(8,128)(2,1)S(1)}, bf16[64,2304]{1,0:T(8,128)(2,1)S(1)}, u32[]{:S(2)}, u32[]{:S(2)}) collective-permute-start(bf16[64,2304]{1,0:T(8,128)(2,1)S(1)} %get-tuple-element.14), channel_id=1, source_target_pairs={{128,0},{256,128},{384,256},{0,384},{129,1},{257,129},{385,257},{1... | collective-permute-start | bytes 884744 | tf_op jit(solution)/shard_map/ppermute | solution.py:15
  16.8 12.9 %collective-permute-start.8 = (bf16[64,2304]{1,0:T(8,128)(2,1)S(1)}, bf16[64,2304]{1,0:T(8,128)(2,1)S(1)}, u32[]{:S(2)}, u32[]{:S(2)}) collective-permute-start(bf16[64,2304]{1,0:T(8,128)(2,1)S(1)} %get-tuple-element.14), channel_id=1, source_target_pairs={{384,0},{0,128},{128,256},{256,384},{385,1},{1,129},{129,257},{257... | collective-permute-start | bytes 884744 | tf_op jit(solution)/shard_map/ppermute | solution.py:15
  18.7 12.9 %collective-permute-start = (bf16[64,2304]{1,0:T(8,128)(2,1)S(1)}, bf16[64,2304]{1,0:T(8,128)(2,1)S(1)}, u32[]{:S(2)}, u32[]{:S(2)}) collective-permute-start(bf16[64,2304]{1,0:T(8,128)(2,1)S(1)} %get-tuple-element.15), channel_id=1, source_target_pairs={{32,0},{64,32},{96,64},{0,96},{33,1},{65,33},{97,65},{1,97},{34,2}... | collective-permute-start | bytes 884744 | tf_op jit(solution)/shard_map/ppermute | solution.py:15
  23.1 13.1 %collective-permute-start.2 = (bf16[64,2304]{1,0:T(8,128)(2,1)S(1)}, bf16[64,2304]{1,0:T(8,128)(2,1)S(1)}, u32[]{:S(2)}, u32[]{:S(2)}) collective-permute-start(bf16[64,2304]{1,0:T(8,128)(2,1)S(1)} %get-tuple-element.15), channel_id=1, source_target_pairs={{96,0},{0,32},{32,64},{64,96},{97,1},{1,33},{33,65},{65,97},{98,2}... | collective-permute-start | bytes 884744 | tf_op jit(solution)/shard_map/ppermute | solution.py:15
  25.1 13.1 %collective-permute-start.7 = (bf16[32,2304]{1,0:T(8,128)(2,1)S(1)}, bf16[32,2304]{1,0:T(8,128)(2,1)S(1)}, u32[]{:S(2)}, u32[]{:S(2)}) collective-permute-start(bf16[32,2304]{1,0:T(8,128)(2,1)S(1)} %slice.85), channel_id=1, source_target_pairs={{128,0},{256,128},{384,256},{0,384},{129,1},{257,129},{385,257},{1... | collective-permute-start | bytes 442376 | tf_op jit(solution)/shard_map/ppermute | solution.py:15
  29.7 8.5 %collective-permute-start.9 = (bf16[32,2304]{1,0:T(8,128)(2,1)S(1)}, bf16[32,2304]{1,0:T(8,128)(2,1)S(1)}, u32[]{:S(2)}, u32[]{:S(2)}) collective-permute-start(bf16[32,2304]{1,0:T(8,128)(2,1)S(1)} %slice.86), channel_id=1, source_target_pairs={{384,0},{0,128},{128,256},{256,384},{385,1},{1,129},{129,257},{257... | collective-permute-start | bytes 442376 | tf_op jit(solution)/shard_map/ppermute | solution.py:15
  31.6 13.3 %collective-permute-start.1 = (bf16[32,2304]{1,0:T(8,128)(2,1)S(1)}, bf16[32,2304]{1,0:T(8,128)(2,1)S(1)}, u32[]{:S(2)}, u32[]{:S(2)}) collective-permute-start(bf16[32,2304]{1,0:T(8,128)(2,1)S(1)} %slice.82), channel_id=1, source_target_pairs={{32,0},{64,32},{96,64},{0,96},{33,1},{65,33},{97,65},{1,97},{34,2}... | collective-permute-start | bytes 442376 | tf_op jit(solution)/shard_map/ppermute | solution.py:15
  36.3 8.7 %collective-permute-start.3 = (bf16[32,2304]{1,0:T(8,128)(2,1)S(1)}, bf16[32,2304]{1,0:T(8,128)(2,1)S(1)}, u32[]{:S(2)}, u32[]{:S(2)}) collective-permute-start(bf16[32,2304]{1,0:T(8,128)(2,1)S(1)} %slice.83), channel_id=1, source_target_pairs={{96,0},{0,32},{32,64},{64,96},{97,1},{1,33},{33,65},{65,97},{98,2}... | collective-permute-start | bytes 442376 | tf_op jit(solution)/shard_map/ppermute | solution.py:15
  38.4 26.8 %copy-start = (bf16[4,64,2304]{2,1,0:T(8,128)(2,1)}, bf16[4,64,2304]{2,1,0:T(8,128)(2,1)S(1)}, u32[]{:S(2)}) copy-start(bf16[4,64,2304]{2,1,0:T(8,128)(2,1)S(1)} %pad_maximum_fusion.1) | copy-start | bytes 3538948
  38.4 26.8 %collective-permute-start.10 = (bf16[4,64,2304]{2,1,0:T(8,128)(2,1)S(1)}, bf16[4,64,2304]{2,1,0:T(8,128)(2,1)S(1)}, u32[]{:S(2)}, u32[]{:S(2)}) collective-permute-start(bf16[4,64,2304]{2,1,0:T(8,128)(2,1)S(1)} %pad_maximum_fusion.1), channel_id=1, source_target_pairs={{32,0},{64,32},{96,64},{0,96},{33,1},{65,33},{97,65},{1,97},{34,2}... | collective-permute-start | bytes 3538952 | tf_op jit(solution)/shard_map/ppermute | solution.py:15
  43.0 27.6 %collective-permute-start.11 = (bf16[4,64,2304]{2,1,0:T(8,128)(2,1)S(1)}, bf16[4,64,2304]{2,1,0:T(8,128)(2,1)S(1)}, u32[]{:S(2)}, u32[]{:S(2)}) collective-permute-start(bf16[4,64,2304]{2,1,0:T(8,128)(2,1)S(1)} %pad_maximum_fusion.1), channel_id=1, source_target_pairs={{96,0},{0,32},{32,64},{64,96},{97,1},{1,33},{33,65},{65,97},{98,2}... | collective-permute-start | bytes 3538952 | tf_op jit(solution)/shard_map/ppermute | solution.py:15
  45.1 27.5 %copy-start.1 = (bf16[4,64,2304]{2,1,0:T(8,128)(2,1)}, bf16[4,64,2304]{2,1,0:T(8,128)(2,1)S(1)}, u32[]{:S(2)}) copy-start(bf16[4,64,2304]{2,1,0:T(8,128)(2,1)S(1)} %pad_maximum_fusion) | copy-start | bytes 3538948
  45.1 27.4 %collective-permute-start.4 = (bf16[4,64,2304]{2,1,0:T(8,128)(2,1)S(1)}, bf16[4,64,2304]{2,1,0:T(8,128)(2,1)S(1)}, u32[]{:S(2)}, u32[]{:S(2)}) collective-permute-start(bf16[4,64,2304]{2,1,0:T(8,128)(2,1)S(1)} %pad_maximum_fusion), channel_id=1, source_target_pairs={{128,0},{256,128},{384,256},{0,384},{129,1},{257,129},{385,257},{1... | collective-permute-start | bytes 3538952 | tf_op jit(solution)/shard_map/ppermute | solution.py:15
  49.7 27.8 %collective-permute-start.5 = (bf16[4,64,2304]{2,1,0:T(8,128)(2,1)S(1)}, bf16[4,64,2304]{2,1,0:T(8,128)(2,1)S(1)}, u32[]{:S(2)}, u32[]{:S(2)}) collective-permute-start(bf16[4,64,2304]{2,1,0:T(8,128)(2,1)S(1)} %pad_maximum_fusion), channel_id=1, source_target_pairs={{384,0},{0,128},{128,256},{256,384},{385,1},{1,129},{129,257},{257... | collective-permute-start | bytes 3538952 | tf_op jit(solution)/shard_map/ppermute | solution.py:15
  65.2 7.5 %copy-start.3 = (bf16[4,64,2304]{2,1,0:T(8,128)(2,1)}, bf16[4,64,2304]{2,1,0:T(8,128)(2,1)S(1)}, u32[]{:S(2)}) copy-start(bf16[4,64,2304]{2,1,0:T(8,128)(2,1)S(1)} %collective-permute-done.10) | copy-start | bytes 3538948
  65.2 15.4 %collective-permute-start.14 = (bf16[4,32,2304]{2,1,0:T(8,128)(2,1)S(1)}, bf16[4,32,2304]{2,1,0:T(8,128)(2,1)S(1)}, u32[]{:S(2)}, u32[]{:S(2)}) collective-permute-start(bf16[4,32,2304]{2,1,0:T(8,128)(2,1)S(1)} %slice.89), channel_id=1, source_target_pairs={{32,0},{64,32},{96,64},{0,96},{33,1},{65,33},{97,65},{1,97},{34,2}... | collective-permute-start | bytes 1769480 | tf_op jit(solution)/shard_map/ppermute | solution.py:15
  70.6 2.0 copy-start.4
  70.6 13.8 %collective-permute-start.15 = (bf16[4,32,2304]{2,1,0:T(8,128)(2,1)S(1)}, bf16[4,32,2304]{2,1,0:T(8,128)(2,1)}, u32[]{:S(2)}, u32[]{:S(2)}) collective-permute-start(bf16[4,32,2304]{2,1,0:T(8,128)(2,1)S(1)} %slice.90), channel_id=1, source_target_pairs={{96,0},{0,32},{32,64},{64,96},{97,1},{1,33},{33,65},{65,97},{98,2}... | collective-permute-start | bytes 1769480 | tf_op jit(solution)/shard_map/ppermute | solution.py:15
  72.6 4.9 %copy-start.5 = (bf16[4,64,2304]{2,1,0:T(8,128)(2,1)}, bf16[4,64,2304]{2,1,0:T(8,128)(2,1)S(1)}, u32[]{:S(2)}) copy-start(bf16[4,64,2304]{2,1,0:T(8,128)(2,1)S(1)} %collective-permute-done.4) | copy-start | bytes 3538948
  72.7 13.4 %collective-permute-start.12 = (bf16[4,32,2304]{2,1,0:T(8,128)(2,1)S(1)}, bf16[4,32,2304]{2,1,0:T(8,128)(2,1)S(1)}, u32[]{:S(2)}, u32[]{:S(2)}) collective-permute-start(bf16[4,32,2304]{2,1,0:T(8,128)(2,1)S(1)} %slice.87), channel_id=1, source_target_pairs={{128,0},{256,128},{384,256},{0,384},{129,1},{257,129},{385,257},{1... | collective-permute-start | bytes 1769480 | tf_op jit(solution)/shard_map/ppermute | solution.py:15
  78.7 13.8 %collective-permute-start.13 = (bf16[4,32,2304]{2,1,0:T(8,128)(2,1)}, bf16[4,32,2304]{2,1,0:T(8,128)(2,1)S(1)}, u32[]{:S(2)}, u32[]{:S(2)}) collective-permute-start(bf16[4,32,2304]{2,1,0:T(8,128)(2,1)} %slice.88), channel_id=1, source_target_pairs={{384,0},{0,128},{128,256},{256,384},{385,1},{1,129},{129,257},{257... | collective-permute-start | bytes 1769480 | tf_op jit(solution)/shard_map/ppermute | solution.py:15
  110.4 10.9 %collective-permute-start.16 = (bf16[512,2048]{1,0:T(8,128)(2,1)S(1)}, bf16[512,2048]{1,0:T(8,128)(2,1)S(1)}, u32[]{:S(2)}, u32[]{:S(2)}) collective-permute-start(bf16[512,2048]{1,0:T(8,128)(2,1)S(1)} %bitcast.50), channel_id=1, source_target_pairs={{0,1},{1,0},{2,3},{3,2},{4,5},{5,4},{6,7},{7,6},{8,9},{9,8},{10,11... | collective-permute-start | bytes 6291464 | tf_op jit(solution)/shard_map/ppermute | solution.py:165
  123.6 66.7 %copy-start.12 = (f32[32]{0:T(128)S(1)}, f32[32]{0:T(128)}, u32[]{:S(2)}) copy-start(f32[32]{0:T(128)} %param.10) | copy-start | bytes 388
  190.9 54.8 %copy-start.2 = (bf16[32,2048]{1,0:T(8,128)(2,1)}, bf16[32,2048]{1,0:T(8,128)(2,1)S(1)}, u32[]{:S(2)}) copy-start(bf16[32,2048]{1,0:T(8,128)(2,1)S(1)} %reshape.148) | copy-start | bytes 393220
  191.2 54.8 %copy-start.13 = (bf16[1024,768]{1,0:T(8,128)(2,1)S(1)}, bf16[1024,768]{1,0:T(8,128)(2,1)}, u32[]{:S(2)}) copy-start(bf16[1024,768]{1,0:T(8,128)(2,1)} %get-tuple-element.5) | copy-start | bytes 4718596
  (1 other events, 1.2 us)
Sparse Core Ops, SparseCore 0:
  11.2 80.2 all-gather.2
  123.7 64.1 reduce-scatter.1
